TPU v7x, 128 devices: a whole 4x4x4 slice. The times are simulated.
128 devices in a mesh: seq: 64 (over x_lo, z, y, core), hid: 2 (over x_hi).
Axes of the slice: x: 4 (x_hi: 2, x_lo: 2; x = x_hi * 2 + x_lo), y: 4, z: 4, core: 2. Of those that a mesh axis runs over, the one named last changes fastest.
Arguments:
- queries: bfloat16 [24576, 3072], P('seq', 'hid'), may hold values from -6 to 6
- keys: bfloat16 [24576, 3072], P('seq', 'hid'), may hold values from -4 to 4
- values: bfloat16 [24576, 3072], P('seq', 'hid'), may hold values from -6 to 6
- residual: bfloat16 [24576, 3072], P('seq', 'hid'), may hold values from -24 to 24
- w_in: bfloat16 [3072, 6144], P(None, 'hid'), may hold values from -0.109375 to 0.109375
- w_out: bfloat16 [6144, 3072], P('hid', 'seq'), may hold values from -0.078125 to 0.078125
- mod_scale: float32 [3072], replicated, may hold values from -0.5 to 0.5
- mod_gate: float32 [3072], replicated, may hold values from 0.5 to 1.5
- slot_tiles: int32 [64], replicated, may hold values from 0 to 63, as said below
- key_tiles: int32 [64, 27], replicated, may hold values from -1 to 63, as said below
Outputs:
- block_out: bfloat16 [24576, 3072], P('seq', 'hid')
Inputs may be any that keep to these rules, and one draw needn't show every extreme that they name: slot_tiles is a permutation of the tiles of a grid of 32 x 1 x 2, tile id (t + h) * 2 + w; two tiles that differ by at most one along every grid dimension sit at most 3 slots apart. `key_tiles`: row q lists distinct tile ids, each within one step of tile q along every grid dimension, in a fixed order of the 27 offsets; column 13 is q itself; other entries are -1.
All inputs are finite; a program needn't handle non-finite values.
Results may differ from a plain program's by a relative error of at most 0.0052.
Values may be sent and summed in bfloat16 or wider, within the bound.
No kernel may reach another device: no remote copies, remote signals or barrier semaphores. Data moves between devices by JAX's collectives and lax.ppermute only.
A program may use at most 128 MiB of HBM per device.

v0:
```python
import math

import jax
import jax.numpy as jnp
from jax import lax
from jax.sharding import PartitionSpec as P

HEAD_DIM = 128
TILE = 384
REACH = 3


def passed_along(value, axis, steps):
    count = lax.axis_size(axis)
    initial, last = (max(0, -steps), min(count, count - steps))
    return lax.ppermute(value, axis, [(source, source + steps) for source in range(initial, last)])


def attend_rows(query_rows, key_rows, value_rows, allowed):
    head_count = query_rows.shape[1] // HEAD_DIM
    q_heads = jnp.transpose(
        query_rows.reshape(query_rows.shape[0], head_count, HEAD_DIM), (1, 0, 2)
    )
    k_heads = jnp.transpose(key_rows.reshape(key_rows.shape[0], head_count, HEAD_DIM), (1, 0, 2))
    v_heads = jnp.transpose(
        value_rows.reshape(value_rows.shape[0], head_count, HEAD_DIM), (1, 0, 2)
    )

    def one_head(operands):
        q_one, k_one, v_one = operands
        scores = lax.dot_general(
            q_one, k_one, (((1,), (1,)), ((), ())), preferred_element_type=jnp.float32
        )
        scores = scores * (1.0 / math.sqrt(HEAD_DIM))
        scores = jnp.where(allowed, scores, -jnp.inf)
        row_max = jnp.max(scores, axis=-1, keepdims=True)
        probs = jnp.exp(scores - row_max)
        row_total = jnp.sum(probs, axis=-1)
        blended = jnp.dot(probs.astype(jnp.bfloat16), v_one, preferred_element_type=jnp.float32)
        return (blended / row_total[:, None]).astype(jnp.bfloat16)

    mixed = lax.map(one_head, (q_heads, k_heads, v_heads))
    return jnp.transpose(mixed, (1, 0, 2)).reshape(query_rows.shape[0], -1)


def on_device(
    queries, keys, values, residual, w_in, w_out, mod_scale, mod_gate, slot_tiles, key_tiles
):
    tok_rows, width = queries.shape
    stacked = jnp.stack((keys, values))
    hop_count = -(-(REACH * TILE) // tok_rows)
    offsets = list(range(hop_count, 0, -1)) + [0] + list(range(-1, -hop_count - 1, -1))
    pieces = []
    for hop_dist in offsets:
        if hop_dist == 0:
            pieces.append(stacked)
        else:
            pieces.append(passed_along(stacked, "seq", hop_dist))
    window_rows = jnp.concatenate(pieces, axis=1)
    padded_keys = window_rows[0]
    padded_values = window_rows[1]
    tile_count = tok_rows // TILE
    span = tile_count + 2 * REACH
    tile_total = slot_tiles.shape[0]
    first_slot = lax.axis_index("seq") * tile_count
    buffer_slots = first_slot - REACH + jnp.arange(span, dtype=jnp.int32)
    inside = (buffer_slots >= 0) & (buffer_slots < tile_total)
    buffer_tiles = slot_tiles[jnp.clip(buffer_slots, 0, tile_total - 1)]
    own_tiles = lax.dynamic_slice_in_dim(slot_tiles, first_slot, tile_count)
    wanted = key_tiles[own_tiles]
    listed = jnp.any(wanted[:, :, None] == buffer_tiles[None, None, :], axis=1) & inside[None, :]
    distance = (
        jnp.arange(span, dtype=jnp.int32)[None, :]
        - jnp.arange(tile_count, dtype=jnp.int32)[:, None]
    )
    near_ok = (distance >= 0) & (distance <= 2 * REACH)
    tile_mask = listed & near_ok
    row_mask = jnp.repeat(jnp.repeat(tile_mask, TILE, axis=0), TILE, axis=1)
    attn = attend_rows(queries, padded_keys, padded_values, row_mask)
    combined = (residual.astype(jnp.float32) + attn.astype(jnp.float32)).astype(jnp.bfloat16)
    whole = lax.all_gather(combined, "hid", axis=1, tiled=True)
    wide = whole.astype(jnp.float32)
    square = jnp.mean(wide * wide, axis=-1, keepdims=True)
    normed = (wide * lax.rsqrt(square + 1e-06) * (1.0 + mod_scale)).astype(jnp.bfloat16)
    inner = jnp.dot(normed, w_in, preferred_element_type=jnp.float32)
    hidden = jax.nn.gelu(inner, approximate=True).astype(jnp.bfloat16)
    terms = jnp.dot(
        hidden, lax.all_gather(w_out, "seq", axis=1, tiled=True), preferred_element_type=jnp.float32
    )
    mlp_part = lax.psum_scatter(terms, "hid", scatter_dimension=1, tiled=True)
    gate_part = lax.dynamic_slice_in_dim(mod_gate, lax.axis_index("hid") * width, width)
    return (combined.astype(jnp.float32) + gate_part * mlp_part).astype(jnp.bfloat16)


def solution(mesh):
    placed = (
        P("seq", "hid"),
        P("seq", "hid"),
        P("seq", "hid"),
        P("seq", "hid"),
        P(None, "hid"),
        P("hid", "seq"),
        P(),
        P(),
        P(),
        P(),
    )
    return jax.shard_map(
        on_device, mesh=mesh, in_specs=placed, out_specs=P("seq", "hid"), check_vma=False
    )
```

profile of v0, /device:TPU:7, one launch (start us, length us, event | category | flops | bytes accessed | tf_op | source)
XLA Modules:
  0.0 532.4 jit_solution(6438873940661303609)
XLA Ops:
  11.7 5.4 %collective-permute-start = (bf16[2,384,1536]{1,2,0:T(8,128)(2,1)}, bf16[2,384,1536]{1,2,0:T(8,128)(2,1)}, u32[]{:S(2)}, u32[]{:S(2)}) collective-permute-start(bf16[2,384,1536]{1,2,0:T(8,128)(2,1)} %pad_maximum_fusion), channel_id=1, source_target_pairs={{0,6},{2,8},{4,10},{6,12},{8,14},{10,16},{12,18},{14,20},{16,22},{... | collective-permute-start | bytes 7077896 | tf_op jit(solution)/shard_map/ppermute | solution.py:16
  17.0 2.3 collective-permute-start.1
  19.4 2.2 collective-permute-start.2
  21.6 2.1 collective-permute-start.3
  23.7 7.2 %collective-permute-start.4 = (bf16[2,384,1536]{1,2,0:T(8,128)(2,1)}, bf16[2,384,1536]{1,2,0:T(8,128)(2,1)}, u32[]{:S(2)}, u32[]{:S(2)}) collective-permute-start(bf16[2,384,1536]{1,2,0:T(8,128)(2,1)} %pad_maximum_fusion), channel_id=1, source_target_pairs={{4,0},{6,2},{8,4},{10,6},{12,8},{14,10},{16,12},{18,14},{20,16},{2... | collective-permute-start | bytes 7077896 | tf_op jit(solution)/shard_map/ppermute | solution.py:16
  33.0 44.0 %collective-permute-done = bf16[2,384,1536]{1,2,0:T(8,128)(2,1)} collective-permute-done((bf16[2,384,1536]{1,2,0:T(8,128)(2,1)}, bf16[2,384,1536]{1,2,0:T(8,128)(2,1)}, u32[]{:S(2)}, u32[]{:S(2)}) %collective-permute-start) | collective-permute-done | bytes 2359328 | tf_op jit(solution)/shard_map/ppermute | solution.py:16
  84.4 43.3 %collective-permute-done.1 = bf16[2,384,1536]{1,2,0:T(8,128)(2,1)} collective-permute-done((bf16[2,384,1536]{1,2,0:T(8,128)(2,1)}, bf16[2,384,1536]{1,2,0:T(8,128)(2,1)}, u32[]{:S(2)}, u32[]{:S(2)}) %collective-permute-start.1) | collective-permute-done | bytes 2359328 | tf_op jit(solution)/shard_map/ppermute | solution.py:16
  127.6 2.1 constant_dynamic-update-slice_fusion.6
  129.8 12.8 %collective-permute-done.2 = bf16[2,384,1536]{1,2,0:T(8,128)(2,1)} collective-permute-done((bf16[2,384,1536]{1,2,0:T(8,128)(2,1)}, bf16[2,384,1536]{1,2,0:T(8,128)(2,1)}, u32[]{:S(2)}, u32[]{:S(2)}) %collective-permute-start.2) | collective-permute-done | bytes 2359328 | tf_op jit(solution)/shard_map/ppermute | solution.py:16
  142.6 2.1 constant_dynamic-update-slice_fusion.5
  145.3 2.1 constant_dynamic-update-slice_fusion.3
  147.4 2.1 constant_dynamic-update-slice_fusion.2
  149.6 22.5 %collective-permute-done.5 = bf16[2,384,1536]{1,2,0:T(8,128)(2,1)} collective-permute-done((bf16[2,384,1536]{1,2,0:T(8,128)(2,1)}, bf16[2,384,1536]{1,2,0:T(8,128)(2,1)}, u32[]{:S(2)}, u32[]{:S(2)}) %collective-permute-start.5) | collective-permute-done | bytes 2359328 | tf_op jit(solution)/shard_map/ppermute | solution.py:16
  172.0 2.1 constant_dynamic-update-slice_fusion.1
  174.2 5.9 %fusion.56 = (bf16[1,2688,1536]{1,2,0:T(8,128)(2,1)}, bf16[1,2688,1536]{1,2,0:T(8,128)(2,1)}) fusion(bf16[2,2688,1536]{1,2,0:T(8,128)(2,1)S(1)} %constant_dynamic-update-slice_fusion.1), kind=kLoop, calls=%fused_computation.66 | loop fusion | bytes 33030144 | tf_op jit(solution)/shard_map/slice | solution.py:61
  180.1 57.0 %while.12 = (s32[]{:T(128)}, bf16[12,384,128]{1,2,0:T(8,128)(2,1)S(1)}, bf16[12,384,128]{1,2,0:T(8,128)(2,1)S(1)}, bf16[12,2688,128]{1,2,0:T(8,128)(2,1)}, bf16[...) while((s32[]{:T(128)}, bf16[12,384,128]{1,2,0:T(8,128)(2,1)S(1)}, ...), condition=%wide.region_4.5_spmd.clone, body=%wide.region_1.4_spmd.clone.sunk | while | flops 535805184 | bytes 14364753 | solution.py:42
  237.3 2.1 copy.27
  239.4 3.0 add_convert_fusion.1
  243.4 62.9 %all-gather.3.cloned.1.call-done = bf16[384,3072]{1,0:T(8,128)(2,1)} async-done(((bf16[384,1536]{1,0:T(8,128)(2,1)}), bf16[384,3072]{1,0:T(8,128)(2,1)}) %all-gather.3.cloned.1.call-update) | async-done | bytes 2359312 | tf_op jit(solution)/shard_map/all_gather | solution.py:81
  306.4 2.2 fusion.25
  308.6 126.0 %all-gather.5.cloned.1.call-done = bf16[3072,3072]{0,1:T(8,128)(2,1)} async-done(((bf16[3072,48]{0,1:T(8,128)(2,1)}), bf16[3072,3072]{0,1:T(8,128)(2,1)}) %all-gather.5.cloned.1.call-update) | async-done | bytes 18874384 | tf_op jit(solution)/shard_map/all_gather | solution.py:88
  434.5 26.7 %fusion.36 = f32[384,3072]{1,0:T(8,128)} fusion(bf16[3072,3072]{0,1:T(8,128)(2,1)} %all-gather.5.cloned.1.call-done, bf16[3072,3072]{1,0:T(8,128)(2,1)} %param.16, bf16[384,3072]{1,0:T(8,128)(2,1)} %all-gather.3.cloned.1.call-done, f32[3072]{0:T(1024)S(1)} %broadcast_add_fusion, f32[384]{0:T(512)S(1)} %add_rsqrt_fusion), kind=kOutput, calls=%fused_computation.35 | convolution fusion | flops 14510850048 | bytes 44840448 | tf_op jit(solution)/shard_map/dot_general | solution.py:87
  462.1 60.8 %reduce-scatter.2.cloned.1.call-done = f32[384,1536]{1,0:T(8,128)} async-done(((f32[384,3072]{1,0:T(8,128)}), f32[384,1536]{1,0:T(8,128)}) %reduce-scatter.2.cloned.1.call-update) | async-done | bytes 2359312 | tf_op jit(solution)/shard_map/reduce_scatter | solution.py:90
  522.9 3.0 add_convert_fusion
  (105 shorter events, 71.4 us)
Async XLA Ops:
  6.5 73.7 %copy-start = (s32[64,27]{0,1:T(8,128)S(1)}, s32[64,27]{0,1:T(8,128)}, u32[]{:S(2)}) copy-start(s32[64,27]{0,1:T(8,128)} %param.21) | copy-start | bytes 20740
  6.5 299.8 %all-gather.3.cloned.1.call-start = ((), (), s32[]{:S(2)}) async-start(), calls=%async_computation.1 | async-start | bytes 3538944 | tf_op jit(solution)/shard_map/all_gather | solution.py:81
  8.3 22.7 %copy-start.2 = (s32[64]{0:T(128)S(1)}, s32[64]{0:T(128)}, u32[]{:S(2)}) copy-start(s32[64]{0:T(128)} %param.20) | copy-start | bytes 772
  11.7 65.3 %collective-permute-start = (bf16[2,384,1536]{1,2,0:T(8,128)(2,1)}, bf16[2,384,1536]{1,2,0:T(8,128)(2,1)}, u32[]{:S(2)}, u32[]{:S(2)}) collective-permute-start(bf16[2,384,1536]{1,2,0:T(8,128)(2,1)} %pad_maximum_fusion), channel_id=1, source_target_pairs={{0,6},{2,8},{4,10},{6,12},{8,14},{10,16},{12,18},{14,20},{16,22},{... | collective-permute-start | bytes 7077896 | tf_op jit(solution)/shard_map/ppermute | solution.py:16
  17.0 110.6 %collective-permute-start.1 = (bf16[2,384,1536]{1,2,0:T(8,128)(2,1)}, bf16[2,384,1536]{1,2,0:T(8,128)(2,1)}, u32[]{:S(2)}, u32[]{:S(2)}) collective-permute-start(bf16[2,384,1536]{1,2,0:T(8,128)(2,1)} %pad_maximum_fusion), channel_id=1, source_target_pairs={{0,4},{2,6},{4,8},{6,10},{8,12},{10,14},{12,16},{14,18},{16,20},{1... | collective-permute-start | bytes 7077896 | tf_op jit(solution)/shard_map/ppermute | solution.py:16
  19.4 123.3 %collective-permute-start.2 = (bf16[2,384,1536]{1,2,0:T(8,128)(2,1)}, bf16[2,384,1536]{1,2,0:T(8,128)(2,1)}, u32[]{:S(2)}, u32[]{:S(2)}) collective-permute-start(bf16[2,384,1536]{1,2,0:T(8,128)(2,1)} %pad_maximum_fusion), channel_id=1, source_target_pairs={{0,2},{2,4},{4,6},{6,8},{8,10},{10,12},{12,14},{14,16},{16,18},{18... | collective-permute-start | bytes 7077896 | tf_op jit(solution)/shard_map/ppermute | solution.py:16
  21.6 123.7 %collective-permute-start.3 = (bf16[2,384,1536]{1,2,0:T(8,128)(2,1)}, bf16[2,384,1536]{1,2,0:T(8,128)(2,1)}, u32[]{:S(2)}, u32[]{:S(2)}) collective-permute-start(bf16[2,384,1536]{1,2,0:T(8,128)(2,1)} %pad_maximum_fusion), channel_id=1, source_target_pairs={{2,0},{4,2},{6,4},{8,6},{10,8},{12,10},{14,12},{16,14},{18,16},{20... | collective-permute-start | bytes 7077896 | tf_op jit(solution)/shard_map/ppermute | solution.py:16
  23.7 123.7 %collective-permute-start.4 = (bf16[2,384,1536]{1,2,0:T(8,128)(2,1)}, bf16[2,384,1536]{1,2,0:T(8,128)(2,1)}, u32[]{:S(2)}, u32[]{:S(2)}) collective-permute-start(bf16[2,384,1536]{1,2,0:T(8,128)(2,1)} %pad_maximum_fusion), channel_id=1, source_target_pairs={{4,0},{6,2},{8,4},{10,6},{12,8},{14,10},{16,12},{18,14},{20,16},{2... | collective-permute-start | bytes 7077896 | tf_op jit(solution)/shard_map/ppermute | solution.py:16
  77.0 95.1 %collective-permute-start.5 = (bf16[2,384,1536]{1,2,0:T(8,128)(2,1)}, bf16[2,384,1536]{1,2,0:T(8,128)(2,1)}, u32[]{:S(2)}, u32[]{:S(2)}) collective-permute-start(bf16[2,384,1536]{1,2,0:T(8,128)(2,1)} %pad_maximum_fusion), channel_id=1, source_target_pairs={{6,0},{8,2},{10,4},{12,6},{14,8},{16,10},{18,12},{20,14},{22,16},{... | collective-permute-start | bytes 7077896 | tf_op jit(solution)/shard_map/ppermute | solution.py:16
  174.2 6.0 %copy-start.4 = (bf16[12,384,128]{1,2,0:T(8,128)(2,1)S(1)}, bf16[12,384,128]{1,2,0:T(8,128)(2,1)}, u32[]{:S(2)}) copy-start(bf16[12,384,128]{1,2,0:T(8,128)(2,1)} %custom-call.3) | copy-start | bytes 3538948
  237.3 2.1 copy-start.5
  239.4 4.0 copy-start.6
  242.4 192.1 %all-gather.5.cloned.1.call-start = ((), (), s32[]{:S(2)}) async-start(), calls=%async_computation.2 | async-start | bytes 19169280 | tf_op jit(solution)/shard_map/all_gather | solution.py:88
  243.2 279.7 %reduce-scatter.2.cloned.1.call-start = ((), (), s32[]{:S(2)}) async-start(), calls=%async_computation.3 | async-start | bytes 7077888 | tf_op jit(solution)/shard_map/reduce_scatter | solution.py:90
  461.3 0.7 copy-start.7
  461.3 61.6 %copy-start.3 = (bf16[384,1536]{1,0:T(8,128)(2,1)S(1)}, bf16[384,1536]{1,0:T(8,128)(2,1)}, u32[]{:S(2)}) copy-start(bf16[384,1536]{1,0:T(8,128)(2,1)} %add_convert_fusion.1) | copy-start | bytes 3538948
  461.3 64.6 %copy-start.1 = (s32[64,27]{0,1:T(8,128)S(1)}, s32[64,27]{0,1:T(8,128)}, u32[]{:S(2)}) copy-start(s32[64,27]{0,1:T(8,128)} %param.21) | copy-start | bytes 20740
Sparse Core Ops, SparseCore 0:
  242.6 63.7 all-gather.2
  308.1 126.4 all-gather.4
  461.4 61.3 reduce-scatter.1
where the time goes:
time: 537 us; the launch traced here: 532 us
  waiting for transfers between devices  373 us (69%)
  matrix products  73.1 us (14%)
  local copies, waits for them, and re-layouts  29.8 us (6%)
  starting transfers between devices  21.4 us (4%)
  other arithmetic  19.3 us (4%)
  between operations  15.4 us (3%)
    all_gather x1, waiting for transfers between devices, on_device(): lax.all_gather(w_out, 'seq', axis=1, tiled=True)  126 us
    ppermute x6, waiting for transfers between devices, passed_along(): lax.ppermute(value, axis, [(source, source + steps) for source in range(i...  123 us
    all_gather x1, waiting for transfers between devices, on_device(): whole = lax.all_gather(combined, 'hid', axis=1, tiled=True)  62.9 us
    reduce_scatter x1, waiting for transfers between devices, on_device(): mlp_part = lax.psum_scatter(terms, 'hid', scatter_dimension=1, tiled=True)  60.8 us
    dot_general x1, matrix products, on_device(): jnp.dot(hidden, lax.all_gather(w_out, 'seq', axis=1, tiled=True), preferr...  26.7 us
    dot_general x12, matrix products, one_head(): lax.dot_general(q_one, k_one, (((1,), (1,)), ((), ())), preferred_element...  23.6 us
    dot_general x12, matrix products, one_head(): jnp.dot(probs.astype(jnp.bfloat16), v_one, preferred_element_type=jnp.flo...  22.7 us
    ppermute x6, starting transfers between devices, passed_along(): lax.ppermute(value, axis, [(source, source + steps) for source in range(i...  21.1 us
  transfers between devices with their start and end apart: 9, of which 7 were waited for; matrix products, arithmetic and copies ran while one was open for 3% of the time, Pallas kernels for 0%

commit v1 on v0

v1 whole, which is shorter than its diff:
```python
import functools
import math

import jax
import jax.numpy as jnp
from jax import lax
from jax.experimental import pallas as pl
from jax.experimental.pallas import tpu as pltpu
from jax.sharding import PartitionSpec as P

HEAD_DIM = 128
TILE = 384
FEAT = 3072
HALF = 1536
UNITS = 3072
PIECE = 48
BLOCK = 384
HEAD_CHUNKS = (2, 4, 4, 2)
LOG2_SCALE = math.log2(math.e) / math.sqrt(HEAD_DIM)
AXES = ("seq", "hid")
VMEM_BYTES = 56 << 20
LIGHT = pl.CostEstimate(flops=1, bytes_accessed=1, transcendentals=0)


def place(device):
    hid = device % 2
    seq = device // 2
    return seq // 32, seq // 8 % 4, seq // 2 % 4, seq % 2, hid


def device_at(x_lo, z, y, core, hid):
    return (((x_lo * 4 + z % 4) * 4 + y % 4) * 2 + core) * 2 + hid


def moved(value, target):
    pairs = []
    for device in range(128):
        there = target(*place(device))
        if there is not None:
            pairs.append((device, there))
    return lax.ppermute(value, AXES, pairs)


def after(value, *others):
    return lax.optimization_barrier((value, *others))[0]


def to_partner_core(x_lo, z, y, core, hid):
    return device_at(x_lo, z, y, 1 - core, hid)


def to_next_frame(x_lo, z, y, core, hid):
    chip = (x_lo * 4 + z) * 4 + y + (1 if core == 0 else -1)
    if not 0 <= chip < 32:
        return None
    return (chip * 2 + core) * 2 + hid


def along_y(x_lo, z, y, core, hid):
    return device_at(x_lo, z, y + (1 if core == 0 else -1), core, hid)


def along_z(x_lo, z, y, core, hid):
    return device_at(x_lo, z + (1 if core == 0 else -1), y, core, hid)


def along_x(x_lo, z, y, core, hid):
    return device_at(1 - x_lo, z, y, core, hid)


def to_other_hid(x_lo, z, y, core, hid):
    return device_at(x_lo, z, y, core, 1 - hid)


def attend_kernel(bias_ref, q_ref, res_ref, *refs):
    pairs, out_ref = refs[:3], refs[3]
    tiles = [(ref, row) for ref in pairs for row in (0, TILE)]
    for head in range(q_ref.shape[1] // HEAD_DIM):
        cols = slice(head * HEAD_DIM, (head + 1) * HEAD_DIM)
        query = q_ref[:, cols]
        scores = []
        tops = []
        for t, (ref, row) in enumerate(tiles):
            s = lax.dot_general(
                query, ref[row : row + TILE, cols], (((1,), (1,)), ((), ())), preferred_element_type=jnp.float32
            )
            scores.append(s)
            tops.append(jnp.max(s, axis=-1, keepdims=True) + bias_ref[t])
        top = functools.reduce(jnp.maximum, tops) * LOG2_SCALE
        total = None
        blended = None
        for t, (ref, row) in enumerate(tiles):
            probs = jnp.exp2(scores[t] * LOG2_SCALE + (bias_ref[t] - top))
            row_sum = jnp.sum(probs, axis=-1, keepdims=True)
            part = jnp.dot(
                probs.astype(jnp.bfloat16),
                ref[2 * TILE + row : 3 * TILE + row, cols],
                preferred_element_type=jnp.float32,
            )
            total = row_sum if total is None else total + row_sum
            blended = part if blended is None else blended + part
        attn = (blended / total).astype(jnp.bfloat16)
        out_ref[:, cols] = (res_ref[:, cols].astype(jnp.float32) + attn.astype(jnp.float32)).astype(
            jnp.bfloat16
        )


def attend(bias, queries, residual, both, mine, theirs, first, heads):
    wide = 2 * HEAD_DIM
    tall = lambda rows, at: pl.BlockSpec((rows, wide), lambda i: (0, at // 2 + i))
    return pl.pallas_call(
        attend_kernel,
        out_shape=jax.ShapeDtypeStruct((TILE, heads * HEAD_DIM), jnp.bfloat16),
        grid=(heads // 2,),
        in_specs=[pl.BlockSpec(memory_space=pltpu.SMEM)] + [tall(TILE, first)] * 2 + [tall(4 * TILE, 0)] * 3,
        out_specs=tall(TILE, 0),
        compiler_params=pltpu.CompilerParams(vmem_limit_bytes=VMEM_BYTES),
        cost_estimate=LIGHT,
        name="attend",
    )(bias, queries, residual, both, mine, theirs)


def gelu(x):
    return 0.5 * x * (1.0 + jnp.tanh(math.sqrt(2.0 / math.pi) * (x + 0.044715 * (x * x * x))))


def scaled_features(hid, groups, first, scale_ref, held_ref):
    square = None
    at = 0
    for half, group in zip((hid, 1 - hid), groups):
        feature = first
        for ref in group:
            width = ref.shape[1]
            gain = 1.0 + scale_ref[:, pl.ds(pl.multiple_of(half * HALF + feature, 128), width)]
            wide = ref[...].astype(jnp.float32)
            held_ref[:, at : at + width] = (wide * gain).astype(jnp.bfloat16)
            part = jnp.sum(wide * wide, axis=-1, keepdims=True)
            square = part if square is None else square + part
            feature += width
            at += width
    return square


def project_in_kernel(counts, blocks, first, has_earlier, is_last, hid_ref, *refs):
    own, other = refs[: counts[0]], refs[counts[0] : sum(counts)]
    scale_ref, *refs = refs[sum(counts) :]
    weights, refs = refs[: 2 * blocks], list(refs[2 * blocks :])
    acc_ref, earlier_square_ref = (refs.pop(0), refs.pop(0)) if has_earlier else (None, None)
    out_ref = refs.pop(0)
    square_ref, held_ref = refs

    @pl.when(pl.program_id(0) == 0)
    def _():
        square = scaled_features(hid_ref[0], (own, other), first, scale_ref, held_ref)
        square_ref[...] = square + earlier_square_ref[...] if has_earlier else square

    rows = weights[0].shape[0]
    inner = acc_ref[...] if has_earlier else None
    for i, w_ref in enumerate(weights):
        part = jnp.dot(held_ref[:, i * rows : (i + 1) * rows], w_ref[...], preferred_element_type=jnp.float32)
        inner = part if inner is None else inner + part
    if is_last:
        factor = lax.rsqrt(square_ref[...] * (1.0 / FEAT) + 1e-6)
        out_ref[...] = gelu(inner * factor).astype(jnp.bfloat16)
    else:
        out_ref[...] = inner


def project_in(hid, own, other, first, rows, mod_scale, w_in, earlier=None, is_last=False):
    cols = 512
    depth = sum(v.shape[1] for v in own)
    blocks = depth // rows
    assert first % rows == 0 and depth % rows == 0 and HALF % rows == 0
    whole = lambda v: pl.BlockSpec(v.shape, lambda i, h: (0, 0))
    column = pl.BlockSpec((TILE, cols), lambda i, h: (0, i))
    one = jax.ShapeDtypeStruct((TILE, 1), jnp.float32)
    scale = mod_scale.reshape(1, FEAT)

    def block(half, i):
        at = first // rows + i
        return pl.BlockSpec((rows, cols), lambda j, h: ((h[0] if half == 0 else 1 - h[0]) * (HALF // rows) + at, j))

    in_specs = [whole(v) for v in own + other] + [whole(scale)]
    in_specs += [block(half, i) for half in (0, 1) for i in range(blocks)]
    operands = [*own, *other, scale] + [w_in] * (2 * blocks)
    scratch = [pltpu.VMEM((TILE, 2 * depth), jnp.bfloat16)]
    if earlier is not None:
        in_specs += [column, whole(one)]
        operands += earlier
    if is_last:
        out_shape, out_specs = jax.ShapeDtypeStruct((TILE, UNITS), jnp.bfloat16), column
        scratch.insert(0, pltpu.VMEM((TILE, 1), jnp.float32))
    else:
        out_shape = (jax.ShapeDtypeStruct((TILE, UNITS), jnp.float32), one)
        out_specs = (column, whole(one))
    return pl.pallas_call(
        functools.partial(project_in_kernel, (len(own), len(other)), blocks, first, earlier is not None, is_last),
        out_shape=out_shape,
        grid_spec=pltpu.PrefetchScalarGridSpec(
            num_scalar_prefetch=1,
            grid=(UNITS // cols,),
            in_specs=in_specs,
            out_specs=out_specs,
            scratch_shapes=scratch,
        ),
        compiler_params=pltpu.CompilerParams(vmem_limit_bytes=VMEM_BYTES),
        cost_estimate=LIGHT,
        name="project_in",
    )(hid, *operands)


def project_out_kernel(hidden_ref, w_ref, out_ref):
    out_ref[...] = lax.dot_general(
        hidden_ref[...], w_ref[...], (((1,), (1,)), ((), ())), preferred_element_type=jnp.float32
    ).astype(out_ref.dtype)


def project_out(hidden, w_rows, dtype):
    cols = 512
    return pl.pallas_call(
        project_out_kernel,
        out_shape=jax.ShapeDtypeStruct((TILE, w_rows.shape[0]), dtype),
        grid=(w_rows.shape[0] // cols,),
        in_specs=[
            pl.BlockSpec((TILE, UNITS), lambda i: (0, 0)),
            pl.BlockSpec((cols, UNITS), lambda i: (i, 0)),
        ],
        out_specs=pl.BlockSpec((TILE, cols), lambda i: (0, i)),
        compiler_params=pltpu.CompilerParams(vmem_limit_bytes=VMEM_BYTES),
        cost_estimate=LIGHT,
        name="project_out",
    )(hidden, w_rows)


FETCHED = ((0, 0), (1, 0), (1, 1), (2, 0))
BOTH = FETCHED + tuple((-back, 1 - flip) for back, flip in FETCHED)
PIECES = tuple(
    (passed, tuple((z_back, back, flip) for back, flip in content))
    for passed, z_back, content in ((0, 0, BOTH), (0, 1, BOTH), (1, 1, BOTH), (0, 2, FETCHED), (1, 2, FETCHED))
)


def project_out_pieces_kernel(where_ref, hidden_ref, *refs):
    arrays = refs[: len(PIECES)]
    out_ref, w_buf, sems = refs[len(PIECES) :]
    z, y, core = (where_ref[i] for i in range(3))
    for ref, (passed, pieces) in zip(arrays, PIECES):
        fetcher = core + passed - 2 * core * passed
        step = 1 - 2 * fetcher
        for i, (z_back, y_back, flip) in enumerate(pieces):
            block = (z - step * z_back + 4) % 4
            y_at = (y - step * y_back + 4) % 4
            core_at = fetcher + flip - 2 * fetcher * flip
            row = pl.multiple_of(block * BLOCK + y_at * (2 * PIECE) + core_at * PIECE, 16)
            pltpu.make_async_copy(
                ref.at[pl.ds(i * PIECE, PIECE)], w_buf.at[pl.ds(row, PIECE)], sems.at[block]
            ).start()
    there = 0
    for at in range(0, HALF, 512):
        while there * BLOCK < at + 512:
            block = w_buf.at[pl.ds(there * BLOCK, BLOCK)]
            pltpu.make_async_copy(block, block, sems.at[there]).wait()
            there += 1
        out_ref[:, at : at + 512] = lax.dot_general(
            hidden_ref[...],
            w_buf[at : at + 512, :],
            (((1,), (1,)), ((), ())),
            preferred_element_type=jnp.float32,
        )


def project_out_pieces(where, hidden, arrays):
    vmem = pl.BlockSpec(memory_space=pltpu.VMEM)
    return pl.pallas_call(
        project_out_pieces_kernel,
        out_shape=jax.ShapeDtypeStruct((TILE, HALF), jnp.float32),
        in_specs=[pl.BlockSpec(memory_space=pltpu.SMEM), vmem]
        + [pl.BlockSpec(memory_space=pl.ANY)] * len(PIECES),
        out_specs=vmem,
        scratch_shapes=[pltpu.VMEM((HALF, UNITS), jnp.bfloat16), pltpu.SemaphoreType.DMA((4,))],
        compiler_params=pltpu.CompilerParams(vmem_limit_bytes=VMEM_BYTES),
        cost_estimate=LIGHT,
        name="project_out_pieces",
    )(where, hidden, *arrays)


def finish_kernel(chunk_count, *refs):
    combined = refs[:chunk_count]
    kept_ref, received_ref, gate_ref, out_ref = refs[chunk_count:]
    at = 0
    for ref in combined:
        cols = slice(at, at + ref.shape[1])
        mlp = kept_ref[:, cols] + received_ref[:, cols].astype(jnp.float32)
        out_ref[:, cols] = (ref[...].astype(jnp.float32) + gate_ref[:, cols] * mlp).astype(jnp.bfloat16)
        at = cols.stop


def finish(combined, kept, received, gate):
    vmem = pl.BlockSpec(memory_space=pltpu.VMEM)
    return pl.pallas_call(
        functools.partial(finish_kernel, len(combined)),
        out_shape=jax.ShapeDtypeStruct((TILE, HALF), jnp.bfloat16),
        in_specs=[vmem] * (len(combined) + 3),
        out_specs=vmem,
        compiler_params=pltpu.CompilerParams(vmem_limit_bytes=VMEM_BYTES),
        cost_estimate=LIGHT,
        name="finish",
    )(*combined, kept, received, gate)


def on_device(
    queries, keys, values, residual, w_in, w_out, mod_scale, mod_gate, slot_tiles, key_tiles
):
    seq = lax.axis_index("seq")
    hid = lax.axis_index("hid")
    core = seq % 2
    y = seq // 2 % 4
    z = seq // 8 % 4
    x_lo = seq // 32

    side = 1 - 2 * core
    slots = seq + side * jnp.array([0, 1, -2, -1, 3, 2], jnp.int32)
    inside = (slots >= 0) & (slots < slot_tiles.shape[0])
    tiles = slot_tiles[jnp.clip(slots, 0, slot_tiles.shape[0] - 1)]
    listed = jnp.any(key_tiles[slot_tiles[seq]][:, None] == tiles[None, :], axis=0)
    bias = jnp.where(listed & inside, 0.0, -jnp.inf).astype(jnp.float32)

    counts = HEAD_CHUNKS
    starts = [sum(counts[:i]) for i in range(len(counts))]
    cols = [slice(f * HEAD_DIM, (f + n) * HEAD_DIM) for f, n in zip(starts, counts)]
    pack = lambda c: jnp.concatenate((keys[:, c], values[:, c]), axis=0)

    swap = lambda v: moved(v, to_partner_core)
    join = lambda *v: jnp.concatenate(v, axis=0)
    hid_1 = hid.reshape(1)
    mine, own, others, theirs, both = [], [], [], [], []

    def join_frame(k, v, k_other, v_other):
        both.append(join(k, k_other, v, v_other))
        mine.append(moved(both[-1], to_next_frame))
        return both[-1]

    def attend_chunk(i, *earlier):
        part = attend(
            after(bias, *earlier), queries, residual, both[i], mine[i], theirs[i], starts[i], counts[i]
        )
        own.append(part)
        return part

    own_is_first = x_lo == 1 - hid
    same = [[32 * x + i for i in range(32)] for x in (0, 1)]
    gathered = lambda v: lax.all_gather(v, "seq", axis=0, tiled=True, axis_index_groups=same)
    piece = w_out.T
    piece_x = moved(piece, along_x)
    pack_0 = after(pack(cols[0]), piece)
    other_0 = swap(pack_0)
    pack_rest = after(pack(slice(cols[1].start, HALF)), pack_0)
    other_0 = after(other_0, pack_rest)
    done = join_frame(pack_0[:TILE], pack_0[TILE:], other_0[:TILE], other_0[TILE:])
    piece_x = after(piece_x, done)
    first = jnp.where(own_is_first, piece, piece_x)
    w_remote = gathered(first)
    pack_rest = after(pack_rest, first)
    other_rest = swap(pack_rest)

    def join_chunk(i, *earlier):
        near = slice(cols[i].start - cols[1].start, cols[i].stop - cols[1].start)
        here = after(pack_rest, *earlier)
        return join_frame(here[:TILE, near], here[TILE:, near], other_rest[:TILE, near], other_rest[TILE:, near])

    done = join_chunk(1)
    mine[0] = after(mine[0], done)
    theirs.append(swap(mine[0]))
    done = join_chunk(2, mine[0])
    done = attend_chunk(0, done)
    mine[1] = after(mine[1], done)
    theirs.append(swap(mine[1]))
    done = join_chunk(3, mine[1])
    done = attend_chunk(1, done)
    others.append(moved(jnp.concatenate(own, axis=1), to_other_hid))
    mine[2] = after(mine[2], done)
    theirs.append(swap(mine[2]))
    done = attend_chunk(2, mine[2], others[0])
    others.append(moved(done, to_other_hid))
    mine[3] = after(mine[3], done)
    theirs.append(swap(mine[3]))
    earlier = project_in(after(hid_1, mine[3]), own[:2], others[:1], 0, 768, mod_scale, w_in)
    done = attend_chunk(3, earlier[1])
    others.append(moved(done, to_other_hid))
    second = after(jnp.where(own_is_first, piece_x, piece), done, w_remote)
    w_kept = gathered(second)
    hidden = project_in(
        after(hid_1, second), own[2:], others[1:], 768, 768, mod_scale, w_in, earlier, is_last=True
    )
    sent = project_out(hidden, w_remote, jnp.bfloat16)
    received = moved(sent, to_other_hid)
    kept = project_out(after(hidden, sent), w_kept, jnp.float32)
    gate = lax.dynamic_slice_in_dim(mod_gate, hid * HALF, HALF).reshape(1, HALF)
    return finish(own, kept, received, gate)


def solution(mesh):
    placed = (
        P("seq", "hid"),
        P("seq", "hid"),
        P("seq", "hid"),
        P("seq", "hid"),
        P(None, "hid"),
        P("hid", "seq"),
        P(),
        P(),
        P(),
        P(),
    )
    return jax.shard_map(
        on_device, mesh=mesh, in_specs=placed, out_specs=P("seq", "hid"), check_vma=False
    )
```

time: 537 us -> 215 us (0.40)
  waiting for transfers between devices: 373 us -> 67.4 us
  matrix products: 73.1 us -> 0 us
  Pallas kernels: 0 us -> 71 us
  starting transfers between devices: 21.4 us -> 37.7 us
  local copies, waits for them, and re-layouts: 29.8 us -> 14.1 us
  other arithmetic: 19.3 us -> 6.59 us
    all_gather x2, waiting for transfers between devices: 189 us -> 14.1 us  [on_device(): lax.all_gather(v, 'seq', axis=0, tiled=True, axis_index_groups=same)]
    dot_general x25 -> x0, matrix products: 73.1 us -> none  [the longest x1 26.7 us: on_device(): jnp.dot(hidden, lax.all_gather(w_out, 'seq', axis=1, tiled=True), preferr...]
    pallas_call x0 -> x9, Pallas kernels: none -> 71 us  [the longest x4 28.2 us: attend(): pl.pallas_call(attend_kernel, out_shape=jax.ShapeDtypeStruct((TILE, heads...]
    ppermute x6 -> x15, waiting for transfers between devices: 123 us -> 53.3 us  [moved(): return lax.ppermute(value, AXES, pairs)]
    reduce_scatter x1 -> x0, waiting for transfers between devices: 60.8 us -> none  [on_device(): mlp_part = lax.psum_scatter(terms, 'hid', scatter_dimension=1, tiled=True)]
    ppermute x6 -> x15, starting transfers between devices: 21.1 us -> 37.6 us  [moved(): return lax.ppermute(value, AXES, pairs)]
    unnamed x24 -> x46, local copies, waits for them, and re-layouts: 16.3 us -> 5.11 us
    reduce_sum x13 -> x0, other arithmetic: 10.6 us -> none  [the longest x12 8.44 us: one_head(): row_total = jnp.sum(probs, axis=-1)]
  transfers between devices with their start and end apart: 9 -> 17, of which waited for: 7 -> 9; matrix products, arithmetic and copies ran while one was open for 3% -> 6% of each run, Pallas kernels for 0% -> 32%
where the time goes in v1:
time: 215 us; the launch traced here: 213 us
  Pallas kernels  71 us (33%)
  waiting for transfers between devices  67.4 us (31%)
  starting transfers between devices  37.7 us (18%)
  between operations  15.9 us (7%)
  local copies, waits for them, and re-layouts  14.1 us (7%)
  other arithmetic  6.59 us (3%)
    ppermute x15, waiting for transfers between devices, moved(): return lax.ppermute(value, AXES, pairs)  53.3 us
    ppermute x15, starting transfers between devices, moved(): return lax.ppermute(value, AXES, pairs)  37.6 us
    pallas_call x4, Pallas kernels, attend(): pl.pallas_call(attend_kernel, out_shape=jax.ShapeDtypeStruct((TILE, heads...  28.2 us
    pallas_call x2, Pallas kernels, project_in(): pl.pallas_call(functools.partial(project_in_kernel, (len(own), len(other)...  21.3 us
    pallas_call x2, Pallas kernels, project_out(): pl.pallas_call(project_out_kernel, out_shape=jax.ShapeDtypeStruct((TILE,...  17.6 us
    all_gather x2, waiting for transfers between devices, on_device(): lax.all_gather(v, 'seq', axis=0, tiled=True, axis_index_groups=same)  14.1 us
    unnamed x46, local copies, waits for them, and re-layouts  5.11 us
  transfers between devices with their start and end apart: 17, of which 9 were waited for; matrix products, arithmetic and copies ran while one was open for 6% of the time, Pallas kernels for 32%

profile of v1, /device:TPU:7, one launch (start us, length us, event | category | flops | bytes accessed | tf_op | source)
XLA Modules:
  0.0 212.7 jit_solution(4432918750537645223)
XLA Ops:
  14.7 1.9 broadcast_select_fusion
  18.3 8.4 %collective-permute-start.2 = (bf16[1536,256]{1,0:T(8,128)(2,1)S(1)}, bf16[1536,256]{1,0:T(8,128)(2,1)}, u32[]{:S(2)}, u32[]{:S(2)}) collective-permute-start(bf16[1536,256]{1,0:T(8,128)(2,1)S(1)} %pad_maximum_fusion.3.refs_0_), channel_id=1, source_target_pairs={{0,4},{1,5},{4,8},{5,9},{6,2},{7,3},{8,12},{9,13},{10,6},{11,7},{1... | collective-permute-start | bytes 2359304 | tf_op jit(solution)/shard_map/ppermute | solution.py:41
  29.4 3.5 %collective-permute-start.5 = (bf16[1536,512]{1,0:T(8,128)(2,1)}, bf16[1536,512]{1,0:T(8,128)(2,1)}, u32[]{:S(2)}, u32[]{:S(2)}) collective-permute-start(bf16[1536,512]{1,0:T(8,128)(2,1)} %pad_maximum_fusion.1.refs_0_), channel_id=1, source_target_pairs={{0,4},{1,5},{4,8},{5,9},{6,2},{7,3},{8,12},{9,13},{10,6},{11,7},{1... | collective-permute-start | bytes 4718600 | tf_op jit(solution)/shard_map/ppermute | solution.py:41
  40.2 5.5 %attend.4.refs_0_ = bf16[384,256]{1,0:T(8,128)(2,1)} custom-call(f32[6]{0:T(128)} %and_select_fusion.bias_ref, bf16[384,1536]{1,0:T(8,128)(2,1)} %q_ref.7, bf16[384,1536]{1,0:T(8,128)(2,1)} %res_ref.7, bf16[1536,256]{1,0:T(8,128)(2,1)} %copy-done.6, bf16[1536,256]{1,0:T(8,128)(2,1)} %collective-permute-done.2.refs_1_, bf16[1536,256]{1,0:T(8,128)(2,1)} %copy-done.15), custom_call_target="tpu_custom_call" | custom-call | flops 1 | bytes 1 | tf_op jit(solution)/shard_map/attend/pallas_call | solution.py:111
  45.6 7.8 %collective-permute-done.5.refs_1_ = bf16[1536,512]{1,0:T(8,128)(2,1)} collective-permute-done((bf16[1536,512]{1,0:T(8,128)(2,1)}, bf16[1536,512]{1,0:T(8,128)(2,1)}, u32[]{:S(2)}, u32[]{:S(2)}) %collective-permute-start.5) | collective-permute-done | bytes 1572896 | tf_op jit(solution)/shard_map/ppermute | solution.py:41
  54.1 7.4 %collective-permute-start.7 = (bf16[1536,512]{1,0:T(8,128)(2,1)S(1)}, bf16[1536,512]{1,0:T(8,128)(2,1)S(1)}, u32[]{:S(2)}, u32[]{:S(2)}) collective-permute-start(bf16[1536,512]{1,0:T(8,128)(2,1)S(1)} %pad_maximum_fusion.2.refs_0_), channel_id=1, source_target_pairs={{0,4},{1,5},{4,8},{5,9},{6,2},{7,3},{8,12},{9,13},{10,6},{11,7},{1... | collective-permute-start | bytes 4718600 | tf_op jit(solution)/shard_map/ppermute | solution.py:41
  62.7 8.8 %attend.5.refs_1_ = bf16[384,512]{1,0:T(8,128)(2,1)} custom-call(f32[6]{0:T(128)} %and_select_fusion.bias_ref, bf16[384,1536]{1,0:T(8,128)(2,1)} %q_ref.7, bf16[384,1536]{1,0:T(8,128)(2,1)} %res_ref.7, bf16[1536,512]{1,0:T(8,128)(2,1)} %pad_maximum_fusion.1.refs_0_, bf16[1536,512]{1,0:T(8,128)(2,1)} %collective-permute-done.5.refs_1_, ...), custom_call_target="tpu_custom_call" | custom-call | flops 1 | bytes 1 | tf_op jit(solution)/shard_map/attend/pallas_call | solution.py:111
  71.5 7.4 %collective-permute-done.7.refs_1_ = bf16[1536,512]{1,0:T(8,128)(2,1)S(1)} collective-permute-done((bf16[1536,512]{1,0:T(8,128)(2,1)S(1)}, bf16[1536,512]{1,0:T(8,128)(2,1)S(1)}, u32[]{:S(2)}, u32[]{:S(2)}) %collective-permute-start.7) | collective-permute-done | bytes 1572896 | tf_op jit(solution)/shard_map/ppermute | solution.py:41
  78.8 1.8 collective-permute-start.9
  80.6 6.3 %collective-permute-start.10 = (bf16[1536,256]{1,0:T(8,128)(2,1)S(1)}, bf16[1536,256]{1,0:T(8,128)(2,1)S(1)}, u32[]{:S(2)}, u32[]{:S(2)}) collective-permute-start(bf16[1536,256]{1,0:T(8,128)(2,1)S(1)} %pad_maximum_fusion.4.refs_0_), channel_id=1, source_target_pairs={{0,4},{1,5},{4,8},{5,9},{6,2},{7,3},{8,12},{9,13},{10,6},{11,7},{1... | collective-permute-start | bytes 2359304 | tf_op jit(solution)/shard_map/ppermute | solution.py:41
  89.2 20.2 %collective-permute-done.8.refs_2_ = bf16[384,768]{1,0:T(8,128)(2,1)S(1)} collective-permute-done((bf16[384,768]{1,0:T(8,128)(2,1)S(1)}, bf16[384,768]{1,0:T(8,128)(2,1)S(1)}, u32[]{:S(2)}, u32[]{:S(2)}) %collective-permute-start.8) | collective-permute-done | bytes 589856 | tf_op jit(solution)/shard_map/ppermute | solution.py:41
  110.5 8.5 %attend.6.refs_0_.refs_2_ = bf16[384,512]{1,0:T(8,128)(2,1)} custom-call(f32[6]{0:T(128)} %and_select_fusion.bias_ref, bf16[384,1536]{1,0:T(8,128)(2,1)} %q_ref.7, bf16[384,1536]{1,0:T(8,128)(2,1)} %res_ref.7, bf16[1536,512]{1,0:T(8,128)(2,1)} %copy-done.3, bf16[1536,512]{1,0:T(8,128)(2,1)} %copy-done.10, bf16[1536,512]{1,0:T(8,128)(2,1)} %copy-done.11), custom_call_target="tpu_custom_call" | custom-call | flops 1 | bytes 1 | tf_op jit(solution)/shard_map/attend/pallas_call | solution.py:111
  119.2 9.9 %project_in.2 = (f32[384,3072]{1,0:T(8,128)}, f32[384,1]{1,0:T(8,128)}) custom-call(s32[1]{0:T(128)} %bitcast.2.hid_ref, bf16[384,256]{1,0:T(8,128)(2,1)} %attend.4.refs_0_, bf16[384,512]{1,0:T(8,128)(2,1)} %attend.5.refs_1_, bf16[384,768]{1,0:T(8,128)(2,1)} %copy-done.17, f32[1,3072]{1,0:T(1,128)} %bitcast.7, bf16[3072,3072]{1,0:T(8,128)(2,1)} %refs_6_.1, ...), custom_call_target="tpu_custom_call" | custom-call | flops 1 | bytes 1 | tf_op jit(solution)/shard_map/project_in/pallas_call | solution.py:196
  130.0 5.4 %attend.7.refs_1_.refs_3_ = bf16[384,256]{1,0:T(8,128)(2,1)} custom-call(f32[6]{0:T(128)} %and_select_fusion.bias_ref, bf16[384,1536]{1,0:T(8,128)(2,1)} %q_ref.7, bf16[384,1536]{1,0:T(8,128)(2,1)} %res_ref.7, bf16[1536,256]{1,0:T(8,128)(2,1)} %copy-done.7, bf16[1536,256]{1,0:T(8,128)(2,1)} %copy-done.14, bf16[1536,256]{1,0:T(8,128)(2,1)} %copy-done.16), custom_call_target="tpu_custom_call" | custom-call | flops 1 | bytes 1 | tf_op jit(solution)/shard_map/attend/pallas_call | solution.py:111
  135.5 1.7 collective-permute-start.12
  138.5 8.9 %collective-permute-done.12.refs_2_ = bf16[384,512]{1,0:T(8,128)(2,1)S(1)} collective-permute-done((bf16[384,512]{1,0:T(8,128)(2,1)S(1)}, bf16[384,512]{1,0:T(8,128)(2,1)S(1)}, u32[]{:S(2)}, u32[]{:S(2)}) %collective-permute-start.12) | collective-permute-done | bytes 393248 | tf_op jit(solution)/shard_map/ppermute | solution.py:41
  147.5 4.2 %collective-permute-done.13.refs_3_ = bf16[384,256]{1,0:T(8,128)(2,1)S(1)} collective-permute-done((bf16[384,256]{1,0:T(8,128)(2,1)}, bf16[384,256]{1,0:T(8,128)(2,1)S(1)}, u32[]{:S(2)}, u32[]{:S(2)}) %collective-permute-start.13) | collective-permute-done | bytes 196640 | tf_op jit(solution)/shard_map/ppermute | solution.py:41
  152.3 11.3 %project_in.3.hidden_ref = bf16[384,3072]{1,0:T(8,128)(2,1)} custom-call(s32[1]{0:T(128)} %bitcast.2.hid_ref, bf16[384,512]{1,0:T(8,128)(2,1)} %attend.6.refs_0_.refs_2_, bf16[384,256]{1,0:T(8,128)(2,1)} %attend.7.refs_1_.refs_3_, bf16[384,512]{1,0:T(8,128)(2,1)} %copy-done.18, bf16[384,256]{1,0:T(8,128)(2,1)} %copy-done.20, f32[1,3072]{1,0:T(1,128)} %bitcast.8, ...), custom_call_target="tpu_custom_call" | custom-call | flops 1 | bytes 1 | tf_op jit(solution)/shard_map/project_in/pallas_call | solution.py:196
  163.7 9.0 %project_out.2 = bf16[384,1536]{1,0:T(8,128)(2,1)} custom-call(bf16[384,3072]{1,0:T(8,128)(2,1)} %project_in.3.hidden_ref, bf16[1536,3072]{1,0:T(8,128)(2,1)} %all-gather.3.cloned.1.call-done.w_ref), custom_call_target="tpu_custom_call" | custom-call | flops 1 | bytes 1 | tf_op jit(solution)/shard_map/project_out/pallas_call | solution.py:220
  172.7 1.7 collective-permute-start.14
  175.1 14.1 %all-gather.5.cloned.1.call-done.w_ref = bf16[1536,3072]{1,0:T(8,128)(2,1)} async-done(((bf16[48,3072]{1,0:T(8,128)(2,1)}), bf16[1536,3072]{1,0:T(8,128)(2,1)}) %all-gather.5.cloned.1.call-update) | async-done | bytes 9437200 | tf_op jit(solution)/shard_map/all_gather | solution.py:352
  189.2 8.6 %project_out.3.refs_4_ = f32[384,1536]{1,0:T(8,128)} custom-call(bf16[384,3072]{1,0:T(8,128)(2,1)} %project_in.3.hidden_ref, bf16[1536,3072]{1,0:T(8,128)(2,1)} %all-gather.5.cloned.1.call-done.w_ref), custom_call_target="tpu_custom_call" | custom-call | flops 1 | bytes 1 | tf_op jit(solution)/shard_map/project_out/pallas_call | solution.py:220
  197.8 3.1 %collective-permute-done.14.refs_5_ = bf16[384,1536]{1,0:T(8,128)(2,1)S(1)} collective-permute-done((bf16[384,1536]{1,0:T(8,128)(2,1)}, bf16[384,1536]{1,0:T(8,128)(2,1)S(1)}, u32[]{:S(2)}, u32[]{:S(2)}) %collective-permute-start.14) | collective-permute-done | bytes 1179680 | tf_op jit(solution)/shard_map/ppermute | solution.py:41
  202.0 3.9 %finish.1 = bf16[384,1536]{1,0:T(8,128)(2,1)} custom-call(bf16[384,256]{1,0:T(8,128)(2,1)} %attend.4.refs_0_, bf16[384,512]{1,0:T(8,128)(2,1)} %attend.5.refs_1_, bf16[384,512]{1,0:T(8,128)(2,1)} %attend.6.refs_0_.refs_2_, bf16[384,256]{1,0:T(8,128)(2,1)} %attend.7.refs_1_.refs_3_, f32[384,1536]{1,0:T(8,128)} %project_out.3.refs_4_, ...), custom_call_target="tpu_custom_call" | custom-call | flops 1 | bytes 1 | tf_op jit(solution)/shard_map/finish/pallas_call | solution.py:300
  (95 shorter events, 27.4 us)
Async XLA Ops:
  6.5 29.9 %copy-start = (s32[64,27]{0,1:T(8,128)S(1)}, s32[64,27]{0,1:T(8,128)}, u32[]{:S(2)}) copy-start(s32[64,27]{0,1:T(8,128)} %param.20) | copy-start | bytes 20740
  6.5 128.9 %all-gather.3.cloned.1.call-start = ((), (), s32[]{:S(2)}) async-start(), calls=%async_computation | async-start | bytes 9732096 | tf_op jit(solution)/shard_map/all_gather | solution.py:352
  6.5 8.2 %collective-permute-start = (bf16[48,3072]{1,0:T(8,128)(2,1)}, bf16[48,3072]{1,0:T(8,128)(2,1)}, u32[]{:S(2)}, u32[]{:S(2)}) collective-permute-start(bf16[48,3072]{1,0:T(8,128)(2,1)} %bitcast.6), channel_id=1, source_target_pairs={{0,64},{1,65},{2,66},{3,67},{4,68},{5,69},{6,70},{7,71},{8,72},{9,... | collective-permute-start | bytes 884744 | tf_op jit(solution)/shard_map/ppermute | solution.py:41
  9.1 4.0 %collective-permute-start.1 = (bf16[768,256]{1,0:T(8,128)(2,1)S(1)}, bf16[768,256]{1,0:T(8,128)(2,1)}, u32[]{:S(2)}, u32[]{:S(2)}) collective-permute-start(bf16[768,256]{1,0:T(8,128)(2,1)S(1)} %pad_maximum_fusion.6), channel_id=1, source_target_pairs={{0,2},{1,3},{2,0},{3,1},{4,6},{5,7},{6,4},{7,5},{8,10},{9,11},{10,... | collective-permute-start | bytes 1179656 | tf_op jit(solution)/shard_map/ppermute | solution.py:41
  14.3 13.5 %copy-start.6 = (bf16[1536,256]{1,0:T(8,128)(2,1)}, bf16[1536,256]{1,0:T(8,128)(2,1)S(1)}, u32[]{:S(2)}) copy-start(bf16[1536,256]{1,0:T(8,128)(2,1)S(1)} %pad_maximum_fusion.3.refs_0_) | copy-start | bytes 2359300
  16.6 172.6 %all-gather.5.cloned.1.call-start = ((), (), s32[]{:S(2)}) async-start(), calls=%async_computation.1 | async-start | bytes 9732096 | tf_op jit(solution)/shard_map/all_gather | solution.py:352
  16.7 10.1 %collective-permute-start.3 = (bf16[768,1280]{1,0:T(8,128)(2,1)S(1)}, bf16[768,1280]{1,0:T(8,128)(2,1)S(1)}, u32[]{:S(2)}, u32[]{:S(2)}) collective-permute-start(bf16[768,1280]{1,0:T(8,128)(2,1)S(1)} %pad_maximum_fusion), channel_id=1, source_target_pairs={{0,2},{1,3},{2,0},{3,1},{4,6},{5,7},{6,4},{7,5},{8,10},{9,11},{10,... | collective-permute-start | bytes 5898248 | tf_op jit(solution)/shard_map/ppermute | solution.py:41
  18.3 18.3 %collective-permute-start.2 = (bf16[1536,256]{1,0:T(8,128)(2,1)S(1)}, bf16[1536,256]{1,0:T(8,128)(2,1)}, u32[]{:S(2)}, u32[]{:S(2)}) collective-permute-start(bf16[1536,256]{1,0:T(8,128)(2,1)S(1)} %pad_maximum_fusion.3.refs_0_), channel_id=1, source_target_pairs={{0,4},{1,5},{4,8},{5,9},{6,2},{7,3},{8,12},{9,13},{10,6},{11,7},{1... | collective-permute-start | bytes 2359304 | tf_op jit(solution)/shard_map/ppermute | solution.py:41
  29.4 24.1 %collective-permute-start.5 = (bf16[1536,512]{1,0:T(8,128)(2,1)}, bf16[1536,512]{1,0:T(8,128)(2,1)}, u32[]{:S(2)}, u32[]{:S(2)}) collective-permute-start(bf16[1536,512]{1,0:T(8,128)(2,1)} %pad_maximum_fusion.1.refs_0_), channel_id=1, source_target_pairs={{0,4},{1,5},{4,8},{5,9},{6,2},{7,3},{8,12},{9,13},{10,6},{11,7},{1... | collective-permute-start | bytes 4718600 | tf_op jit(solution)/shard_map/ppermute | solution.py:41
  36.6 2.6 %collective-permute-start.4 = (bf16[1536,256]{1,0:T(8,128)(2,1)}, bf16[1536,256]{1,0:T(8,128)(2,1)S(1)}, u32[]{:S(2)}, u32[]{:S(2)}) collective-permute-start(bf16[1536,256]{1,0:T(8,128)(2,1)} %collective-permute-done.2.refs_1_), channel_id=1, source_target_pairs={{0,2},{1,3},{2,0},{3,1},{4,6},{5,7},{6,4},{7,5},{8,10},{9,11},{10,... | collective-permute-start | bytes 2359304 | tf_op jit(solution)/shard_map/ppermute | solution.py:41
  38.1 16.0 %copy-start.3 = (bf16[1536,512]{1,0:T(8,128)(2,1)}, bf16[1536,512]{1,0:T(8,128)(2,1)S(1)}, u32[]{:S(2)}) copy-start(bf16[1536,512]{1,0:T(8,128)(2,1)S(1)} %pad_maximum_fusion.2.refs_0_) | copy-start | bytes 4718596
  53.5 9.2 %collective-permute-start.6 = (bf16[1536,512]{1,0:T(8,128)(2,1)}, bf16[1536,512]{1,0:T(8,128)(2,1)}, u32[]{:S(2)}, u32[]{:S(2)}) collective-permute-start(bf16[1536,512]{1,0:T(8,128)(2,1)} %collective-permute-done.5.refs_1_), channel_id=1, source_target_pairs={{0,2},{1,3},{2,0},{3,1},{4,6},{5,7},{6,4},{7,5},{8,10},{9,11},{10,... | collective-permute-start | bytes 4718600 | tf_op jit(solution)/shard_map/ppermute | solution.py:41
  54.1 24.8 %collective-permute-start.7 = (bf16[1536,512]{1,0:T(8,128)(2,1)S(1)}, bf16[1536,512]{1,0:T(8,128)(2,1)S(1)}, u32[]{:S(2)}, u32[]{:S(2)}) collective-permute-start(bf16[1536,512]{1,0:T(8,128)(2,1)S(1)} %pad_maximum_fusion.2.refs_0_), channel_id=1, source_target_pairs={{0,4},{1,5},{4,8},{5,9},{6,2},{7,3},{8,12},{9,13},{10,6},{11,7},{1... | collective-permute-start | bytes 4718600 | tf_op jit(solution)/shard_map/ppermute | solution.py:41
  62.6 18.0 %copy-start.7 = (bf16[1536,256]{1,0:T(8,128)(2,1)}, bf16[1536,256]{1,0:T(8,128)(2,1)S(1)}, u32[]{:S(2)}) copy-start(bf16[1536,256]{1,0:T(8,128)(2,1)S(1)} %pad_maximum_fusion.4.refs_0_) | copy-start | bytes 2359300
  62.7 24.2 %copy-start.5 = (bf16[384,256]{1,0:T(8,128)(2,1)S(1)}, bf16[384,256]{1,0:T(8,128)(2,1)}, u32[]{:S(2)}) copy-start(bf16[384,256]{1,0:T(8,128)(2,1)} %attend.4.refs_0_) | copy-start | bytes 589828
  78.8 30.5 %copy-start.10 = (bf16[1536,512]{1,0:T(8,128)(2,1)}, bf16[1536,512]{1,0:T(8,128)(2,1)S(1)}, u32[]{:S(2)}) copy-start(bf16[1536,512]{1,0:T(8,128)(2,1)S(1)} %collective-permute-done.7.refs_1_) | copy-start | bytes 4718596
  78.8 30.5 %collective-permute-start.9 = (bf16[1536,512]{1,0:T(8,128)(2,1)S(1)}, bf16[1536,512]{1,0:T(8,128)(2,1)S(1)}, u32[]{:S(2)}, u32[]{:S(2)}) collective-permute-start(bf16[1536,512]{1,0:T(8,128)(2,1)S(1)} %collective-permute-done.7.refs_1_), channel_id=1, source_target_pairs={{0,2},{1,3},{2,0},{3,1},{4,6},{5,7},{6,4},{7,5},{8,10},{9,11},{10,... | collective-permute-start | bytes 4718600 | tf_op jit(solution)/shard_map/ppermute | solution.py:41
  80.6 38.4 %collective-permute-start.10 = (bf16[1536,256]{1,0:T(8,128)(2,1)S(1)}, bf16[1536,256]{1,0:T(8,128)(2,1)S(1)}, u32[]{:S(2)}, u32[]{:S(2)}) collective-permute-start(bf16[1536,256]{1,0:T(8,128)(2,1)S(1)} %pad_maximum_fusion.4.refs_0_), channel_id=1, source_target_pairs={{0,4},{1,5},{4,8},{5,9},{6,2},{7,3},{8,12},{9,13},{10,6},{11,7},{1... | collective-permute-start | bytes 2359304 | tf_op jit(solution)/shard_map/ppermute | solution.py:41
  88.1 21.3 %collective-permute-start.8 = (bf16[384,768]{1,0:T(8,128)(2,1)S(1)}, bf16[384,768]{1,0:T(8,128)(2,1)S(1)}, u32[]{:S(2)}, u32[]{:S(2)}) collective-permute-start(bf16[384,768]{1,0:T(8,128)(2,1)S(1)} %pad_maximum_fusion.5), channel_id=1, source_target_pairs={{0,1},{1,0},{2,3},{3,2},{4,5},{5,4},{6,7},{7,6},{8,9},{9,8},{10,11... | collective-permute-start | bytes 1769480 | tf_op jit(solution)/shard_map/ppermute | solution.py:41
  119.0 10.1 %collective-permute-start.11 = (bf16[1536,256]{1,0:T(8,128)(2,1)S(1)}, bf16[1536,256]{1,0:T(8,128)(2,1)S(1)}, u32[]{:S(2)}, u32[]{:S(2)}) collective-permute-start(bf16[1536,256]{1,0:T(8,128)(2,1)S(1)} %collective-permute-done.10.refs_1_), channel_id=1, source_target_pairs={{0,2},{1,3},{2,0},{3,1},{4,6},{5,7},{6,4},{7,5},{8,10},{9,11},{10,... | collective-permute-start | bytes 2359304 | tf_op jit(solution)/shard_map/ppermute | solution.py:41
  135.5 12.0 %collective-permute-start.12 = (bf16[384,512]{1,0:T(8,128)(2,1)S(1)}, bf16[384,512]{1,0:T(8,128)(2,1)S(1)}, u32[]{:S(2)}, u32[]{:S(2)}) collective-permute-start(bf16[384,512]{1,0:T(8,128)(2,1)S(1)} %copy-done.4), channel_id=1, source_target_pairs={{0,1},{1,0},{2,3},{3,2},{4,5},{5,4},{6,7},{7,6},{8,9},{9,8},{10,11... | collective-permute-start | bytes 1179656 | tf_op jit(solution)/shard_map/ppermute | solution.py:41
  137.2 14.5 %collective-permute-start.13 = (bf16[384,256]{1,0:T(8,128)(2,1)}, bf16[384,256]{1,0:T(8,128)(2,1)S(1)}, u32[]{:S(2)}, u32[]{:S(2)}) collective-permute-start(bf16[384,256]{1,0:T(8,128)(2,1)} %attend.7.refs_1_.refs_3_), channel_id=1, source_target_pairs={{0,1},{1,0},{2,3},{3,2},{4,5},{5,4},{6,7},{7,6},{8,9},{9,8},{10,11... | collective-permute-start | bytes 589832 | tf_op jit(solution)/shard_map/ppermute | solution.py:41
  172.7 28.2 %collective-permute-start.14 = (bf16[384,1536]{1,0:T(8,128)(2,1)}, bf16[384,1536]{1,0:T(8,128)(2,1)S(1)}, u32[]{:S(2)}, u32[]{:S(2)}) collective-permute-start(bf16[384,1536]{1,0:T(8,128)(2,1)} %project_out.2), channel_id=1, source_target_pairs={{0,1},{1,0},{2,3},{3,2},{4,5},{5,4},{6,7},{7,6},{8,9},{9,8},{10,11... | collective-permute-start | bytes 3538952 | tf_op jit(solution)/shard_map/ppermute | solution.py:41
  189.2 16.6 %copy-start.1 = (s32[64,27]{0,1:T(8,128)S(1)}, s32[64,27]{0,1:T(8,128)}, u32[]{:S(2)}) copy-start(s32[64,27]{0,1:T(8,128)} %param.20) | copy-start | bytes 20740
  (17 other events, 65.9 us)
Sparse Core Ops, SparseCore 0:
  16.8 102.8 all-gather.2
  135.6 53.5 all-gather.4

commit v2 on v1

--- a/solution.py
+++ b/solution.py
@@ -15,7 +15,8 @@
 UNITS = 3072
 PIECE = 48
 BLOCK = 384
-HEAD_CHUNKS = (2, 4, 4, 2)
+QUARTER = 768
+FRAME_CHUNKS = (4, 8)
 LOG2_SCALE = math.log2(math.e) / math.sqrt(HEAD_DIM)
 AXES = ("seq", "hid")
 VMEM_BYTES = 56 << 20
@@ -70,6 +71,10 @@
 
 def to_other_hid(x_lo, z, y, core, hid):
     return device_at(x_lo, z, y, core, 1 - hid)
+
+
+def to_other_hid_crossed(x_lo, z, y, core, hid):
+    return device_at(x_lo, z, y, 1 - core, 1 - hid)
 
 
 def attend_kernel(bias_ref, q_ref, res_ref, *refs):
@@ -105,14 +110,14 @@
         )
 
 
-def attend(bias, queries, residual, both, mine, theirs, first, heads):
+def attend(bias, queries, residual, both, mine, theirs, first, near, heads):
     wide = 2 * HEAD_DIM
     tall = lambda rows, at: pl.BlockSpec((rows, wide), lambda i: (0, at // 2 + i))
     return pl.pallas_call(
         attend_kernel,
         out_shape=jax.ShapeDtypeStruct((TILE, heads * HEAD_DIM), jnp.bfloat16),
         grid=(heads // 2,),
-        in_specs=[pl.BlockSpec(memory_space=pltpu.SMEM)] + [tall(TILE, first)] * 2 + [tall(4 * TILE, 0)] * 3,
+        in_specs=[pl.BlockSpec(memory_space=pltpu.SMEM)] + [tall(TILE, first)] * 2 + [tall(4 * TILE, near)] * 3,
         out_specs=tall(TILE, 0),
         compiler_params=pltpu.CompilerParams(vmem_limit_bytes=VMEM_BYTES),
         cost_estimate=LIGHT,
@@ -209,103 +214,65 @@
     )(hid, *operands)
 
 
-def project_out_kernel(hidden_ref, w_ref, out_ref):
+def project_out_kernel(part_ref, hidden_ref, w_ref, out_ref):
     out_ref[...] = lax.dot_general(
         hidden_ref[...], w_ref[...], (((1,), (1,)), ((), ())), preferred_element_type=jnp.float32
     ).astype(out_ref.dtype)
 
 
-def project_out(hidden, w_rows, dtype):
-    cols = 512
+def project_out(part, hidden, w_rows, dtype):
+    cols = 384
     return pl.pallas_call(
         project_out_kernel,
-        out_shape=jax.ShapeDtypeStruct((TILE, w_rows.shape[0]), dtype),
-        grid=(w_rows.shape[0] // cols,),
-        in_specs=[
-            pl.BlockSpec((TILE, UNITS), lambda i: (0, 0)),
-            pl.BlockSpec((cols, UNITS), lambda i: (i, 0)),
-        ],
-        out_specs=pl.BlockSpec((TILE, cols), lambda i: (0, i)),
+        out_shape=jax.ShapeDtypeStruct((TILE, QUARTER), dtype),
+        grid_spec=pltpu.PrefetchScalarGridSpec(
+            num_scalar_prefetch=1,
+            grid=(QUARTER // cols,),
+            in_specs=[
+                pl.BlockSpec((TILE, UNITS), lambda i, p: (0, 0)),
+                pl.BlockSpec((cols, UNITS), lambda i, p: (p[0] * (QUARTER // cols) + i, 0)),
+            ],
+            out_specs=pl.BlockSpec((TILE, cols), lambda i, p: (0, i)),
+        ),
         compiler_params=pltpu.CompilerParams(vmem_limit_bytes=VMEM_BYTES),
         cost_estimate=LIGHT,
         name="project_out",
-    )(hidden, w_rows)
-
-
-FETCHED = ((0, 0), (1, 0), (1, 1), (2, 0))
-BOTH = FETCHED + tuple((-back, 1 - flip) for back, flip in FETCHED)
-PIECES = tuple(
-    (passed, tuple((z_back, back, flip) for back, flip in content))
-    for passed, z_back, content in ((0, 0, BOTH), (0, 1, BOTH), (1, 1, BOTH), (0, 2, FETCHED), (1, 2, FETCHED))
-)
-
-
-def project_out_pieces_kernel(where_ref, hidden_ref, *refs):
-    arrays = refs[: len(PIECES)]
-    out_ref, w_buf, sems = refs[len(PIECES) :]
-    z, y, core = (where_ref[i] for i in range(3))
-    for ref, (passed, pieces) in zip(arrays, PIECES):
-        fetcher = core + passed - 2 * core * passed
-        step = 1 - 2 * fetcher
-        for i, (z_back, y_back, flip) in enumerate(pieces):
-            block = (z - step * z_back + 4) % 4
-            y_at = (y - step * y_back + 4) % 4
-            core_at = fetcher + flip - 2 * fetcher * flip
-            row = pl.multiple_of(block * BLOCK + y_at * (2 * PIECE) + core_at * PIECE, 16)
-            pltpu.make_async_copy(
-                ref.at[pl.ds(i * PIECE, PIECE)], w_buf.at[pl.ds(row, PIECE)], sems.at[block]
-            ).start()
-    there = 0
-    for at in range(0, HALF, 512):
-        while there * BLOCK < at + 512:
-            block = w_buf.at[pl.ds(there * BLOCK, BLOCK)]
-            pltpu.make_async_copy(block, block, sems.at[there]).wait()
-            there += 1
-        out_ref[:, at : at + 512] = lax.dot_general(
-            hidden_ref[...],
-            w_buf[at : at + 512, :],
-            (((1,), (1,)), ((), ())),
-            preferred_element_type=jnp.float32,
-        )
-
-
-def project_out_pieces(where, hidden, arrays):
-    vmem = pl.BlockSpec(memory_space=pltpu.VMEM)
-    return pl.pallas_call(
-        project_out_pieces_kernel,
-        out_shape=jax.ShapeDtypeStruct((TILE, HALF), jnp.float32),
-        in_specs=[pl.BlockSpec(memory_space=pltpu.SMEM), vmem]
-        + [pl.BlockSpec(memory_space=pl.ANY)] * len(PIECES),
-        out_specs=vmem,
-        scratch_shapes=[pltpu.VMEM((HALF, UNITS), jnp.bfloat16), pltpu.SemaphoreType.DMA((4,))],
-        compiler_params=pltpu.CompilerParams(vmem_limit_bytes=VMEM_BYTES),
-        cost_estimate=LIGHT,
-        name="project_out_pieces",
-    )(where, hidden, *arrays)
-
-
-def finish_kernel(chunk_count, *refs):
+    )(part, hidden, w_rows)
+
+
+def finish_kernel(chunk_count, core_ref, *refs):
     combined = refs[:chunk_count]
-    kept_ref, received_ref, gate_ref, out_ref = refs[chunk_count:]
-    at = 0
-    for ref in combined:
-        cols = slice(at, at + ref.shape[1])
-        mlp = kept_ref[:, cols] + received_ref[:, cols].astype(jnp.float32)
-        out_ref[:, cols] = (ref[...].astype(jnp.float32) + gate_ref[:, cols] * mlp).astype(jnp.bfloat16)
-        at = cols.stop
-
-
-def finish(combined, kept, received, gate):
+    kept_there, kept_here, received_here, received_there, gate_ref, out_ref = refs[chunk_count:]
+
+    def write(core):
+        at = 0
+        for ref in combined:
+            for left in range(0, ref.shape[1], 256):
+                cols = slice(at + left, at + left + 256)
+                near = slice(cols.start % QUARTER, cols.start % QUARTER + 256)
+                if cols.start // QUARTER == core:
+                    mlp = kept_there[:, near].astype(jnp.float32) + received_here[:, near].astype(jnp.float32)
+                else:
+                    mlp = kept_here[:, near] + received_there[:, near].astype(jnp.float32)
+                wide = ref[:, left : left + 256].astype(jnp.float32)
+                out_ref[:, cols] = (wide + gate_ref[:, cols] * mlp).astype(jnp.bfloat16)
+            at += ref.shape[1]
+
+    for core in (0, 1):
+        pl.when(core_ref[0] == core)(functools.partial(write, core))
+
+
+def finish(core, combined, kept_there, kept_here, received_here, received_there, gate):
     vmem = pl.BlockSpec(memory_space=pltpu.VMEM)
     return pl.pallas_call(
         functools.partial(finish_kernel, len(combined)),
         out_shape=jax.ShapeDtypeStruct((TILE, HALF), jnp.bfloat16),
-        in_specs=[vmem] * (len(combined) + 3),
+        in_specs=[pl.BlockSpec(memory_space=pltpu.SMEM)] + [vmem] * (len(combined) + 5),
         out_specs=vmem,
         compiler_params=pltpu.CompilerParams(vmem_limit_bytes=VMEM_BYTES),
         cost_estimate=LIGHT,
         name="finish",
-    )(*combined, kept, received, gate)
+    )(core, *combined, kept_there, kept_here, received_here, received_there, gate)
 
 
 def on_device(
@@ -325,78 +292,77 @@
     listed = jnp.any(key_tiles[slot_tiles[seq]][:, None] == tiles[None, :], axis=0)
     bias = jnp.where(listed & inside, 0.0, -jnp.inf).astype(jnp.float32)
 
-    counts = HEAD_CHUNKS
+    counts = FRAME_CHUNKS
     starts = [sum(counts[:i]) for i in range(len(counts))]
-    cols = [slice(f * HEAD_DIM, (f + n) * HEAD_DIM) for f, n in zip(starts, counts)]
-    pack = lambda c: jnp.concatenate((keys[:, c], values[:, c]), axis=0)
-
     swap = lambda v: moved(v, to_partner_core)
     join = lambda *v: jnp.concatenate(v, axis=0)
     hid_1 = hid.reshape(1)
     mine, own, others, theirs, both = [], [], [], [], []
 
-    def join_frame(k, v, k_other, v_other):
-        both.append(join(k, k_other, v, v_other))
+    def pack(i):
+        cols = slice(starts[i] * HEAD_DIM, (starts[i] + counts[i]) * HEAD_DIM)
+        return join(keys[:, cols], values[:, cols])
+
+    def send_frame(here, there):
+        both.append(join(here[:TILE], there[:TILE], here[TILE:], there[TILE:]))
         mine.append(moved(both[-1], to_next_frame))
         return both[-1]
 
-    def attend_chunk(i, *earlier):
+    def attend_heads(i, near, heads, *earlier):
         part = attend(
-            after(bias, *earlier), queries, residual, both[i], mine[i], theirs[i], starts[i], counts[i]
+            after(bias, *earlier),
+            queries,
+            residual,
+            both[i],
+            mine[i],
+            theirs[i],
+            starts[i] + near,
+            near,
+            heads,
         )
         own.append(part)
+        others.append(moved(part, to_other_hid))
         return part
 
-    own_is_first = x_lo == 1 - hid
-    same = [[32 * x + i for i in range(32)] for x in (0, 1)]
-    gathered = lambda v: lax.all_gather(v, "seq", axis=0, tiled=True, axis_index_groups=same)
+    own_is_other_half = x_lo == 1 - hid
+    gives_other_half = (core == 0) == (z < 2)
+    same = [[32 * x + 2 * i + c for i in range(16)] for x in (0, 1) for c in (0, 1)]
     piece = w_out.T
     piece_x = moved(piece, along_x)
-    pack_0 = after(pack(cols[0]), piece)
+    pack_0 = after(pack(0), piece)
     other_0 = swap(pack_0)
-    pack_rest = after(pack(slice(cols[1].start, HALF)), pack_0)
-    other_0 = after(other_0, pack_rest)
-    done = join_frame(pack_0[:TILE], pack_0[TILE:], other_0[:TILE], other_0[TILE:])
-    piece_x = after(piece_x, done)
-    first = jnp.where(own_is_first, piece, piece_x)
-    w_remote = gathered(first)
-    pack_rest = after(pack_rest, first)
-    other_rest = swap(pack_rest)
-
-    def join_chunk(i, *earlier):
-        near = slice(cols[i].start - cols[1].start, cols[i].stop - cols[1].start)
-        here = after(pack_rest, *earlier)
-        return join_frame(here[:TILE, near], here[TILE:, near], other_rest[:TILE, near], other_rest[TILE:, near])
-
-    done = join_chunk(1)
+    piece_x = after(piece_x, pack_0)
+    w_hold = jnp.where(own_is_other_half == gives_other_half, piece, piece_x)
+    w_pass = jnp.where(own_is_other_half == gives_other_half, piece_x, piece)
+    w_take = swap(w_pass)
+    done = send_frame(pack_0, after(other_0, w_pass))
+    w_take = after(w_take, done)
+    w_chip = join(jnp.where(core == 0, w_hold, w_take), jnp.where(core == 0, w_take, w_hold))
+    w_rows = lax.all_gather(w_chip, "seq", axis=0, tiled=True, axis_index_groups=same)
+    pack_1 = after(pack(1), w_chip)
+    other_1 = swap(pack_1)
+    done = send_frame(pack_1, other_1)
     mine[0] = after(mine[0], done)
     theirs.append(swap(mine[0]))
-    done = join_chunk(2, mine[0])
-    done = attend_chunk(0, done)
-    mine[1] = after(mine[1], done)
+    done = attend_heads(0, 0, 4)
+    mine[1] = after(mine[1], done, others[0])
     theirs.append(swap(mine[1]))
-    done = join_chunk(3, mine[1])
-    done = attend_chunk(1, done)
-    others.append(moved(jnp.concatenate(own, axis=1), to_other_hid))
-    mine[2] = after(mine[2], done)
-    theirs.append(swap(mine[2]))
-    done = attend_chunk(2, mine[2], others[0])
-    others.append(moved(done, to_other_hid))
-    mine[3] = after(mine[3], done)
-    theirs.append(swap(mine[3]))
-    earlier = project_in(after(hid_1, mine[3]), own[:2], others[:1], 0, 768, mod_scale, w_in)
-    done = attend_chunk(3, earlier[1])
-    others.append(moved(done, to_other_hid))
-    second = after(jnp.where(own_is_first, piece_x, piece), done, w_remote)
-    w_kept = gathered(second)
-    hidden = project_in(
-        after(hid_1, second), own[2:], others[1:], 768, 768, mod_scale, w_in, earlier, is_last=True
-    )
-    sent = project_out(hidden, w_remote, jnp.bfloat16)
-    received = moved(sent, to_other_hid)
-    kept = project_out(after(hidden, sent), w_kept, jnp.float32)
+    done = attend_heads(1, 0, 4)
+    done = attend_heads(1, 4, 4, done)
+    earlier = project_in(after(hid_1, done), own[:2], others[:2], 0, 512, mod_scale, w_in)
+    hidden = project_in(hid_1, own[2:], others[2:], 1024, 512, mod_scale, w_in, earlier, is_last=True)
+    hidden_there = swap(hidden)
+    core_1 = core.reshape(1)
+    sent_here = project_out(core_1, hidden, w_rows, jnp.bfloat16)
+    received_here = moved(sent_here, to_other_hid)
+    hidden_there = after(hidden_there, sent_here)
+    sent_there = project_out(core_1, hidden_there, w_rows, jnp.bfloat16)
+    received_there = moved(sent_there, to_other_hid_crossed)
+    kept_there = project_out(after(1 - core_1, sent_there), hidden_there, w_rows, jnp.bfloat16)
+    kept_here = project_out(after(1 - core_1, kept_there), hidden, w_rows, jnp.float32)
+    kept_there = jnp.concatenate((swap(kept_there[:, :384]), swap(kept_there[:, 384:])), axis=1)
     gate = lax.dynamic_slice_in_dim(mod_gate, hid * HALF, HALF).reshape(1, HALF)
-    return finish(own, kept, received, gate)
+    return finish(core_1, own, kept_there, kept_here, received_here, received_there, gate)
 
 
 def solution(mesh):

time: 215 us -> 191 us (0.89)
  starting transfers between devices: 37.7 us -> 24.3 us
  waiting for transfers between devices: 67.4 us -> 58.8 us
  Pallas kernels: 71 us -> 74.5 us
  other arithmetic: 6.59 us -> 4.33 us
    ppermute x15 -> x16, starting transfers between devices: 37.6 us -> 24.3 us  [moved(): return lax.ppermute(value, AXES, pairs)]
    all_gather x2 -> x1, waiting for transfers between devices: 14.1 us -> 1.1 us  [on_device(): lax.all_gather(w_chip, 'seq', axis=0, tiled=True, axis_index_groups=same)]
    pallas_call x2 -> x4, Pallas kernels: 17.6 us -> 23.9 us  [project_out(): pl.pallas_call(project_out_kernel, out_shape=jax.ShapeDtypeStruct((TILE,...]
    ppermute x15 -> x16, waiting for transfers between devices: 53.3 us -> 57.7 us  [moved(): return lax.ppermute(value, AXES, pairs)]
    pallas_call x4 -> x3, Pallas kernels: 28.2 us -> 25.5 us  [attend(): pl.pallas_call(attend_kernel, out_shape=jax.ShapeDtypeStruct((TILE, heads...]
    slice x11, local copies, waits for them, and re-layouts: 6.83 us -> 4.19 us  [the longest x6 2.74 us: pack(): return join(keys[:, cols], values[:, cols])]
    unnamed x46 -> x28, local copies, waits for them, and re-layouts: 5.11 us -> 6.21 us
  transfers between devices with their start and end apart: 17 -> 17, of which waited for: 9 -> 7; matrix products, arithmetic and copies ran while one was open for 6% -> 5% of each run, Pallas kernels for 32% -> 37%
where the time goes in v2:
time: 191 us; the launch traced here: 190 us
  Pallas kernels  74.5 us (39%)
  waiting for transfers between devices  58.8 us (31%)
  starting transfers between devices  24.3 us (13%)
  between operations  15.5 us (8%)
  local copies, waits for them, and re-layouts  12.5 us (7%)
  other arithmetic  4.33 us (2%)
    ppermute x16, waiting for transfers between devices, moved(): return lax.ppermute(value, AXES, pairs)  57.7 us
    pallas_call x3, Pallas kernels, attend(): pl.pallas_call(attend_kernel, out_shape=jax.ShapeDtypeStruct((TILE, heads...  25.5 us
    ppermute x16, starting transfers between devices, moved(): return lax.ppermute(value, AXES, pairs)  24.3 us
    pallas_call x4, Pallas kernels, project_out(): pl.pallas_call(project_out_kernel, out_shape=jax.ShapeDtypeStruct((TILE,...  23.9 us
    pallas_call x2, Pallas kernels, project_in(): pl.pallas_call(functools.partial(project_in_kernel, (len(own), len(other)...  21.5 us
    unnamed x28, local copies, waits for them, and re-layouts  6.21 us
  transfers between devices with their start and end apart: 17, of which 7 were waited for; matrix products, arithmetic and copies ran while one was open for 5% of the time, Pallas kernels for 37%

profile of v2, /device:TPU:7, one launch (start us, length us, event | category | flops | bytes accessed | tf_op | source)
XLA Modules:
  0.0 190.0 jit_solution(12689622102712148000)
XLA Ops:
  10.4 4.3 %collective-permute-done.1 = bf16[48,3072]{1,0:T(8,128)(2,1)S(1)} collective-permute-done((bf16[48,3072]{1,0:T(8,128)(2,1)}, bf16[48,3072]{1,0:T(8,128)(2,1)S(1)}, u32[]{:S(2)}, u32[]{:S(2)}) %collective-permute-start.1) | collective-permute-done | bytes 294944 | tf_op jit(solution)/shard_map/ppermute | solution.py:42
  14.7 1.6 collective-permute-start.3
  16.4 1.2 pad_maximum_fusion.1.refs_0_
  19.7 8.4 %collective-permute-start.2 = (bf16[1536,512]{1,0:T(8,128)(2,1)}, bf16[1536,512]{1,0:T(8,128)(2,1)}, u32[]{:S(2)}, u32[]{:S(2)}) collective-permute-start(bf16[1536,512]{1,0:T(8,128)(2,1)} %pad_maximum_fusion.1.refs_0_), channel_id=1, source_target_pairs={{0,4},{1,5},{4,8},{5,9},{6,2},{7,3},{8,12},{9,13},{10,6},{11,7},{1... | collective-permute-start | bytes 4718600 | tf_op jit(solution)/shard_map/ppermute | solution.py:42
  28.8 3.0 %collective-permute-start.6 = (bf16[1536,1024]{1,0:T(8,128)(2,1)S(1)}, bf16[1536,1024]{1,0:T(8,128)(2,1)}, u32[]{:S(2)}, u32[]{:S(2)}) collective-permute-start(bf16[1536,1024]{1,0:T(8,128)(2,1)S(1)} %pad_maximum_fusion.refs_0_), channel_id=1, source_target_pairs={{0,4},{1,5},{4,8},{5,9},{6,2},{7,3},{8,12},{9,13},{10,6},{11,7},{1... | collective-permute-start | bytes 9437192 | tf_op jit(solution)/shard_map/ppermute | solution.py:42
  31.8 16.8 %collective-permute-done.2.refs_1_ = bf16[1536,512]{1,0:T(8,128)(2,1)} collective-permute-done((bf16[1536,512]{1,0:T(8,128)(2,1)}, bf16[1536,512]{1,0:T(8,128)(2,1)}, u32[]{:S(2)}, u32[]{:S(2)}) %collective-permute-start.2) | collective-permute-done | bytes 1572896 | tf_op jit(solution)/shard_map/ppermute | solution.py:42
  52.6 8.5 %attend.3.refs_0_ = bf16[384,512]{1,0:T(8,128)(2,1)} custom-call(f32[6]{0:T(128)} %and_select_fusion.bias_ref, bf16[384,1536]{1,0:T(8,128)(2,1)} %q_ref.5, bf16[384,1536]{1,0:T(8,128)(2,1)} %res_ref.5, bf16[1536,512]{1,0:T(8,128)(2,1)} %pad_maximum_fusion.1.refs_0_, bf16[1536,512]{1,0:T(8,128)(2,1)} %collective-permute-done.2.refs_1_, ...), custom_call_target="tpu_custom_call" | custom-call | flops 1 | bytes 1 | tf_op jit(solution)/shard_map/attend/pallas_call | solution.py:116
  62.2 26.9 %collective-permute-done.7.refs_2_ = bf16[384,512]{1,0:T(8,128)(2,1)S(1)} collective-permute-done((bf16[384,512]{1,0:T(8,128)(2,1)}, bf16[384,512]{1,0:T(8,128)(2,1)S(1)}, u32[]{:S(2)}, u32[]{:S(2)}) %collective-permute-start.7) | collective-permute-done | bytes 393248 | tf_op jit(solution)/shard_map/ppermute | solution.py:42
  89.2 5.9 %collective-permute-done.8.refs_2_ = bf16[1536,1024]{1,0:T(8,128)(2,1)S(1)} collective-permute-done((bf16[1536,1024]{1,0:T(8,128)(2,1)}, bf16[1536,1024]{1,0:T(8,128)(2,1)S(1)}, u32[]{:S(2)}, u32[]{:S(2)}) %collective-permute-start.8) | collective-permute-done | bytes 3145760 | tf_op jit(solution)/shard_map/ppermute | solution.py:42
  95.0 1.7 copy-done.4
  96.7 8.5 %attend.4.refs_1_ = bf16[384,512]{1,0:T(8,128)(2,1)} custom-call(f32[6]{0:T(128)} %and_select_fusion.bias_ref, bf16[384,1536]{1,0:T(8,128)(2,1)} %q_ref.5, bf16[384,1536]{1,0:T(8,128)(2,1)} %res_ref.5, bf16[1536,1024]{1,0:T(8,128)(2,1)} %copy-done.3, bf16[1536,1024]{1,0:T(8,128)(2,1)} %collective-permute-done.6.refs_1_, bf16[1536,1024]{1,0:T(8,128)(2,1)} %copy-done.4), custom_call_target="tpu_custom_call" | custom-call | flops 1 | bytes 1 | tf_op jit(solution)/shard_map/attend/pallas_call | solution.py:116
  105.2 2.1 %collective-permute-start.10 = (bf16[384,512]{1,0:T(8,128)(2,1)}, bf16[384,512]{1,0:T(8,128)(2,1)S(1)}, u32[]{:S(2)}, u32[]{:S(2)}) collective-permute-start(bf16[384,512]{1,0:T(8,128)(2,1)} %attend.4.refs_1_), channel_id=1, source_target_pairs={{0,1},{1,0},{2,3},{3,2},{4,5},{5,4},{6,7},{7,6},{8,9},{9,8},{10,11... | collective-permute-start | bytes 1179656 | tf_op jit(solution)/shard_map/ppermute | solution.py:42
  107.3 8.6 %attend.5.refs_0_.refs_2_ = bf16[384,512]{1,0:T(8,128)(2,1)} custom-call(f32[6]{0:T(128)} %and_select_fusion.bias_ref, bf16[384,1536]{1,0:T(8,128)(2,1)} %q_ref.5, bf16[384,1536]{1,0:T(8,128)(2,1)} %res_ref.5, bf16[1536,1024]{1,0:T(8,128)(2,1)} %copy-done.3, bf16[1536,1024]{1,0:T(8,128)(2,1)} %collective-permute-done.6.refs_1_, bf16[1536,1024]{1,0:T(8,128)(2,1)} %copy-done.4), custom_call_target="tpu_custom_call" | custom-call | flops 1 | bytes 1 | tf_op jit(solution)/shard_map/attend/pallas_call | solution.py:116
  118.2 11.7 %project_in.2 = (f32[384,3072]{1,0:T(8,128)}, f32[384,1]{1,0:T(8,128)}) custom-call(s32[1]{0:T(128)} %bitcast.3.hid_ref, bf16[384,512]{1,0:T(8,128)(2,1)} %attend.3.refs_0_, bf16[384,512]{1,0:T(8,128)(2,1)} %attend.4.refs_1_, bf16[384,512]{1,0:T(8,128)(2,1)} %copy-done.9, bf16[384,512]{1,0:T(8,128)(2,1)} %copy-done.10, f32[1,3072]{1,0:T(1,128)} %bitcast.9, ...), custom_call_target="tpu_custom_call" | custom-call | flops 1 | bytes 1 | tf_op jit(solution)/shard_map/project_in/pallas_call | solution.py:201
  130.7 9.8 %project_in.3.hidden_ref = bf16[384,3072]{1,0:T(8,128)(2,1)} custom-call(s32[1]{0:T(128)} %bitcast.3.hid_ref, bf16[384,512]{1,0:T(8,128)(2,1)} %attend.5.refs_0_.refs_2_, bf16[384,512]{1,0:T(8,128)(2,1)} %copy-done.11, f32[1,3072]{1,0:T(1,128)} %bitcast.10, bf16[3072,3072]{1,0:T(8,128)(2,1)} %refs_4_.1, bf16[3072,3072]{1,0:T(8,128)(2,1)} %refs_4_.1, ...), custom_call_target="tpu_custom_call" | custom-call | flops 1 | bytes 1 | tf_op jit(solution)/shard_map/project_in/pallas_call | solution.py:201
  142.6 5.9 %project_out.4 = bf16[384,768]{1,0:T(8,128)(2,1)} custom-call(s32[1]{0:T(128)} %bitcast.part_ref.core_ref, bf16[384,3072]{1,0:T(8,128)(2,1)} %project_in.3.hidden_ref, bf16[1536,3072]{1,0:T(8,128)(2,1)} %all-gather.2.cloned.1.call-done.w_ref), custom_call_target="tpu_custom_call" | custom-call | flops 1 | bytes 1 | tf_op jit(solution)/shard_map/project_out/pallas_call | solution.py:225
  148.5 1.2 collective-permute-start.14
  149.7 1.4 copy-done.5
  151.1 6.0 %project_out.5 = bf16[384,768]{1,0:T(8,128)(2,1)} custom-call(s32[1]{0:T(128)} %bitcast.part_ref.core_ref, bf16[384,3072]{1,0:T(8,128)(2,1)} %copy-done.5, bf16[1536,3072]{1,0:T(8,128)(2,1)} %all-gather.2.cloned.1.call-done.w_ref), custom_call_target="tpu_custom_call" | custom-call | flops 1 | bytes 1 | tf_op jit(solution)/shard_map/project_out/pallas_call | solution.py:225
  157.0 2.6 %collective-permute-start.15 = (bf16[384,768]{1,0:T(8,128)(2,1)}, bf16[384,768]{1,0:T(8,128)(2,1)S(1)}, u32[]{:S(2)}, u32[]{:S(2)}) collective-permute-start(bf16[384,768]{1,0:T(8,128)(2,1)} %project_out.5), channel_id=1, source_target_pairs={{0,3},{1,2},{2,1},{3,0},{4,7},{5,6},{6,5},{7,4},{8,11},{9,10},{10,... | collective-permute-start | bytes 1769480 | tf_op jit(solution)/shard_map/ppermute | solution.py:42
  159.7 5.9 %project_out.6 = bf16[384,768]{1,0:T(8,128)(2,1)} custom-call(s32[1]{0:T(128)S(6)} %sub.21.part_ref, bf16[384,3072]{1,0:T(8,128)(2,1)} %copy-done.5, bf16[1536,3072]{1,0:T(8,128)(2,1)} %all-gather.2.cloned.1.call-done.w_ref), custom_call_target="tpu_custom_call" | custom-call | flops 1 | bytes 1 | tf_op jit(solution)/shard_map/project_out/pallas_call | solution.py:225
  167.9 6.1 %project_out.7.refs_4_ = f32[384,768]{1,0:T(8,128)} custom-call(s32[1]{0:T(128)S(6)} %sub.21.part_ref, bf16[384,3072]{1,0:T(8,128)(2,1)} %project_in.3.hidden_ref, bf16[1536,3072]{1,0:T(8,128)(2,1)} %all-gather.2.cloned.1.call-done.w_ref), custom_call_target="tpu_custom_call" | custom-call | flops 1 | bytes 1 | tf_op jit(solution)/shard_map/project_out/pallas_call | solution.py:225
  174.9 3.0 %collective-permute-done.15.refs_6_ = bf16[384,768]{1,0:T(8,128)(2,1)S(1)} collective-permute-done((bf16[384,768]{1,0:T(8,128)(2,1)}, bf16[384,768]{1,0:T(8,128)(2,1)S(1)}, u32[]{:S(2)}, u32[]{:S(2)}) %collective-permute-start.15) | collective-permute-done | bytes 589856 | tf_op jit(solution)/shard_map/ppermute | solution.py:42
  179.5 3.6 %finish.1 = bf16[384,1536]{1,0:T(8,128)(2,1)} custom-call(s32[1]{0:T(128)} %bitcast.part_ref.core_ref, bf16[384,512]{1,0:T(8,128)(2,1)} %attend.3.refs_0_, bf16[384,512]{1,0:T(8,128)(2,1)} %attend.4.refs_1_, bf16[384,512]{1,0:T(8,128)(2,1)} %attend.5.refs_0_.refs_2_, bf16[384,768]{1,0:T(8,128)(2,1)} %pad_maximum_fusion.5.refs_3_, ...), custom_call_target="tpu_custom_call" | custom-call | flops 1 | bytes 1 | tf_op jit(solution)/shard_map/finish/pallas_call | solution.py:267
  (77 shorter events, 19.9 us)
Async XLA Ops:
  6.5 45.2 %copy-start = (s32[64,27]{0,1:T(8,128)S(1)}, s32[64,27]{0,1:T(8,128)}, u32[]{:S(2)}) copy-start(s32[64,27]{0,1:T(8,128)} %param.20) | copy-start | bytes 20740
  6.5 136.0 %all-gather.2.cloned.1.call-start = ((), (), s32[]{:S(2)}) async-start(), calls=%async_computation | async-start | bytes 10027008 | tf_op jit(solution)/shard_map/all_gather | solution.py:341
  6.5 8.1 %collective-permute-start.1 = (bf16[48,3072]{1,0:T(8,128)(2,1)}, bf16[48,3072]{1,0:T(8,128)(2,1)S(1)}, u32[]{:S(2)}, u32[]{:S(2)}) collective-permute-start(bf16[48,3072]{1,0:T(8,128)(2,1)} %bitcast.8), channel_id=1, source_target_pairs={{0,64},{1,65},{2,66},{3,67},{4,68},{5,69},{6,70},{7,71},{8,72},{9,... | collective-permute-start | bytes 884744 | tf_op jit(solution)/shard_map/ppermute | solution.py:42
  9.2 7.1 %collective-permute-start = (bf16[768,512]{1,0:T(8,128)(2,1)S(1)}, bf16[768,512]{1,0:T(8,128)(2,1)S(1)}, u32[]{:S(2)}, u32[]{:S(2)}) collective-permute-start(bf16[768,512]{1,0:T(8,128)(2,1)S(1)} %pad_maximum_fusion.3), channel_id=1, source_target_pairs={{0,2},{1,3},{2,0},{3,1},{4,6},{5,7},{6,4},{7,5},{8,10},{9,11},{10,... | collective-permute-start | bytes 2359304 | tf_op jit(solution)/shard_map/ppermute | solution.py:42
  14.7 2.9 %collective-permute-start.3 = (bf16[48,3072]{1,0:T(8,128)(2,1)S(1)}, bf16[48,3072]{1,0:T(8,128)(2,1)S(1)}, u32[]{:S(2)}, u32[]{:S(2)}) collective-permute-start(bf16[48,3072]{1,0:T(8,128)(2,1)S(1)} %broadcast_select_fusion.3), channel_id=1, source_target_pairs={{0,2},{1,3},{2,0},{3,1},{4,6},{5,7},{6,4},{7,5},{8,10},{9,11},{10,... | collective-permute-start | bytes 884744 | tf_op jit(solution)/shard_map/ppermute | solution.py:42
  19.4 8.9 %collective-permute-start.4 = (bf16[768,1024]{1,0:T(8,128)(2,1)S(1)}, bf16[768,1024]{1,0:T(8,128)(2,1)S(1)}, u32[]{:S(2)}, u32[]{:S(2)}) collective-permute-start(bf16[768,1024]{1,0:T(8,128)(2,1)S(1)} %pad_maximum_fusion.2), channel_id=1, source_target_pairs={{0,2},{1,3},{2,0},{3,1},{4,6},{5,7},{6,4},{7,5},{8,10},{9,11},{10,... | collective-permute-start | bytes 4718600 | tf_op jit(solution)/shard_map/ppermute | solution.py:42
  19.7 28.9 %collective-permute-start.2 = (bf16[1536,512]{1,0:T(8,128)(2,1)}, bf16[1536,512]{1,0:T(8,128)(2,1)}, u32[]{:S(2)}, u32[]{:S(2)}) collective-permute-start(bf16[1536,512]{1,0:T(8,128)(2,1)} %pad_maximum_fusion.1.refs_0_), channel_id=1, source_target_pairs={{0,4},{1,5},{4,8},{5,9},{6,2},{7,3},{8,12},{9,13},{10,6},{11,7},{1... | collective-permute-start | bytes 4718600 | tf_op jit(solution)/shard_map/ppermute | solution.py:42
  28.4 20.2 %copy-start.2 = (s32[64]{0:T(128)S(1)}, s32[64]{0:T(128)}, u32[]{:S(2)}) copy-start(s32[64]{0:T(128)} %param.19) | copy-start | bytes 772
  28.4 22.1 %copy-start.13 = (s32[6]{0:T(128)S(1)}, s32[6]{0:T(128)}, u32[]{:S(2)}) copy-start(s32[6]{0:T(128)} %constant.77.clone) | copy-start | bytes 76
  28.8 32.3 %copy-start.3 = (bf16[1536,1024]{1,0:T(8,128)(2,1)}, bf16[1536,1024]{1,0:T(8,128)(2,1)S(1)}, u32[]{:S(2)}) copy-start(bf16[1536,1024]{1,0:T(8,128)(2,1)S(1)} %pad_maximum_fusion.refs_0_) | copy-start | bytes 9437188
  28.8 60.3 %collective-permute-start.6 = (bf16[1536,1024]{1,0:T(8,128)(2,1)S(1)}, bf16[1536,1024]{1,0:T(8,128)(2,1)}, u32[]{:S(2)}, u32[]{:S(2)}) collective-permute-start(bf16[1536,1024]{1,0:T(8,128)(2,1)S(1)} %pad_maximum_fusion.refs_0_), channel_id=1, source_target_pairs={{0,4},{1,5},{4,8},{5,9},{6,2},{7,3},{8,12},{9,13},{10,6},{11,7},{1... | collective-permute-start | bytes 9437192 | tf_op jit(solution)/shard_map/ppermute | solution.py:42
  48.6 4.0 %collective-permute-start.5 = (bf16[1536,512]{1,0:T(8,128)(2,1)}, bf16[1536,512]{1,0:T(8,128)(2,1)}, u32[]{:S(2)}, u32[]{:S(2)}) collective-permute-start(bf16[1536,512]{1,0:T(8,128)(2,1)} %collective-permute-done.2.refs_1_), channel_id=1, source_target_pairs={{0,2},{1,3},{2,0},{3,1},{4,6},{5,7},{6,4},{7,5},{8,10},{9,11},{10,... | collective-permute-start | bytes 4718600 | tf_op jit(solution)/shard_map/ppermute | solution.py:42
  61.1 28.0 %collective-permute-start.7 = (bf16[384,512]{1,0:T(8,128)(2,1)}, bf16[384,512]{1,0:T(8,128)(2,1)S(1)}, u32[]{:S(2)}, u32[]{:S(2)}) collective-permute-start(bf16[384,512]{1,0:T(8,128)(2,1)} %attend.3.refs_0_), channel_id=1, source_target_pairs={{0,1},{1,0},{2,3},{3,2},{4,5},{5,4},{6,7},{7,6},{8,9},{9,8},{10,11... | collective-permute-start | bytes 1179656 | tf_op jit(solution)/shard_map/ppermute | solution.py:42
  89.2 26.7 %copy-start.9 = (bf16[384,512]{1,0:T(8,128)(2,1)}, bf16[384,512]{1,0:T(8,128)(2,1)S(1)}, u32[]{:S(2)}) copy-start(bf16[384,512]{1,0:T(8,128)(2,1)S(1)} %collective-permute-done.7.refs_2_) | copy-start | bytes 1179652
  89.2 5.9 %collective-permute-start.8 = (bf16[1536,1024]{1,0:T(8,128)(2,1)}, bf16[1536,1024]{1,0:T(8,128)(2,1)S(1)}, u32[]{:S(2)}, u32[]{:S(2)}) collective-permute-start(bf16[1536,1024]{1,0:T(8,128)(2,1)} %collective-permute-done.6.refs_1_), channel_id=1, source_target_pairs={{0,2},{1,3},{2,0},{3,1},{4,6},{5,7},{6,4},{7,5},{8,10},{9,11},{10,... | collective-permute-start | bytes 9437192 | tf_op jit(solution)/shard_map/ppermute | solution.py:42
  105.2 12.3 %collective-permute-start.10 = (bf16[384,512]{1,0:T(8,128)(2,1)}, bf16[384,512]{1,0:T(8,128)(2,1)S(1)}, u32[]{:S(2)}, u32[]{:S(2)}) collective-permute-start(bf16[384,512]{1,0:T(8,128)(2,1)} %attend.4.refs_1_), channel_id=1, source_target_pairs={{0,1},{1,0},{2,3},{3,2},{4,5},{5,4},{6,7},{7,6},{8,9},{9,8},{10,11... | collective-permute-start | bytes 1179656 | tf_op jit(solution)/shard_map/ppermute | solution.py:42
  115.9 14.1 %collective-permute-start.9 = (bf16[384,512]{1,0:T(8,128)(2,1)}, bf16[384,512]{1,0:T(8,128)(2,1)S(1)}, u32[]{:S(2)}, u32[]{:S(2)}) collective-permute-start(bf16[384,512]{1,0:T(8,128)(2,1)} %attend.5.refs_0_.refs_2_), channel_id=1, source_target_pairs={{0,1},{1,0},{2,3},{3,2},{4,5},{5,4},{6,7},{7,6},{8,9},{9,8},{10,11... | collective-permute-start | bytes 1179656 | tf_op jit(solution)/shard_map/ppermute | solution.py:42
  140.5 9.2 %collective-permute-start.11 = (bf16[384,3072]{1,0:T(8,128)(2,1)}, bf16[384,3072]{1,0:T(8,128)(2,1)S(1)}, u32[]{:S(2)}, u32[]{:S(2)}) collective-permute-start(bf16[384,3072]{1,0:T(8,128)(2,1)} %project_in.3.hidden_ref), channel_id=1, source_target_pairs={{0,2},{1,3},{2,0},{3,1},{4,6},{5,7},{6,4},{7,5},{8,10},{9,11},{10,... | collective-permute-start | bytes 7077896 | tf_op jit(solution)/shard_map/ppermute | solution.py:42
  148.5 29.4 %collective-permute-start.14 = (bf16[384,768]{1,0:T(8,128)(2,1)}, bf16[384,768]{1,0:T(8,128)(2,1)S(1)}, u32[]{:S(2)}, u32[]{:S(2)}) collective-permute-start(bf16[384,768]{1,0:T(8,128)(2,1)} %project_out.4), channel_id=1, source_target_pairs={{0,1},{1,0},{2,3},{3,2},{4,5},{5,4},{6,7},{7,6},{8,9},{9,8},{10,11... | collective-permute-start | bytes 1769480 | tf_op jit(solution)/shard_map/ppermute | solution.py:42
  157.0 10.3 %copy-start.12 = (f32[3072]{0:T(1024)S(1)}, f32[3072]{0:T(1024)}, u32[]{:S(2)}) copy-start(f32[3072]{0:T(1024)} %param.18) | copy-start | bytes 36868
  157.0 20.9 %collective-permute-start.15 = (bf16[384,768]{1,0:T(8,128)(2,1)}, bf16[384,768]{1,0:T(8,128)(2,1)S(1)}, u32[]{:S(2)}, u32[]{:S(2)}) collective-permute-start(bf16[384,768]{1,0:T(8,128)(2,1)} %project_out.5), channel_id=1, source_target_pairs={{0,3},{1,2},{2,1},{3,0},{4,7},{5,6},{6,5},{7,4},{8,11},{9,10},{10,... | collective-permute-start | bytes 1769480 | tf_op jit(solution)/shard_map/ppermute | solution.py:42
  166.7 7.3 %collective-permute-start.12 = (bf16[384,384]{1,0:T(8,128)(2,1)S(1)}, bf16[384,384]{1,0:T(8,128)(2,1)S(1)}, u32[]{:S(2)}, u32[]{:S(2)}) collective-permute-start(bf16[384,384]{1,0:T(8,128)(2,1)S(1)} %get-tuple-element.43), channel_id=1, source_target_pairs={{0,2},{1,3},{2,0},{3,1},{4,6},{5,7},{6,4},{7,5},{8,10},{9,11},{10,... | collective-permute-start | bytes 884744 | tf_op jit(solution)/shard_map/ppermute | solution.py:42
  166.8 7.2 %collective-permute-start.13 = (bf16[384,384]{1,0:T(8,128)(2,1)S(1)}, bf16[384,384]{1,0:T(8,128)(2,1)S(1)}, u32[]{:S(2)}, u32[]{:S(2)}) collective-permute-start(bf16[384,384]{1,0:T(8,128)(2,1)S(1)} %get-tuple-element.44), channel_id=1, source_target_pairs={{0,2},{1,3},{2,0},{3,1},{4,6},{5,7},{6,4},{7,5},{8,10},{9,11},{10,... | collective-permute-start | bytes 884744 | tf_op jit(solution)/shard_map/ppermute | solution.py:42
  174.0 9.1 %copy-start.1 = (s32[64,27]{0,1:T(8,128)S(1)}, s32[64,27]{0,1:T(8,128)}, u32[]{:S(2)}) copy-start(s32[64,27]{0,1:T(8,128)} %param.20) | copy-start | bytes 20740
  (9 other events, 17.2 us)
Sparse Core Ops, SparseCore 0:
  18.7 123.8 all-gather.1

commit v3 on v2

--- a/solution.py
+++ b/solution.py
@@ -16,10 +16,11 @@
 PIECE = 48
 BLOCK = 384
 QUARTER = 768
-FRAME_CHUNKS = (4, 8)
+FRAME_CHUNKS = (8, 4)
 LOG2_SCALE = math.log2(math.e) / math.sqrt(HEAD_DIM)
 AXES = ("seq", "hid")
 VMEM_BYTES = 56 << 20
+SMALL_VMEM_BYTES = 24 << 20
 LIGHT = pl.CostEstimate(flops=1, bytes_accessed=1, transcendentals=0)
 
 
@@ -119,7 +120,7 @@
         grid=(heads // 2,),
         in_specs=[pl.BlockSpec(memory_space=pltpu.SMEM)] + [tall(TILE, first)] * 2 + [tall(4 * TILE, near)] * 3,
         out_specs=tall(TILE, 0),
-        compiler_params=pltpu.CompilerParams(vmem_limit_bytes=VMEM_BYTES),
+        compiler_params=pltpu.CompilerParams(vmem_limit_bytes=SMALL_VMEM_BYTES),
         cost_estimate=LIGHT,
         name="attend",
     )(bias, queries, residual, both, mine, theirs)
@@ -221,7 +222,7 @@
 
 
 def project_out(part, hidden, w_rows, dtype):
-    cols = 384
+    cols = 256
     return pl.pallas_call(
         project_out_kernel,
         out_shape=jax.ShapeDtypeStruct((TILE, QUARTER), dtype),
@@ -269,7 +270,7 @@
         out_shape=jax.ShapeDtypeStruct((TILE, HALF), jnp.bfloat16),
         in_specs=[pl.BlockSpec(memory_space=pltpu.SMEM)] + [vmem] * (len(combined) + 5),
         out_specs=vmem,
-        compiler_params=pltpu.CompilerParams(vmem_limit_bytes=VMEM_BYTES),
+        compiler_params=pltpu.CompilerParams(vmem_limit_bytes=SMALL_VMEM_BYTES),
         cost_estimate=LIGHT,
         name="finish",
     )(core, *combined, kept_there, kept_here, received_here, received_there, gate)
@@ -331,12 +332,11 @@
     piece_x = moved(piece, along_x)
     pack_0 = after(pack(0), piece)
     other_0 = swap(pack_0)
-    piece_x = after(piece_x, pack_0)
+    done = send_frame(pack_0, other_0)
+    piece_x = after(piece_x, done)
     w_hold = jnp.where(own_is_other_half == gives_other_half, piece, piece_x)
     w_pass = jnp.where(own_is_other_half == gives_other_half, piece_x, piece)
     w_take = swap(w_pass)
-    done = send_frame(pack_0, after(other_0, w_pass))
-    w_take = after(w_take, done)
     w_chip = join(jnp.where(core == 0, w_hold, w_take), jnp.where(core == 0, w_take, w_hold))
     w_rows = lax.all_gather(w_chip, "seq", axis=0, tiled=True, axis_index_groups=same)
     pack_1 = after(pack(1), w_chip)
@@ -345,12 +345,11 @@
     mine[0] = after(mine[0], done)
     theirs.append(swap(mine[0]))
     done = attend_heads(0, 0, 4)
-    mine[1] = after(mine[1], done, others[0])
+    done = attend_heads(0, 4, 4, done)
+    mine[1] = after(mine[1], done)
     theirs.append(swap(mine[1]))
     done = attend_heads(1, 0, 4)
-    done = attend_heads(1, 4, 4, done)
-    earlier = project_in(after(hid_1, done), own[:2], others[:2], 0, 512, mod_scale, w_in)
-    hidden = project_in(hid_1, own[2:], others[2:], 1024, 512, mod_scale, w_in, earlier, is_last=True)
+    hidden = project_in(after(hid_1, done), own, others, 0, HALF, mod_scale, w_in, is_last=True)
     hidden_there = swap(hidden)
     core_1 = core.reshape(1)
     sent_here = project_out(core_1, hidden, w_rows, jnp.bfloat16)

time: 191 us -> 189 us (0.990)
  Pallas kernels: 74.5 us -> 62.7 us
  waiting for transfers between devices: 58.8 us -> 65.7 us
  starting transfers between devices: 24.3 us -> 31 us
  local copies, waits for them, and re-layouts: 12.5 us -> 9.18 us
    ppermute x16, waiting for transfers between devices: 57.7 us -> 65.7 us  [moved(): return lax.ppermute(value, AXES, pairs)]
    pallas_call x2 -> x1, Pallas kernels: 21.5 us -> 14.7 us  [project_in(): pl.pallas_call(functools.partial(project_in_kernel, (len(own), len(other)...]
    ppermute x16, starting transfers between devices: 24.3 us -> 31 us  [moved(): return lax.ppermute(value, AXES, pairs)]
    pallas_call x3, Pallas kernels: 25.5 us -> 22.5 us  [attend(): pl.pallas_call(attend_kernel, out_shape=jax.ShapeDtypeStruct((TILE, heads...]
    pallas_call x1, Pallas kernels: 3.61 us -> 1.52 us  [finish(): pl.pallas_call(functools.partial(finish_kernel, len(combined)), out_shape...]
    unnamed x28 -> x38, local copies, waits for them, and re-layouts: 6.21 us -> 4.86 us
  transfers between devices with their start and end apart: 17 -> 17, of which waited for: 7 -> 9; matrix products, arithmetic and copies ran while one was open for 5% -> 3% of each run, Pallas kernels for 37% -> 33%
where the time goes in v3:
time: 189 us; the launch traced here: 188 us
  waiting for transfers between devices  65.7 us (35%)
  Pallas kernels  62.7 us (33%)
  starting transfers between devices  31 us (16%)
  between operations  15.4 us (8%)
  local copies, waits for them, and re-layouts  9.18 us (5%)
  other arithmetic  3.98 us (2%)
    ppermute x16, waiting for transfers between devices, moved(): return lax.ppermute(value, AXES, pairs)  65.7 us
    ppermute x16, starting transfers between devices, moved(): return lax.ppermute(value, AXES, pairs)  31 us
    pallas_call x4, Pallas kernels, project_out(): pl.pallas_call(project_out_kernel, out_shape=jax.ShapeDtypeStruct((TILE,...  24 us
    pallas_call x3, Pallas kernels, attend(): pl.pallas_call(attend_kernel, out_shape=jax.ShapeDtypeStruct((TILE, heads...  22.5 us
    pallas_call x1, Pallas kernels, project_in(): pl.pallas_call(functools.partial(project_in_kernel, (len(own), len(other)...  14.7 us
    unnamed x38, local copies, waits for them, and re-layouts  4.86 us
  transfers between devices with their start and end apart: 17, of which 9 were waited for; matrix products, arithmetic and copies ran while one was open for 3% of the time, Pallas kernels for 33%

profile of v3, /device:TPU:7, one launch (start us, length us, event | category | flops | bytes accessed | tf_op | source)
XLA Modules:
  0.0 188.0 jit_solution(4151656436995727776)
XLA Ops:
  9.6 2.3 %collective-permute-done = bf16[768,1024]{1,0:T(8,128)(2,1)S(1)} collective-permute-done((bf16[768,1024]{1,0:T(8,128)(2,1)S(1)}, bf16[768,1024]{1,0:T(8,128)(2,1)S(1)}, u32[]{:S(2)}, u32[]{:S(2)}) %collective-permute-start) | collective-permute-done | bytes 1572896 | tf_op jit(solution)/shard_map/ppermute | solution.py:43
  12.4 4.5 %collective-permute-done.2 = bf16[48,3072]{1,0:T(8,128)(2,1)} collective-permute-done((bf16[48,3072]{1,0:T(8,128)(2,1)S(1)}, bf16[48,3072]{1,0:T(8,128)(2,1)}, u32[]{:S(2)}, u32[]{:S(2)}) %collective-permute-start.2) | collective-permute-done | bytes 294944 | tf_op jit(solution)/shard_map/ppermute | solution.py:43
  20.7 8.5 %collective-permute-start.1 = (bf16[1536,1024]{1,0:T(8,128)(2,1)S(1)}, bf16[1536,1024]{1,0:T(8,128)(2,1)}, u32[]{:S(2)}, u32[]{:S(2)}) collective-permute-start(bf16[1536,1024]{1,0:T(8,128)(2,1)S(1)} %pad_maximum_fusion.refs_0_), channel_id=1, source_target_pairs={{0,4},{1,5},{4,8},{5,9},{6,2},{7,3},{8,12},{9,13},{10,6},{11,7},{1... | collective-permute-start | bytes 9437192 | tf_op jit(solution)/shard_map/ppermute | solution.py:43
  29.5 2.2 %collective-permute-done.4 = bf16[768,512]{1,0:T(8,128)(2,1)S(1)} collective-permute-done((bf16[768,512]{1,0:T(8,128)(2,1)S(1)}, bf16[768,512]{1,0:T(8,128)(2,1)S(1)}, u32[]{:S(2)}, u32[]{:S(2)}) %collective-permute-start.4) | collective-permute-done | bytes 786464 | tf_op jit(solution)/shard_map/ppermute | solution.py:43
  33.0 33.4 %collective-permute-done.1.refs_1_ = bf16[1536,1024]{1,0:T(8,128)(2,1)} collective-permute-done((bf16[1536,1024]{1,0:T(8,128)(2,1)S(1)}, bf16[1536,1024]{1,0:T(8,128)(2,1)}, u32[]{:S(2)}, u32[]{:S(2)}) %collective-permute-start.1) | collective-permute-done | bytes 3145760 | tf_op jit(solution)/shard_map/ppermute | solution.py:43
  66.4 11.3 %collective-permute-start.6 = (bf16[1536,512]{1,0:T(8,128)(2,1)}, bf16[1536,512]{1,0:T(8,128)(2,1)}, u32[]{:S(2)}, u32[]{:S(2)}) collective-permute-start(bf16[1536,512]{1,0:T(8,128)(2,1)} %pad_maximum_fusion.2.refs_0_), channel_id=1, source_target_pairs={{0,4},{1,5},{4,8},{5,9},{6,2},{7,3},{8,12},{9,13},{10,6},{11,7},{1... | collective-permute-start | bytes 4718600 | tf_op jit(solution)/shard_map/ppermute | solution.py:43
  81.1 1.3 copy-done.2
  82.3 1.3 copy-done.3
  83.6 7.5 %attend.3.refs_0_ = bf16[384,512]{1,0:T(8,128)(2,1)S(1)} custom-call(f32[6]{0:T(128)S(1)} %and_select_fusion.bias_ref, bf16[384,1536]{1,0:T(8,128)(2,1)S(1)} %copy-done.2, bf16[384,1536]{1,0:T(8,128)(2,1)S(1)} %copy-done.3, bf16[1536,1024]{1,0:T(8,128)(2,1)S(1)} %pad_maximum_fusion.refs_0_, bf16[1536,1024]{1,0:T(8,128)(2,1)} %collective-permute-done.1.refs_1_, ...), custom_call_target="tpu_custom_call" | custom-call | flops 1 | bytes 1 | tf_op jit(solution)/shard_map/attend/pallas_call | solution.py:117
  91.1 7.6 %attend.4.refs_1_ = bf16[384,512]{1,0:T(8,128)(2,1)S(1)} custom-call(f32[6]{0:T(128)S(1)} %and_select_fusion.bias_ref, bf16[384,1536]{1,0:T(8,128)(2,1)S(1)} %copy-done.2, bf16[384,1536]{1,0:T(8,128)(2,1)S(1)} %copy-done.3, bf16[1536,1024]{1,0:T(8,128)(2,1)S(1)} %pad_maximum_fusion.refs_0_, bf16[1536,1024]{1,0:T(8,128)(2,1)} %collective-permute-done.1.refs_1_, ...), custom_call_target="tpu_custom_call" | custom-call | flops 1 | bytes 1 | tf_op jit(solution)/shard_map/attend/pallas_call | solution.py:117
  99.7 2.1 %collective-permute-start.8 = (bf16[384,512]{1,0:T(8,128)(2,1)S(1)}, bf16[384,512]{1,0:T(8,128)(2,1)S(1)}, u32[]{:S(2)}, u32[]{:S(2)}) collective-permute-start(bf16[384,512]{1,0:T(8,128)(2,1)S(1)} %attend.3.refs_0_), channel_id=1, source_target_pairs={{0,1},{1,0},{2,3},{3,2},{4,5},{5,4},{6,7},{7,6},{8,9},{9,8},{10,11... | collective-permute-start | bytes 1179656 | tf_op jit(solution)/shard_map/ppermute | solution.py:43
  102.4 7.4 %attend.5.refs_2_ = bf16[384,512]{1,0:T(8,128)(2,1)S(1)} custom-call(f32[6]{0:T(128)S(1)} %and_select_fusion.bias_ref, bf16[384,1536]{1,0:T(8,128)(2,1)S(1)} %copy-done.2, bf16[384,1536]{1,0:T(8,128)(2,1)S(1)} %copy-done.3, bf16[1536,512]{1,0:T(8,128)(2,1)} %pad_maximum_fusion.2.refs_0_, bf16[1536,512]{1,0:T(8,128)(2,1)} %collective-permute-done.6.refs_1_, ...), custom_call_target="tpu_custom_call" | custom-call | flops 1 | bytes 1 | tf_op jit(solution)/shard_map/attend/pallas_call | solution.py:117
  110.8 8.3 %collective-permute-done.8.refs_3_ = bf16[384,512]{1,0:T(8,128)(2,1)S(1)} collective-permute-done((bf16[384,512]{1,0:T(8,128)(2,1)S(1)}, bf16[384,512]{1,0:T(8,128)(2,1)S(1)}, u32[]{:S(2)}, u32[]{:S(2)}) %collective-permute-start.8) | collective-permute-done | bytes 393248 | tf_op jit(solution)/shard_map/ppermute | solution.py:43
  119.1 8.4 %collective-permute-done.10.refs_5_ = bf16[384,512]{1,0:T(8,128)(2,1)S(1)} collective-permute-done((bf16[384,512]{1,0:T(8,128)(2,1)S(1)}, bf16[384,512]{1,0:T(8,128)(2,1)S(1)}, u32[]{:S(2)}, u32[]{:S(2)}) %collective-permute-start.10) | collective-permute-done | bytes 393248 | tf_op jit(solution)/shard_map/ppermute | solution.py:43
  128.3 14.7 %project_in.1.hidden_ref = bf16[384,3072]{1,0:T(8,128)(2,1)} custom-call(s32[1]{0:T(128)} %bitcast.3.hid_ref, bf16[384,512]{1,0:T(8,128)(2,1)} %copy-done.5, bf16[384,512]{1,0:T(8,128)(2,1)} %copy-done.7, bf16[384,512]{1,0:T(8,128)(2,1)} %copy-done.9, bf16[384,512]{1,0:T(8,128)(2,1)} %copy-done.15, bf16[384,512]{1,0:T(8,128)(2,1)} %copy-done.14, ...), custom_call_target="tpu_custom_call" | custom-call | flops 1 | bytes 1 | tf_op jit(solution)/shard_map/project_in/pallas_call | solution.py:202
  143.0 1.3 collective-permute-start.11
  144.2 6.0 %project_out.4 = bf16[384,768]{1,0:T(8,128)(2,1)} custom-call(s32[1]{0:T(128)} %bitcast.part_ref.core_ref, bf16[384,3072]{1,0:T(8,128)(2,1)} %project_in.1.hidden_ref, bf16[1536,3072]{1,0:T(8,128)(2,1)} %all-gather.2.cloned.1.call-done.w_ref), custom_call_target="tpu_custom_call" | custom-call | flops 1 | bytes 1 | tf_op jit(solution)/shard_map/project_out/pallas_call | solution.py:226
  151.0 1.4 copy-done.12
  152.4 5.9 %project_out.5 = bf16[384,768]{1,0:T(8,128)(2,1)} custom-call(s32[1]{0:T(128)} %bitcast.part_ref.core_ref, bf16[384,3072]{1,0:T(8,128)(2,1)} %copy-done.12, bf16[1536,3072]{1,0:T(8,128)(2,1)} %all-gather.2.cloned.1.call-done.w_ref), custom_call_target="tpu_custom_call" | custom-call | flops 1 | bytes 1 | tf_op jit(solution)/shard_map/project_out/pallas_call | solution.py:226
  158.4 2.4 %collective-permute-start.15 = (bf16[384,768]{1,0:T(8,128)(2,1)}, bf16[384,768]{1,0:T(8,128)(2,1)S(1)}, u32[]{:S(2)}, u32[]{:S(2)}) collective-permute-start(bf16[384,768]{1,0:T(8,128)(2,1)} %project_out.5), channel_id=1, source_target_pairs={{0,3},{1,2},{2,1},{3,0},{4,7},{5,6},{6,5},{7,4},{8,11},{9,10},{10,... | collective-permute-start | bytes 1769480 | tf_op jit(solution)/shard_map/ppermute | solution.py:43
  160.7 5.9 %project_out.6 = bf16[384,768]{1,0:T(8,128)(2,1)} custom-call(s32[1]{0:T(128)S(6)} %sub.21.part_ref, bf16[384,3072]{1,0:T(8,128)(2,1)} %copy-done.12, bf16[1536,3072]{1,0:T(8,128)(2,1)} %all-gather.2.cloned.1.call-done.w_ref), custom_call_target="tpu_custom_call" | custom-call | flops 1 | bytes 1 | tf_op jit(solution)/shard_map/project_out/pallas_call | solution.py:226
  168.5 6.2 %project_out.7.refs_4_ = f32[384,768]{1,0:T(8,128)} custom-call(s32[1]{0:T(128)S(6)} %sub.21.part_ref, bf16[384,3072]{1,0:T(8,128)(2,1)} %project_in.1.hidden_ref, bf16[1536,3072]{1,0:T(8,128)(2,1)} %all-gather.2.cloned.1.call-done.w_ref), custom_call_target="tpu_custom_call" | custom-call | flops 1 | bytes 1 | tf_op jit(solution)/shard_map/project_out/pallas_call | solution.py:226
  174.8 4.8 %collective-permute-done.15.refs_6_ = bf16[384,768]{1,0:T(8,128)(2,1)S(1)} collective-permute-done((bf16[384,768]{1,0:T(8,128)(2,1)}, bf16[384,768]{1,0:T(8,128)(2,1)S(1)}, u32[]{:S(2)}, u32[]{:S(2)}) %collective-permute-start.15) | collective-permute-done | bytes 589856 | tf_op jit(solution)/shard_map/ppermute | solution.py:43
  179.6 1.5 finish.1
  (88 shorter events, 16.4 us)
Async XLA Ops:
  6.5 74.1 %copy-start = (s32[64,27]{0,1:T(8,128)S(1)}, s32[64,27]{0,1:T(8,128)}, u32[]{:S(2)}) copy-start(s32[64,27]{0,1:T(8,128)} %param.20) | copy-start | bytes 20740
  6.5 137.7 %all-gather.2.cloned.1.call-start = ((), (), s32[]{:S(2)}) async-start(), calls=%async_computation | async-start | bytes 10027008 | tf_op jit(solution)/shard_map/all_gather | solution.py:341
  8.0 3.8 %collective-permute-start = (bf16[768,1024]{1,0:T(8,128)(2,1)S(1)}, bf16[768,1024]{1,0:T(8,128)(2,1)S(1)}, u32[]{:S(2)}, u32[]{:S(2)}) collective-permute-start(bf16[768,1024]{1,0:T(8,128)(2,1)S(1)} %pad_maximum_fusion.1), channel_id=1, source_target_pairs={{0,2},{1,3},{2,0},{3,1},{4,6},{5,7},{6,4},{7,5},{8,10},{9,11},{10,... | collective-permute-start | bytes 4718600 | tf_op jit(solution)/shard_map/ppermute | solution.py:43
  8.9 8.0 %collective-permute-start.2 = (bf16[48,3072]{1,0:T(8,128)(2,1)S(1)}, bf16[48,3072]{1,0:T(8,128)(2,1)}, u32[]{:S(2)}, u32[]{:S(2)}) collective-permute-start(bf16[48,3072]{1,0:T(8,128)(2,1)S(1)} %bitcast.8), channel_id=1, source_target_pairs={{0,64},{1,65},{2,66},{3,67},{4,68},{5,69},{6,70},{7,71},{8,72},{9,... | collective-permute-start | bytes 884744 | tf_op jit(solution)/shard_map/ppermute | solution.py:43
  17.9 1.9 collective-permute-start.3
  20.7 45.7 %collective-permute-start.1 = (bf16[1536,1024]{1,0:T(8,128)(2,1)S(1)}, bf16[1536,1024]{1,0:T(8,128)(2,1)}, u32[]{:S(2)}, u32[]{:S(2)}) collective-permute-start(bf16[1536,1024]{1,0:T(8,128)(2,1)S(1)} %pad_maximum_fusion.refs_0_), channel_id=1, source_target_pairs={{0,4},{1,5},{4,8},{5,9},{6,2},{7,3},{8,12},{9,13},{10,6},{11,7},{1... | collective-permute-start | bytes 9437192 | tf_op jit(solution)/shard_map/ppermute | solution.py:43
  29.3 2.4 %collective-permute-start.4 = (bf16[768,512]{1,0:T(8,128)(2,1)S(1)}, bf16[768,512]{1,0:T(8,128)(2,1)S(1)}, u32[]{:S(2)}, u32[]{:S(2)}) collective-permute-start(bf16[768,512]{1,0:T(8,128)(2,1)S(1)} %pad_maximum_fusion.3), channel_id=1, source_target_pairs={{0,2},{1,3},{2,0},{3,1},{4,6},{5,7},{6,4},{7,5},{8,10},{9,11},{10,... | collective-permute-start | bytes 2359304 | tf_op jit(solution)/shard_map/ppermute | solution.py:43
  31.7 46.0 %copy-start.11 = (s32[64]{0:T(128)S(1)}, s32[64]{0:T(128)}, u32[]{:S(2)}) copy-start(s32[64]{0:T(128)} %param.19) | copy-start | bytes 772
  31.7 47.7 %copy-start.18 = (s32[6]{0:T(128)S(1)}, s32[6]{0:T(128)}, u32[]{:S(2)}) copy-start(s32[6]{0:T(128)} %constant.77.clone) | copy-start | bytes 76
  66.4 14.7 %collective-permute-start.5 = (bf16[1536,1024]{1,0:T(8,128)(2,1)}, bf16[1536,1024]{1,0:T(8,128)(2,1)}, u32[]{:S(2)}, u32[]{:S(2)}) collective-permute-start(bf16[1536,1024]{1,0:T(8,128)(2,1)} %collective-permute-done.1.refs_1_), channel_id=1, source_target_pairs={{0,2},{1,3},{2,0},{3,1},{4,6},{5,7},{6,4},{7,5},{8,10},{9,11},{10,... | collective-permute-start | bytes 9437192 | tf_op jit(solution)/shard_map/ppermute | solution.py:43
  66.4 32.4 %collective-permute-start.6 = (bf16[1536,512]{1,0:T(8,128)(2,1)}, bf16[1536,512]{1,0:T(8,128)(2,1)}, u32[]{:S(2)}, u32[]{:S(2)}) collective-permute-start(bf16[1536,512]{1,0:T(8,128)(2,1)} %pad_maximum_fusion.2.refs_0_), channel_id=1, source_target_pairs={{0,4},{1,5},{4,8},{5,9},{6,2},{7,3},{8,12},{9,13},{10,6},{11,7},{1... | collective-permute-start | bytes 4718600 | tf_op jit(solution)/shard_map/ppermute | solution.py:43
  98.7 11.2 %copy-start.7 = (bf16[384,512]{1,0:T(8,128)(2,1)}, bf16[384,512]{1,0:T(8,128)(2,1)S(1)}, u32[]{:S(2)}) copy-start(bf16[384,512]{1,0:T(8,128)(2,1)S(1)} %attend.4.refs_1_) | copy-start | bytes 1179652
  98.7 3.7 %collective-permute-start.7 = (bf16[1536,512]{1,0:T(8,128)(2,1)}, bf16[1536,512]{1,0:T(8,128)(2,1)S(1)}, u32[]{:S(2)}, u32[]{:S(2)}) collective-permute-start(bf16[1536,512]{1,0:T(8,128)(2,1)} %collective-permute-done.6.refs_1_), channel_id=1, source_target_pairs={{0,2},{1,3},{2,0},{3,1},{4,6},{5,7},{6,4},{7,5},{8,10},{9,11},{10,... | collective-permute-start | bytes 4718600 | tf_op jit(solution)/shard_map/ppermute | solution.py:43
  98.8 12.0 %collective-permute-start.9 = (bf16[384,512]{1,0:T(8,128)(2,1)S(1)}, bf16[384,512]{1,0:T(8,128)(2,1)S(1)}, u32[]{:S(2)}, u32[]{:S(2)}) collective-permute-start(bf16[384,512]{1,0:T(8,128)(2,1)S(1)} %attend.4.refs_1_), channel_id=1, source_target_pairs={{0,1},{1,0},{2,3},{3,2},{4,5},{5,4},{6,7},{7,6},{8,9},{9,8},{10,11... | collective-permute-start | bytes 1179656 | tf_op jit(solution)/shard_map/ppermute | solution.py:43
  99.7 19.4 %collective-permute-start.8 = (bf16[384,512]{1,0:T(8,128)(2,1)S(1)}, bf16[384,512]{1,0:T(8,128)(2,1)S(1)}, u32[]{:S(2)}, u32[]{:S(2)}) collective-permute-start(bf16[384,512]{1,0:T(8,128)(2,1)S(1)} %attend.3.refs_0_), channel_id=1, source_target_pairs={{0,1},{1,0},{2,3},{3,2},{4,5},{5,4},{6,7},{7,6},{8,9},{9,8},{10,11... | collective-permute-start | bytes 1179656 | tf_op jit(solution)/shard_map/ppermute | solution.py:43
  109.9 17.7 %copy-start.9 = (bf16[384,512]{1,0:T(8,128)(2,1)}, bf16[384,512]{1,0:T(8,128)(2,1)S(1)}, u32[]{:S(2)}) copy-start(bf16[384,512]{1,0:T(8,128)(2,1)S(1)} %attend.5.refs_2_) | copy-start | bytes 1179652
  109.9 17.7 %collective-permute-start.10 = (bf16[384,512]{1,0:T(8,128)(2,1)S(1)}, bf16[384,512]{1,0:T(8,128)(2,1)S(1)}, u32[]{:S(2)}, u32[]{:S(2)}) collective-permute-start(bf16[384,512]{1,0:T(8,128)(2,1)S(1)} %attend.5.refs_2_), channel_id=1, source_target_pairs={{0,1},{1,0},{2,3},{3,2},{4,5},{5,4},{6,7},{7,6},{8,9},{9,8},{10,11... | collective-permute-start | bytes 1179656 | tf_op jit(solution)/shard_map/ppermute | solution.py:43
  110.8 16.8 %copy-start.14 = (bf16[384,512]{1,0:T(8,128)(2,1)}, bf16[384,512]{1,0:T(8,128)(2,1)S(1)}, u32[]{:S(2)}) copy-start(bf16[384,512]{1,0:T(8,128)(2,1)S(1)} %collective-permute-done.9.refs_4_) | copy-start | bytes 1179652
  143.0 8.0 %collective-permute-start.11 = (bf16[384,3072]{1,0:T(8,128)(2,1)}, bf16[384,3072]{1,0:T(8,128)(2,1)S(1)}, u32[]{:S(2)}, u32[]{:S(2)}) collective-permute-start(bf16[384,3072]{1,0:T(8,128)(2,1)} %project_in.1.hidden_ref), channel_id=1, source_target_pairs={{0,2},{1,3},{2,0},{3,1},{4,6},{5,7},{6,4},{7,5},{8,10},{9,11},{10,... | collective-permute-start | bytes 7077896 | tf_op jit(solution)/shard_map/ppermute | solution.py:43
  150.2 29.4 %collective-permute-start.14 = (bf16[384,768]{1,0:T(8,128)(2,1)}, bf16[384,768]{1,0:T(8,128)(2,1)S(1)}, u32[]{:S(2)}, u32[]{:S(2)}) collective-permute-start(bf16[384,768]{1,0:T(8,128)(2,1)} %project_out.4), channel_id=1, source_target_pairs={{0,1},{1,0},{2,3},{3,2},{4,5},{5,4},{6,7},{7,6},{8,9},{9,8},{10,11... | collective-permute-start | bytes 1769480 | tf_op jit(solution)/shard_map/ppermute | solution.py:43
  158.4 21.2 %collective-permute-start.15 = (bf16[384,768]{1,0:T(8,128)(2,1)}, bf16[384,768]{1,0:T(8,128)(2,1)S(1)}, u32[]{:S(2)}, u32[]{:S(2)}) collective-permute-start(bf16[384,768]{1,0:T(8,128)(2,1)} %project_out.5), channel_id=1, source_target_pairs={{0,3},{1,2},{2,1},{3,0},{4,7},{5,6},{6,5},{7,4},{8,11},{9,10},{10,... | collective-permute-start | bytes 1769480 | tf_op jit(solution)/shard_map/ppermute | solution.py:43
  167.8 6.9 %collective-permute-start.12 = (bf16[384,384]{1,0:T(8,128)(2,1)S(1)}, bf16[384,384]{1,0:T(8,128)(2,1)S(1)}, u32[]{:S(2)}, u32[]{:S(2)}) collective-permute-start(bf16[384,384]{1,0:T(8,128)(2,1)S(1)} %get-tuple-element.35), channel_id=1, source_target_pairs={{0,2},{1,3},{2,0},{3,1},{4,6},{5,7},{6,4},{7,5},{8,10},{9,11},{10,... | collective-permute-start | bytes 884744 | tf_op jit(solution)/shard_map/ppermute | solution.py:43
  168.0 6.6 %collective-permute-start.13 = (bf16[384,384]{1,0:T(8,128)(2,1)S(1)}, bf16[384,384]{1,0:T(8,128)(2,1)S(1)}, u32[]{:S(2)}, u32[]{:S(2)}) collective-permute-start(bf16[384,384]{1,0:T(8,128)(2,1)S(1)} %get-tuple-element.36), channel_id=1, source_target_pairs={{0,2},{1,3},{2,0},{3,1},{4,6},{5,7},{6,4},{7,5},{8,10},{9,11},{10,... | collective-permute-start | bytes 884744 | tf_op jit(solution)/shard_map/ppermute | solution.py:43
  168.5 11.1 %copy-start.6 = (bf16[384,512]{1,0:T(8,128)(2,1)S(1)}, bf16[384,512]{1,0:T(8,128)(2,1)}, u32[]{:S(2)}) copy-start(bf16[384,512]{1,0:T(8,128)(2,1)} %copy-done.5) | copy-start | bytes 1179652
  (16 other events, 86.9 us)
Sparse Core Ops, SparseCore 0:
  20.8 118.4 all-gather.1

commit v4 on v3

--- a/solution.py
+++ b/solution.py
@@ -150,7 +150,7 @@
 def project_in_kernel(counts, blocks, first, has_earlier, is_last, hid_ref, *refs):
     own, other = refs[: counts[0]], refs[counts[0] : sum(counts)]
     scale_ref, *refs = refs[sum(counts) :]
-    weights, refs = refs[: 2 * blocks], list(refs[2 * blocks :])
+    weights, refs = refs[:blocks], list(refs[blocks:])
     acc_ref, earlier_square_ref = (refs.pop(0), refs.pop(0)) if has_earlier else (None, None)
     out_ref = refs.pop(0)
     square_ref, held_ref = refs
@@ -174,9 +174,9 @@
 
 def project_in(hid, own, other, first, rows, mod_scale, w_in, earlier=None, is_last=False):
     cols = 512
-    depth = sum(v.shape[1] for v in own)
-    blocks = depth // rows
-    assert first % rows == 0 and depth % rows == 0 and HALF % rows == 0
+    depths = [sum(v.shape[1] for v in group) for group in (own, other)]
+    blocks = [(half, i) for half, depth in enumerate(depths) for i in range(depth // rows)]
+    assert first % rows == 0 and HALF % rows == 0 and all(depth % rows == 0 for depth in depths)
     whole = lambda v: pl.BlockSpec(v.shape, lambda i, h: (0, 0))
     column = pl.BlockSpec((TILE, cols), lambda i, h: (0, i))
     one = jax.ShapeDtypeStruct((TILE, 1), jnp.float32)
@@ -187,9 +187,9 @@
         return pl.BlockSpec((rows, cols), lambda j, h: ((h[0] if half == 0 else 1 - h[0]) * (HALF // rows) + at, j))
 
     in_specs = [whole(v) for v in own + other] + [whole(scale)]
-    in_specs += [block(half, i) for half in (0, 1) for i in range(blocks)]
-    operands = [*own, *other, scale] + [w_in] * (2 * blocks)
-    scratch = [pltpu.VMEM((TILE, 2 * depth), jnp.bfloat16)]
+    in_specs += [block(half, i) for half, i in blocks]
+    operands = [*own, *other, scale] + [w_in] * len(blocks)
+    scratch = [pltpu.VMEM((TILE, sum(depths)), jnp.bfloat16)]
     if earlier is not None:
         in_specs += [column, whole(one)]
         operands += earlier
@@ -200,7 +200,7 @@
         out_shape = (jax.ShapeDtypeStruct((TILE, UNITS), jnp.float32), one)
         out_specs = (column, whole(one))
     return pl.pallas_call(
-        functools.partial(project_in_kernel, (len(own), len(other)), blocks, first, earlier is not None, is_last),
+        functools.partial(project_in_kernel, (len(own), len(other)), len(blocks), first, earlier is not None, is_last),
         out_shape=out_shape,
         grid_spec=pltpu.PrefetchScalarGridSpec(
             num_scalar_prefetch=1,
@@ -332,11 +332,12 @@
     piece_x = moved(piece, along_x)
     pack_0 = after(pack(0), piece)
     other_0 = swap(pack_0)
-    done = send_frame(pack_0, other_0)
-    piece_x = after(piece_x, done)
+    piece_x = after(piece_x, pack_0)
     w_hold = jnp.where(own_is_other_half == gives_other_half, piece, piece_x)
     w_pass = jnp.where(own_is_other_half == gives_other_half, piece_x, piece)
     w_take = swap(w_pass)
+    done = send_frame(pack_0, after(other_0, w_pass))
+    w_take = after(w_take, done)
     w_chip = join(jnp.where(core == 0, w_hold, w_take), jnp.where(core == 0, w_take, w_hold))
     w_rows = lax.all_gather(w_chip, "seq", axis=0, tiled=True, axis_index_groups=same)
     pack_1 = after(pack(1), w_chip)
@@ -349,7 +350,8 @@
     mine[1] = after(mine[1], done)
     theirs.append(swap(mine[1]))
     done = attend_heads(1, 0, 4)
-    hidden = project_in(after(hid_1, done), own, others, 0, HALF, mod_scale, w_in, is_last=True)
+    earlier = project_in(after(hid_1, done), own, [], 0, HALF, mod_scale, w_in)
+    hidden = project_in(hid_1, [], others, 0, HALF, mod_scale, w_in, earlier, is_last=True)
     hidden_there = swap(hidden)
     core_1 = core.reshape(1)
     sent_here = project_out(core_1, hidden, w_rows, jnp.bfloat16)

time: 189 us -> 187 us (0.989)
  waiting for transfers between devices: 65.7 us -> 55.8 us
  Pallas kernels: 62.7 us -> 69.2 us
  local copies, waits for them, and re-layouts: 9.18 us -> 11.5 us
    ppermute x16, waiting for transfers between devices: 65.7 us -> 55.8 us  [moved(): return lax.ppermute(value, AXES, pairs)]
    pallas_call x1 -> x2, Pallas kernels: 14.7 us -> 21.1 us  [project_in(): pl.pallas_call(functools.partial(project_in_kernel, (len(own), len(other)...]
    unnamed x38 -> x40, local copies, waits for them, and re-layouts: 4.86 us -> 6.08 us
  transfers between devices with their start and end apart: 17 -> 17, of which waited for: 9 -> 7; matrix products, arithmetic and copies ran while one was open for 3% -> 4% of each run, Pallas kernels for 33% -> 36%
where the time goes in v4:
time: 187 us; the launch traced here: 186 us
  Pallas kernels  69.2 us (37%)
  waiting for transfers between devices  55.8 us (30%)
  starting transfers between devices  29.8 us (16%)
  between operations  15.4 us (8%)
  local copies, waits for them, and re-layouts  11.5 us (6%)
  other arithmetic  4 us (2%)
    ppermute x16, waiting for transfers between devices, moved(): return lax.ppermute(value, AXES, pairs)  55.8 us
    ppermute x16, starting transfers between devices, moved(): return lax.ppermute(value, AXES, pairs)  29.8 us
    pallas_call x4, Pallas kernels, project_out(): pl.pallas_call(project_out_kernel, out_shape=jax.ShapeDtypeStruct((TILE,...  24 us
    pallas_call x3, Pallas kernels, attend(): pl.pallas_call(attend_kernel, out_shape=jax.ShapeDtypeStruct((TILE, heads...  22.5 us
    pallas_call x2, Pallas kernels, project_in(): pl.pallas_call(functools.partial(project_in_kernel, (len(own), len(other)...  21.1 us
    unnamed x40, local copies, waits for them, and re-layouts  6.08 us
  transfers between devices with their start and end apart: 17, of which 7 were waited for; matrix products, arithmetic and copies ran while one was open for 4% of the time, Pallas kernels for 36%

profile of v4, /device:TPU:7, one launch (start us, length us, event | category | flops | bytes accessed | tf_op | source)
XLA Modules:
  0.0 185.8 jit_solution(16141625830356239438)
XLA Ops:
  9.6 8.0 %collective-permute-done.1 = bf16[48,3072]{1,0:T(8,128)(2,1)} collective-permute-done((bf16[48,3072]{1,0:T(8,128)(2,1)S(1)}, bf16[48,3072]{1,0:T(8,128)(2,1)}, u32[]{:S(2)}, u32[]{:S(2)}) %collective-permute-start.1) | collective-permute-done | bytes 294944 | tf_op jit(solution)/shard_map/ppermute | solution.py:43
  21.2 8.4 %collective-permute-start.2 = (bf16[1536,1024]{1,0:T(8,128)(2,1)S(1)}, bf16[1536,1024]{1,0:T(8,128)(2,1)}, u32[]{:S(2)}, u32[]{:S(2)}) collective-permute-start(bf16[1536,1024]{1,0:T(8,128)(2,1)S(1)} %pad_maximum_fusion.refs_0_), channel_id=1, source_target_pairs={{0,4},{1,5},{4,8},{5,9},{6,2},{7,3},{8,12},{9,13},{10,6},{11,7},{1... | collective-permute-start | bytes 9437192 | tf_op jit(solution)/shard_map/ppermute | solution.py:43
  30.9 2.2 %collective-permute-done.4 = bf16[768,512]{1,0:T(8,128)(2,1)S(1)} collective-permute-done((bf16[768,512]{1,0:T(8,128)(2,1)S(1)}, bf16[768,512]{1,0:T(8,128)(2,1)S(1)}, u32[]{:S(2)}, u32[]{:S(2)}) %collective-permute-start.4) | collective-permute-done | bytes 786464 | tf_op jit(solution)/shard_map/ppermute | solution.py:43
  33.1 1.3 pad_maximum_fusion.2.refs_0_
  34.3 32.4 %collective-permute-done.2.refs_1_ = bf16[1536,1024]{1,0:T(8,128)(2,1)} collective-permute-done((bf16[1536,1024]{1,0:T(8,128)(2,1)S(1)}, bf16[1536,1024]{1,0:T(8,128)(2,1)}, u32[]{:S(2)}, u32[]{:S(2)}) %collective-permute-start.2) | collective-permute-done | bytes 3145760 | tf_op jit(solution)/shard_map/ppermute | solution.py:43
  66.7 11.1 %collective-permute-start.6 = (bf16[1536,512]{1,0:T(8,128)(2,1)}, bf16[1536,512]{1,0:T(8,128)(2,1)}, u32[]{:S(2)}, u32[]{:S(2)}) collective-permute-start(bf16[1536,512]{1,0:T(8,128)(2,1)} %pad_maximum_fusion.2.refs_0_), channel_id=1, source_target_pairs={{0,4},{1,5},{4,8},{5,9},{6,2},{7,3},{8,12},{9,13},{10,6},{11,7},{1... | collective-permute-start | bytes 4718600 | tf_op jit(solution)/shard_map/ppermute | solution.py:43
  81.2 1.3 copy-done.2
  82.4 1.3 copy-done.3
  83.7 7.5 %attend.3.refs_0_ = bf16[384,512]{1,0:T(8,128)(2,1)S(1)} custom-call(f32[6]{0:T(128)S(1)} %and_select_fusion.bias_ref, bf16[384,1536]{1,0:T(8,128)(2,1)S(1)} %copy-done.2, bf16[384,1536]{1,0:T(8,128)(2,1)S(1)} %copy-done.3, bf16[1536,1024]{1,0:T(8,128)(2,1)S(1)} %pad_maximum_fusion.refs_0_, bf16[1536,1024]{1,0:T(8,128)(2,1)} %collective-permute-done.2.refs_1_, ...), custom_call_target="tpu_custom_call" | custom-call | flops 1 | bytes 1 | tf_op jit(solution)/shard_map/attend/pallas_call | solution.py:117
  91.2 7.6 %attend.4.refs_1_ = bf16[384,512]{1,0:T(8,128)(2,1)S(1)} custom-call(f32[6]{0:T(128)S(1)} %and_select_fusion.bias_ref, bf16[384,1536]{1,0:T(8,128)(2,1)S(1)} %copy-done.2, bf16[384,1536]{1,0:T(8,128)(2,1)S(1)} %copy-done.3, bf16[1536,1024]{1,0:T(8,128)(2,1)S(1)} %pad_maximum_fusion.refs_0_, bf16[1536,1024]{1,0:T(8,128)(2,1)} %collective-permute-done.2.refs_1_, ...), custom_call_target="tpu_custom_call" | custom-call | flops 1 | bytes 1 | tf_op jit(solution)/shard_map/attend/pallas_call | solution.py:117
  99.6 2.4 %collective-permute-start.8 = (bf16[384,512]{1,0:T(8,128)(2,1)S(1)}, bf16[384,512]{1,0:T(8,128)(2,1)S(1)}, u32[]{:S(2)}, u32[]{:S(2)}) collective-permute-start(bf16[384,512]{1,0:T(8,128)(2,1)S(1)} %attend.3.refs_0_), channel_id=1, source_target_pairs={{0,1},{1,0},{2,3},{3,2},{4,5},{5,4},{6,7},{7,6},{8,9},{9,8},{10,11... | collective-permute-start | bytes 1179656 | tf_op jit(solution)/shard_map/ppermute | solution.py:43
  102.5 7.4 %attend.5.refs_2_ = bf16[384,512]{1,0:T(8,128)(2,1)S(1)} custom-call(f32[6]{0:T(128)S(1)} %and_select_fusion.bias_ref, bf16[384,1536]{1,0:T(8,128)(2,1)S(1)} %copy-done.2, bf16[384,1536]{1,0:T(8,128)(2,1)S(1)} %copy-done.3, bf16[1536,512]{1,0:T(8,128)(2,1)} %pad_maximum_fusion.2.refs_0_, bf16[1536,512]{1,0:T(8,128)(2,1)} %collective-permute-done.6.refs_1_, ...), custom_call_target="tpu_custom_call" | custom-call | flops 1 | bytes 1 | tf_op jit(solution)/shard_map/attend/pallas_call | solution.py:117
  110.7 10.1 %project_in.2 = (f32[384,3072]{1,0:T(8,128)}, f32[384,1]{1,0:T(8,128)}) custom-call(s32[1]{0:T(128)} %bitcast.3.hid_ref, bf16[384,512]{1,0:T(8,128)(2,1)} %copy-done.5, bf16[384,512]{1,0:T(8,128)(2,1)} %copy-done.7, bf16[384,512]{1,0:T(8,128)(2,1)} %copy-done.9, f32[1,3072]{1,0:T(1,128)} %bitcast.9, bf16[3072,3072]{1,0:T(8,128)(2,1)} %refs_4_.3), custom_call_target="tpu_custom_call" | custom-call | flops 1 | bytes 1 | tf_op jit(solution)/shard_map/project_in/pallas_call | solution.py:202
  120.8 6.8 %collective-permute-done.10.refs_2_ = bf16[384,512]{1,0:T(8,128)(2,1)S(1)} collective-permute-done((bf16[384,512]{1,0:T(8,128)(2,1)S(1)}, bf16[384,512]{1,0:T(8,128)(2,1)S(1)}, u32[]{:S(2)}, u32[]{:S(2)}) %collective-permute-start.10) | collective-permute-done | bytes 393248 | tf_op jit(solution)/shard_map/ppermute | solution.py:43
  128.4 11.1 %project_in.3.hidden_ref = bf16[384,3072]{1,0:T(8,128)(2,1)} custom-call(s32[1]{0:T(128)} %bitcast.3.hid_ref, bf16[384,512]{1,0:T(8,128)(2,1)} %copy-done.16, bf16[384,512]{1,0:T(8,128)(2,1)} %copy-done.15, bf16[384,512]{1,0:T(8,128)(2,1)} %copy-done.17, f32[1,3072]{1,0:T(1,128)} %bitcast.10, bf16[3072,3072]{1,0:T(8,128)(2,1)} %refs_4_.3, ...), custom_call_target="tpu_custom_call" | custom-call | flops 1 | bytes 1 | tf_op jit(solution)/shard_map/project_in/pallas_call | solution.py:202
  140.7 6.0 %project_out.4 = bf16[384,768]{1,0:T(8,128)(2,1)} custom-call(s32[1]{0:T(128)} %bitcast.part_ref.core_ref, bf16[384,3072]{1,0:T(8,128)(2,1)} %project_in.3.hidden_ref, bf16[1536,3072]{1,0:T(8,128)(2,1)} %all-gather.2.cloned.1.call-done.w_ref), custom_call_target="tpu_custom_call" | custom-call | flops 1 | bytes 1 | tf_op jit(solution)/shard_map/project_out/pallas_call | solution.py:226
  147.4 1.4 copy-done.12
  148.7 6.0 %project_out.5 = bf16[384,768]{1,0:T(8,128)(2,1)} custom-call(s32[1]{0:T(128)} %bitcast.part_ref.core_ref, bf16[384,3072]{1,0:T(8,128)(2,1)} %copy-done.12, bf16[1536,3072]{1,0:T(8,128)(2,1)} %all-gather.2.cloned.1.call-done.w_ref), custom_call_target="tpu_custom_call" | custom-call | flops 1 | bytes 1 | tf_op jit(solution)/shard_map/project_out/pallas_call | solution.py:226
  154.7 2.5 %collective-permute-start.15 = (bf16[384,768]{1,0:T(8,128)(2,1)}, bf16[384,768]{1,0:T(8,128)(2,1)S(1)}, u32[]{:S(2)}, u32[]{:S(2)}) collective-permute-start(bf16[384,768]{1,0:T(8,128)(2,1)} %project_out.5), channel_id=1, source_target_pairs={{0,3},{1,2},{2,1},{3,0},{4,7},{5,6},{6,5},{7,4},{8,11},{9,10},{10,... | collective-permute-start | bytes 1769480 | tf_op jit(solution)/shard_map/ppermute | solution.py:43
  157.3 5.9 %project_out.6 = bf16[384,768]{1,0:T(8,128)(2,1)} custom-call(s32[1]{0:T(128)S(6)} %sub.21.part_ref, bf16[384,3072]{1,0:T(8,128)(2,1)} %copy-done.12, bf16[1536,3072]{1,0:T(8,128)(2,1)} %all-gather.2.cloned.1.call-done.w_ref), custom_call_target="tpu_custom_call" | custom-call | flops 1 | bytes 1 | tf_op jit(solution)/shard_map/project_out/pallas_call | solution.py:226
  165.0 6.2 %project_out.7.refs_4_ = f32[384,768]{1,0:T(8,128)} custom-call(s32[1]{0:T(128)S(6)} %sub.21.part_ref, bf16[384,3072]{1,0:T(8,128)(2,1)} %project_in.3.hidden_ref, bf16[1536,3072]{1,0:T(8,128)(2,1)} %all-gather.2.cloned.1.call-done.w_ref), custom_call_target="tpu_custom_call" | custom-call | flops 1 | bytes 1 | tf_op jit(solution)/shard_map/project_out/pallas_call | solution.py:226
  171.3 4.9 %collective-permute-done.15.refs_6_ = bf16[384,768]{1,0:T(8,128)(2,1)S(1)} collective-permute-done((bf16[384,768]{1,0:T(8,128)(2,1)}, bf16[384,768]{1,0:T(8,128)(2,1)S(1)}, u32[]{:S(2)}, u32[]{:S(2)}) %collective-permute-start.15) | collective-permute-done | bytes 589856 | tf_op jit(solution)/shard_map/ppermute | solution.py:43
  176.1 1.3 copy-done.4
  177.4 1.5 finish.1
  (90 shorter events, 16.1 us)
Async XLA Ops:
  6.5 74.2 %copy-start = (s32[64,27]{0,1:T(8,128)S(1)}, s32[64,27]{0,1:T(8,128)}, u32[]{:S(2)}) copy-start(s32[64,27]{0,1:T(8,128)} %param.20) | copy-start | bytes 20740
  6.5 134.2 %all-gather.2.cloned.1.call-start = ((), (), s32[]{:S(2)}) async-start(), calls=%async_computation | async-start | bytes 10027008 | tf_op jit(solution)/shard_map/all_gather | solution.py:342
  8.1 10.5 %collective-permute-start = (bf16[768,1024]{1,0:T(8,128)(2,1)S(1)}, bf16[768,1024]{1,0:T(8,128)(2,1)S(1)}, u32[]{:S(2)}, u32[]{:S(2)}) collective-permute-start(bf16[768,1024]{1,0:T(8,128)(2,1)S(1)} %pad_maximum_fusion.1), channel_id=1, source_target_pairs={{0,2},{1,3},{2,0},{3,1},{4,6},{5,7},{6,4},{7,5},{8,10},{9,11},{10,... | collective-permute-start | bytes 4718600 | tf_op jit(solution)/shard_map/ppermute | solution.py:43
  8.9 8.7 %collective-permute-start.1 = (bf16[48,3072]{1,0:T(8,128)(2,1)S(1)}, bf16[48,3072]{1,0:T(8,128)(2,1)}, u32[]{:S(2)}, u32[]{:S(2)}) collective-permute-start(bf16[48,3072]{1,0:T(8,128)(2,1)S(1)} %bitcast.8), channel_id=1, source_target_pairs={{0,64},{1,65},{2,66},{3,67},{4,68},{5,69},{6,70},{7,71},{8,72},{9,... | collective-permute-start | bytes 884744 | tf_op jit(solution)/shard_map/ppermute | solution.py:43
  18.6 1.7 collective-permute-start.3
  19.2 11.4 %slice-start.1 = ((bf16[384,1536]{1,0:T(8,128)(2,1)}), bf16[384,512]{1,0:T(8,128)(2,1)S(1)}, s32[]{:S(2)}) async-start(bf16[384,1536]{1,0:T(8,128)(2,1)} %param.12), calls=%async_computation.2 | async-start | bytes 786432 | tf_op jit(solution)/shard_map/slice | solution.py:305
  21.2 45.5 %collective-permute-start.2 = (bf16[1536,1024]{1,0:T(8,128)(2,1)S(1)}, bf16[1536,1024]{1,0:T(8,128)(2,1)}, u32[]{:S(2)}, u32[]{:S(2)}) collective-permute-start(bf16[1536,1024]{1,0:T(8,128)(2,1)S(1)} %pad_maximum_fusion.refs_0_), channel_id=1, source_target_pairs={{0,4},{1,5},{4,8},{5,9},{6,2},{7,3},{8,12},{9,13},{10,6},{11,7},{1... | collective-permute-start | bytes 9437192 | tf_op jit(solution)/shard_map/ppermute | solution.py:43
  30.7 2.4 %collective-permute-start.4 = (bf16[768,512]{1,0:T(8,128)(2,1)S(1)}, bf16[768,512]{1,0:T(8,128)(2,1)S(1)}, u32[]{:S(2)}, u32[]{:S(2)}) collective-permute-start(bf16[768,512]{1,0:T(8,128)(2,1)S(1)} %pad_maximum_fusion.3), channel_id=1, source_target_pairs={{0,2},{1,3},{2,0},{3,1},{4,6},{5,7},{6,4},{7,5},{8,10},{9,11},{10,... | collective-permute-start | bytes 2359304 | tf_op jit(solution)/shard_map/ppermute | solution.py:43
  30.8 47.0 %copy-start.11 = (s32[64]{0:T(128)S(1)}, s32[64]{0:T(128)}, u32[]{:S(2)}) copy-start(s32[64]{0:T(128)} %param.19) | copy-start | bytes 772
  30.8 48.7 %copy-start.19 = (s32[6]{0:T(128)S(1)}, s32[6]{0:T(128)}, u32[]{:S(2)}) copy-start(s32[6]{0:T(128)} %constant.77.clone) | copy-start | bytes 76
  66.7 14.4 %collective-permute-start.5 = (bf16[1536,1024]{1,0:T(8,128)(2,1)}, bf16[1536,1024]{1,0:T(8,128)(2,1)}, u32[]{:S(2)}, u32[]{:S(2)}) collective-permute-start(bf16[1536,1024]{1,0:T(8,128)(2,1)} %collective-permute-done.2.refs_1_), channel_id=1, source_target_pairs={{0,2},{1,3},{2,0},{3,1},{4,6},{5,7},{6,4},{7,5},{8,10},{9,11},{10,... | collective-permute-start | bytes 9437192 | tf_op jit(solution)/shard_map/ppermute | solution.py:43
  66.7 32.1 %collective-permute-start.6 = (bf16[1536,512]{1,0:T(8,128)(2,1)}, bf16[1536,512]{1,0:T(8,128)(2,1)}, u32[]{:S(2)}, u32[]{:S(2)}) collective-permute-start(bf16[1536,512]{1,0:T(8,128)(2,1)} %pad_maximum_fusion.2.refs_0_), channel_id=1, source_target_pairs={{0,4},{1,5},{4,8},{5,9},{6,2},{7,3},{8,12},{9,13},{10,6},{11,7},{1... | collective-permute-start | bytes 4718600 | tf_op jit(solution)/shard_map/ppermute | solution.py:43
  98.8 11.2 %copy-start.7 = (bf16[384,512]{1,0:T(8,128)(2,1)}, bf16[384,512]{1,0:T(8,128)(2,1)S(1)}, u32[]{:S(2)}) copy-start(bf16[384,512]{1,0:T(8,128)(2,1)S(1)} %attend.4.refs_1_) | copy-start | bytes 1179652
  98.8 3.7 %collective-permute-start.7 = (bf16[1536,512]{1,0:T(8,128)(2,1)}, bf16[1536,512]{1,0:T(8,128)(2,1)S(1)}, u32[]{:S(2)}, u32[]{:S(2)}) collective-permute-start(bf16[1536,512]{1,0:T(8,128)(2,1)} %collective-permute-done.6.refs_1_), channel_id=1, source_target_pairs={{0,2},{1,3},{2,0},{3,1},{4,6},{5,7},{6,4},{7,5},{8,10},{9,11},{10,... | collective-permute-start | bytes 4718600 | tf_op jit(solution)/shard_map/ppermute | solution.py:43
  98.9 21.9 %collective-permute-start.9 = (bf16[384,512]{1,0:T(8,128)(2,1)S(1)}, bf16[384,512]{1,0:T(8,128)(2,1)S(1)}, u32[]{:S(2)}, u32[]{:S(2)}) collective-permute-start(bf16[384,512]{1,0:T(8,128)(2,1)S(1)} %attend.4.refs_1_), channel_id=1, source_target_pairs={{0,1},{1,0},{2,3},{3,2},{4,5},{5,4},{6,7},{7,6},{8,9},{9,8},{10,11... | collective-permute-start | bytes 1179656 | tf_op jit(solution)/shard_map/ppermute | solution.py:43
  99.6 21.2 %collective-permute-start.8 = (bf16[384,512]{1,0:T(8,128)(2,1)S(1)}, bf16[384,512]{1,0:T(8,128)(2,1)S(1)}, u32[]{:S(2)}, u32[]{:S(2)}) collective-permute-start(bf16[384,512]{1,0:T(8,128)(2,1)S(1)} %attend.3.refs_0_), channel_id=1, source_target_pairs={{0,1},{1,0},{2,3},{3,2},{4,5},{5,4},{6,7},{7,6},{8,9},{9,8},{10,11... | collective-permute-start | bytes 1179656 | tf_op jit(solution)/shard_map/ppermute | solution.py:43
  110.0 17.7 %collective-permute-start.10 = (bf16[384,512]{1,0:T(8,128)(2,1)S(1)}, bf16[384,512]{1,0:T(8,128)(2,1)S(1)}, u32[]{:S(2)}, u32[]{:S(2)}) collective-permute-start(bf16[384,512]{1,0:T(8,128)(2,1)S(1)} %attend.5.refs_2_), channel_id=1, source_target_pairs={{0,1},{1,0},{2,3},{3,2},{4,5},{5,4},{6,7},{7,6},{8,9},{9,8},{10,11... | collective-permute-start | bytes 1179656 | tf_op jit(solution)/shard_map/ppermute | solution.py:43
  139.5 7.9 %collective-permute-start.11 = (bf16[384,3072]{1,0:T(8,128)(2,1)}, bf16[384,3072]{1,0:T(8,128)(2,1)S(1)}, u32[]{:S(2)}, u32[]{:S(2)}) collective-permute-start(bf16[384,3072]{1,0:T(8,128)(2,1)} %project_in.3.hidden_ref), channel_id=1, source_target_pairs={{0,2},{1,3},{2,0},{3,1},{4,6},{5,7},{6,4},{7,5},{8,10},{9,11},{10,... | collective-permute-start | bytes 7077896 | tf_op jit(solution)/shard_map/ppermute | solution.py:43
  146.7 29.4 %collective-permute-start.14 = (bf16[384,768]{1,0:T(8,128)(2,1)}, bf16[384,768]{1,0:T(8,128)(2,1)S(1)}, u32[]{:S(2)}, u32[]{:S(2)}) collective-permute-start(bf16[384,768]{1,0:T(8,128)(2,1)} %project_out.4), channel_id=1, source_target_pairs={{0,1},{1,0},{2,3},{3,2},{4,5},{5,4},{6,7},{7,6},{8,9},{9,8},{10,11... | collective-permute-start | bytes 1769480 | tf_op jit(solution)/shard_map/ppermute | solution.py:43
  154.7 21.4 %collective-permute-start.15 = (bf16[384,768]{1,0:T(8,128)(2,1)}, bf16[384,768]{1,0:T(8,128)(2,1)S(1)}, u32[]{:S(2)}, u32[]{:S(2)}) collective-permute-start(bf16[384,768]{1,0:T(8,128)(2,1)} %project_out.5), channel_id=1, source_target_pairs={{0,3},{1,2},{2,1},{3,0},{4,7},{5,6},{6,5},{7,4},{8,11},{9,10},{10,... | collective-permute-start | bytes 1769480 | tf_op jit(solution)/shard_map/ppermute | solution.py:43
  164.3 6.9 %collective-permute-start.12 = (bf16[384,384]{1,0:T(8,128)(2,1)S(1)}, bf16[384,384]{1,0:T(8,128)(2,1)S(1)}, u32[]{:S(2)}, u32[]{:S(2)}) collective-permute-start(bf16[384,384]{1,0:T(8,128)(2,1)S(1)} %get-tuple-element.43), channel_id=1, source_target_pairs={{0,2},{1,3},{2,0},{3,1},{4,6},{5,7},{6,4},{7,5},{8,10},{9,11},{10,... | collective-permute-start | bytes 884744 | tf_op jit(solution)/shard_map/ppermute | solution.py:43
  164.5 6.6 %collective-permute-start.13 = (bf16[384,384]{1,0:T(8,128)(2,1)S(1)}, bf16[384,384]{1,0:T(8,128)(2,1)S(1)}, u32[]{:S(2)}, u32[]{:S(2)}) collective-permute-start(bf16[384,384]{1,0:T(8,128)(2,1)S(1)} %get-tuple-element.44), channel_id=1, source_target_pairs={{0,2},{1,3},{2,0},{3,1},{4,6},{5,7},{6,4},{7,5},{8,10},{9,11},{10,... | collective-permute-start | bytes 884744 | tf_op jit(solution)/shard_map/ppermute | solution.py:43
  165.0 11.1 %copy-start.6 = (bf16[384,512]{1,0:T(8,128)(2,1)S(1)}, bf16[384,512]{1,0:T(8,128)(2,1)}, u32[]{:S(2)}) copy-start(bf16[384,512]{1,0:T(8,128)(2,1)} %copy-done.5) | copy-start | bytes 1179652
  165.0 11.1 %copy-start.8 = (bf16[384,512]{1,0:T(8,128)(2,1)S(1)}, bf16[384,512]{1,0:T(8,128)(2,1)}, u32[]{:S(2)}) copy-start(bf16[384,512]{1,0:T(8,128)(2,1)} %copy-done.7) | copy-start | bytes 1179652
  (16 other events, 64.3 us)
Sparse Core Ops, SparseCore 0:
  21.3 118.2 all-gather.1

commit v5 on v4

--- a/solution.py
+++ b/solution.py
@@ -215,26 +215,29 @@
     )(hid, *operands)
 
 
-def project_out_kernel(part_ref, hidden_ref, w_ref, out_ref):
-    out_ref[...] = lax.dot_general(
-        hidden_ref[...], w_ref[...], (((1,), (1,)), ((), ())), preferred_element_type=jnp.float32
-    ).astype(out_ref.dtype)
+def project_out_kernel(part_ref, hidden_ref, w_ref, out_ref, w_buf, sems):
+    cols = 256
+    copies = []
+    for i in range(QUARTER // cols):
+        row = pl.multiple_of(part_ref[0] * QUARTER + i * cols, cols)
+        copies.append(pltpu.make_async_copy(w_ref.at[pl.ds(row, cols)], w_buf.at[i], sems.at[i]))
+    for copy in copies:
+        copy.start()
+    for i, copy in enumerate(copies):
+        copy.wait()
+        out_ref[:, i * cols : (i + 1) * cols] = lax.dot_general(
+            hidden_ref[...], w_buf[i], (((1,), (1,)), ((), ())), preferred_element_type=jnp.float32
+        ).astype(out_ref.dtype)
 
 
 def project_out(part, hidden, w_rows, dtype):
-    cols = 256
+    vmem = pl.BlockSpec(memory_space=pltpu.VMEM)
     return pl.pallas_call(
         project_out_kernel,
         out_shape=jax.ShapeDtypeStruct((TILE, QUARTER), dtype),
-        grid_spec=pltpu.PrefetchScalarGridSpec(
-            num_scalar_prefetch=1,
-            grid=(QUARTER // cols,),
-            in_specs=[
-                pl.BlockSpec((TILE, UNITS), lambda i, p: (0, 0)),
-                pl.BlockSpec((cols, UNITS), lambda i, p: (p[0] * (QUARTER // cols) + i, 0)),
-            ],
-            out_specs=pl.BlockSpec((TILE, cols), lambda i, p: (0, i)),
-        ),
+        in_specs=[pl.BlockSpec(memory_space=pltpu.SMEM), vmem, pl.BlockSpec(memory_space=pl.ANY)],
+        out_specs=vmem,
+        scratch_shapes=[pltpu.VMEM((3, 256, UNITS), jnp.bfloat16), pltpu.SemaphoreType.DMA((3,))],
         compiler_params=pltpu.CompilerParams(vmem_limit_bytes=VMEM_BYTES),
         cost_estimate=LIGHT,
         name="project_out",

time: 187 us -> 189 us (1.011)
  Pallas kernels: 69.2 us -> 75.6 us
  waiting for transfers between devices: 55.8 us -> 50.9 us
    pallas_call x4, Pallas kernels: 24 us -> 30.4 us  [project_out(): pl.pallas_call(project_out_kernel, out_shape=jax.ShapeDtypeStruct((TILE,...]
    ppermute x16, waiting for transfers between devices: 55.8 us -> 50.9 us  [moved(): return lax.ppermute(value, AXES, pairs)]
  transfers between devices with their start and end apart: 17 -> 17, of which waited for: 7 -> 6; matrix products, arithmetic and copies ran while one was open for 4% -> 4% of each run, Pallas kernels for 36% -> 40%
where the time goes in v5:
time: 189 us; the launch traced here: 188 us
  Pallas kernels  75.6 us (40%)
  waiting for transfers between devices  50.9 us (27%)
  starting transfers between devices  30 us (16%)
  between operations  15.5 us (8%)
  local copies, waits for them, and re-layouts  11.5 us (6%)
  other arithmetic  4 us (2%)
    ppermute x16, waiting for transfers between devices, moved(): return lax.ppermute(value, AXES, pairs)  50.9 us
    pallas_call x4, Pallas kernels, project_out(): pl.pallas_call(project_out_kernel, out_shape=jax.ShapeDtypeStruct((TILE,...  30.4 us
    ppermute x16, starting transfers between devices, moved(): return lax.ppermute(value, AXES, pairs)  30 us
    pallas_call x3, Pallas kernels, attend(): pl.pallas_call(attend_kernel, out_shape=jax.ShapeDtypeStruct((TILE, heads...  22.5 us
    pallas_call x2, Pallas kernels, project_in(): pl.pallas_call(functools.partial(project_in_kernel, (len(own), len(other)...  21.1 us
    unnamed x40, local copies, waits for them, and re-layouts  6.09 us
  transfers between devices with their start and end apart: 17, of which 6 were waited for; matrix products, arithmetic and copies ran while one was open for 4% of the time, Pallas kernels for 40%

profile of v5, /device:TPU:7, one launch (start us, length us, event | category | flops | bytes accessed | tf_op | source)
XLA Modules:
  0.0 187.5 jit_solution(8390362199827241644)
XLA Ops:
  9.6 8.0 %collective-permute-done.1 = bf16[48,3072]{1,0:T(8,128)(2,1)} collective-permute-done((bf16[48,3072]{1,0:T(8,128)(2,1)S(1)}, bf16[48,3072]{1,0:T(8,128)(2,1)}, u32[]{:S(2)}, u32[]{:S(2)}) %collective-permute-start.1) | collective-permute-done | bytes 294944 | tf_op jit(solution)/shard_map/ppermute | solution.py:43
  21.2 8.4 %collective-permute-start.2 = (bf16[1536,1024]{1,0:T(8,128)(2,1)S(1)}, bf16[1536,1024]{1,0:T(8,128)(2,1)}, u32[]{:S(2)}, u32[]{:S(2)}) collective-permute-start(bf16[1536,1024]{1,0:T(8,128)(2,1)S(1)} %pad_maximum_fusion.refs_0_), channel_id=1, source_target_pairs={{0,4},{1,5},{4,8},{5,9},{6,2},{7,3},{8,12},{9,13},{10,6},{11,7},{1... | collective-permute-start | bytes 9437192 | tf_op jit(solution)/shard_map/ppermute | solution.py:43
  30.9 2.2 %collective-permute-done.4 = bf16[768,512]{1,0:T(8,128)(2,1)S(1)} collective-permute-done((bf16[768,512]{1,0:T(8,128)(2,1)S(1)}, bf16[768,512]{1,0:T(8,128)(2,1)S(1)}, u32[]{:S(2)}, u32[]{:S(2)}) %collective-permute-start.4) | collective-permute-done | bytes 786464 | tf_op jit(solution)/shard_map/ppermute | solution.py:43
  33.1 1.3 pad_maximum_fusion.2.refs_0_
  34.3 32.4 %collective-permute-done.2.refs_1_ = bf16[1536,1024]{1,0:T(8,128)(2,1)} collective-permute-done((bf16[1536,1024]{1,0:T(8,128)(2,1)S(1)}, bf16[1536,1024]{1,0:T(8,128)(2,1)}, u32[]{:S(2)}, u32[]{:S(2)}) %collective-permute-start.2) | collective-permute-done | bytes 3145760 | tf_op jit(solution)/shard_map/ppermute | solution.py:43
  66.7 11.1 %collective-permute-start.6 = (bf16[1536,512]{1,0:T(8,128)(2,1)}, bf16[1536,512]{1,0:T(8,128)(2,1)}, u32[]{:S(2)}, u32[]{:S(2)}) collective-permute-start(bf16[1536,512]{1,0:T(8,128)(2,1)} %pad_maximum_fusion.2.refs_0_), channel_id=1, source_target_pairs={{0,4},{1,5},{4,8},{5,9},{6,2},{7,3},{8,12},{9,13},{10,6},{11,7},{1... | collective-permute-start | bytes 4718600 | tf_op jit(solution)/shard_map/ppermute | solution.py:43
  81.2 1.3 copy-done.2
  82.4 1.3 copy-done.3
  83.7 7.5 %attend.3.refs_0_ = bf16[384,512]{1,0:T(8,128)(2,1)S(1)} custom-call(f32[6]{0:T(128)S(1)} %and_select_fusion.bias_ref, bf16[384,1536]{1,0:T(8,128)(2,1)S(1)} %copy-done.2, bf16[384,1536]{1,0:T(8,128)(2,1)S(1)} %copy-done.3, bf16[1536,1024]{1,0:T(8,128)(2,1)S(1)} %pad_maximum_fusion.refs_0_, bf16[1536,1024]{1,0:T(8,128)(2,1)} %collective-permute-done.2.refs_1_, ...), custom_call_target="tpu_custom_call" | custom-call | flops 1 | bytes 1 | tf_op jit(solution)/shard_map/attend/pallas_call | solution.py:117
  91.2 7.6 %attend.4.refs_1_ = bf16[384,512]{1,0:T(8,128)(2,1)S(1)} custom-call(f32[6]{0:T(128)S(1)} %and_select_fusion.bias_ref, bf16[384,1536]{1,0:T(8,128)(2,1)S(1)} %copy-done.2, bf16[384,1536]{1,0:T(8,128)(2,1)S(1)} %copy-done.3, bf16[1536,1024]{1,0:T(8,128)(2,1)S(1)} %pad_maximum_fusion.refs_0_, bf16[1536,1024]{1,0:T(8,128)(2,1)} %collective-permute-done.2.refs_1_, ...), custom_call_target="tpu_custom_call" | custom-call | flops 1 | bytes 1 | tf_op jit(solution)/shard_map/attend/pallas_call | solution.py:117
  99.6 2.4 %collective-permute-start.8 = (bf16[384,512]{1,0:T(8,128)(2,1)S(1)}, bf16[384,512]{1,0:T(8,128)(2,1)S(1)}, u32[]{:S(2)}, u32[]{:S(2)}) collective-permute-start(bf16[384,512]{1,0:T(8,128)(2,1)S(1)} %attend.3.refs_0_), channel_id=1, source_target_pairs={{0,1},{1,0},{2,3},{3,2},{4,5},{5,4},{6,7},{7,6},{8,9},{9,8},{10,11... | collective-permute-start | bytes 1179656 | tf_op jit(solution)/shard_map/ppermute | solution.py:43
  102.5 7.4 %attend.5.refs_2_ = bf16[384,512]{1,0:T(8,128)(2,1)S(1)} custom-call(f32[6]{0:T(128)S(1)} %and_select_fusion.bias_ref, bf16[384,1536]{1,0:T(8,128)(2,1)S(1)} %copy-done.2, bf16[384,1536]{1,0:T(8,128)(2,1)S(1)} %copy-done.3, bf16[1536,512]{1,0:T(8,128)(2,1)} %pad_maximum_fusion.2.refs_0_, bf16[1536,512]{1,0:T(8,128)(2,1)} %collective-permute-done.6.refs_1_, ...), custom_call_target="tpu_custom_call" | custom-call | flops 1 | bytes 1 | tf_op jit(solution)/shard_map/attend/pallas_call | solution.py:117
  110.7 10.1 %project_in.2 = (f32[384,3072]{1,0:T(8,128)}, f32[384,1]{1,0:T(8,128)}) custom-call(s32[1]{0:T(128)} %bitcast.3.hid_ref, bf16[384,512]{1,0:T(8,128)(2,1)} %copy-done.5, bf16[384,512]{1,0:T(8,128)(2,1)} %copy-done.7, bf16[384,512]{1,0:T(8,128)(2,1)} %copy-done.9, f32[1,3072]{1,0:T(1,128)} %bitcast.9, bf16[3072,3072]{1,0:T(8,128)(2,1)} %refs_4_.3), custom_call_target="tpu_custom_call" | custom-call | flops 1 | bytes 1 | tf_op jit(solution)/shard_map/project_in/pallas_call | solution.py:202
  120.8 6.8 %collective-permute-done.10.refs_2_ = bf16[384,512]{1,0:T(8,128)(2,1)S(1)} collective-permute-done((bf16[384,512]{1,0:T(8,128)(2,1)S(1)}, bf16[384,512]{1,0:T(8,128)(2,1)S(1)}, u32[]{:S(2)}, u32[]{:S(2)}) %collective-permute-start.10) | collective-permute-done | bytes 393248 | tf_op jit(solution)/shard_map/ppermute | solution.py:43
  128.4 11.1 %project_in.3.hidden_ref = bf16[384,3072]{1,0:T(8,128)(2,1)} custom-call(s32[1]{0:T(128)} %bitcast.3.hid_ref, bf16[384,512]{1,0:T(8,128)(2,1)} %copy-done.16, bf16[384,512]{1,0:T(8,128)(2,1)} %copy-done.15, bf16[384,512]{1,0:T(8,128)(2,1)} %copy-done.17, f32[1,3072]{1,0:T(1,128)} %bitcast.10, bf16[3072,3072]{1,0:T(8,128)(2,1)} %refs_4_.3, ...), custom_call_target="tpu_custom_call" | custom-call | flops 1 | bytes 1 | tf_op jit(solution)/shard_map/project_in/pallas_call | solution.py:202
  139.5 1.2 collective-permute-start.11
  140.7 7.5 %project_out.4 = bf16[384,768]{1,0:T(8,128)(2,1)} custom-call(s32[1]{0:T(128)} %bitcast.part_ref.core_ref, bf16[384,3072]{1,0:T(8,128)(2,1)} %project_in.3.hidden_ref, bf16[1536,3072]{1,0:T(8,128)(2,1)} %all-gather.2.cloned.1.call-done.w_ref), custom_call_target="tpu_custom_call" | custom-call | flops 1 | bytes 1 | tf_op jit(solution)/shard_map/project_out/pallas_call | solution.py:235
  149.0 1.4 copy-done.12
  150.4 7.6 %project_out.5 = bf16[384,768]{1,0:T(8,128)(2,1)} custom-call(s32[1]{0:T(128)} %bitcast.part_ref.core_ref, bf16[384,3072]{1,0:T(8,128)(2,1)} %copy-done.12, bf16[1536,3072]{1,0:T(8,128)(2,1)} %all-gather.2.cloned.1.call-done.w_ref), custom_call_target="tpu_custom_call" | custom-call | flops 1 | bytes 1 | tf_op jit(solution)/shard_map/project_out/pallas_call | solution.py:235
  158.0 2.6 %collective-permute-start.15 = (bf16[384,768]{1,0:T(8,128)(2,1)}, bf16[384,768]{1,0:T(8,128)(2,1)S(1)}, u32[]{:S(2)}, u32[]{:S(2)}) collective-permute-start(bf16[384,768]{1,0:T(8,128)(2,1)} %project_out.5), channel_id=1, source_target_pairs={{0,3},{1,2},{2,1},{3,0},{4,7},{5,6},{6,5},{7,4},{8,11},{9,10},{10,... | collective-permute-start | bytes 1769480 | tf_op jit(solution)/shard_map/ppermute | solution.py:43
  160.6 7.5 %project_out.6 = bf16[384,768]{1,0:T(8,128)(2,1)} custom-call(s32[1]{0:T(128)S(6)} %sub.21.part_ref, bf16[384,3072]{1,0:T(8,128)(2,1)} %copy-done.12, bf16[1536,3072]{1,0:T(8,128)(2,1)} %all-gather.2.cloned.1.call-done.w_ref), custom_call_target="tpu_custom_call" | custom-call | flops 1 | bytes 1 | tf_op jit(solution)/shard_map/project_out/pallas_call | solution.py:235
  169.9 7.8 %project_out.7.refs_4_ = f32[384,768]{1,0:T(8,128)} custom-call(s32[1]{0:T(128)S(6)} %sub.21.part_ref, bf16[384,3072]{1,0:T(8,128)(2,1)} %project_in.3.hidden_ref, bf16[1536,3072]{1,0:T(8,128)(2,1)} %all-gather.2.cloned.1.call-done.w_ref), custom_call_target="tpu_custom_call" | custom-call | flops 1 | bytes 1 | tf_op jit(solution)/shard_map/project_out/pallas_call | solution.py:235
  177.9 1.3 copy-done.4
  179.2 1.5 finish.1
  (90 shorter events, 15.0 us)
Async XLA Ops:
  6.5 74.2 %copy-start = (s32[64,27]{0,1:T(8,128)S(1)}, s32[64,27]{0,1:T(8,128)}, u32[]{:S(2)}) copy-start(s32[64,27]{0,1:T(8,128)} %param.20) | copy-start | bytes 20740
  6.5 134.2 %all-gather.2.cloned.1.call-start = ((), (), s32[]{:S(2)}) async-start(), calls=%async_computation | async-start | bytes 10027008 | tf_op jit(solution)/shard_map/all_gather | solution.py:345
  8.1 10.5 %collective-permute-start = (bf16[768,1024]{1,0:T(8,128)(2,1)S(1)}, bf16[768,1024]{1,0:T(8,128)(2,1)S(1)}, u32[]{:S(2)}, u32[]{:S(2)}) collective-permute-start(bf16[768,1024]{1,0:T(8,128)(2,1)S(1)} %pad_maximum_fusion.1), channel_id=1, source_target_pairs={{0,2},{1,3},{2,0},{3,1},{4,6},{5,7},{6,4},{7,5},{8,10},{9,11},{10,... | collective-permute-start | bytes 4718600 | tf_op jit(solution)/shard_map/ppermute | solution.py:43
  8.9 8.7 %collective-permute-start.1 = (bf16[48,3072]{1,0:T(8,128)(2,1)S(1)}, bf16[48,3072]{1,0:T(8,128)(2,1)}, u32[]{:S(2)}, u32[]{:S(2)}) collective-permute-start(bf16[48,3072]{1,0:T(8,128)(2,1)S(1)} %bitcast.8), channel_id=1, source_target_pairs={{0,64},{1,65},{2,66},{3,67},{4,68},{5,69},{6,70},{7,71},{8,72},{9,... | collective-permute-start | bytes 884744 | tf_op jit(solution)/shard_map/ppermute | solution.py:43
  18.6 1.7 collective-permute-start.3
  19.2 11.4 %slice-start.1 = ((bf16[384,1536]{1,0:T(8,128)(2,1)}), bf16[384,512]{1,0:T(8,128)(2,1)S(1)}, s32[]{:S(2)}) async-start(bf16[384,1536]{1,0:T(8,128)(2,1)} %param.12), calls=%async_computation.2 | async-start | bytes 786432 | tf_op jit(solution)/shard_map/slice | solution.py:308
  21.2 45.5 %collective-permute-start.2 = (bf16[1536,1024]{1,0:T(8,128)(2,1)S(1)}, bf16[1536,1024]{1,0:T(8,128)(2,1)}, u32[]{:S(2)}, u32[]{:S(2)}) collective-permute-start(bf16[1536,1024]{1,0:T(8,128)(2,1)S(1)} %pad_maximum_fusion.refs_0_), channel_id=1, source_target_pairs={{0,4},{1,5},{4,8},{5,9},{6,2},{7,3},{8,12},{9,13},{10,6},{11,7},{1... | collective-permute-start | bytes 9437192 | tf_op jit(solution)/shard_map/ppermute | solution.py:43
  30.7 2.4 %collective-permute-start.4 = (bf16[768,512]{1,0:T(8,128)(2,1)S(1)}, bf16[768,512]{1,0:T(8,128)(2,1)S(1)}, u32[]{:S(2)}, u32[]{:S(2)}) collective-permute-start(bf16[768,512]{1,0:T(8,128)(2,1)S(1)} %pad_maximum_fusion.3), channel_id=1, source_target_pairs={{0,2},{1,3},{2,0},{3,1},{4,6},{5,7},{6,4},{7,5},{8,10},{9,11},{10,... | collective-permute-start | bytes 2359304 | tf_op jit(solution)/shard_map/ppermute | solution.py:43
  30.8 47.0 %copy-start.11 = (s32[64]{0:T(128)S(1)}, s32[64]{0:T(128)}, u32[]{:S(2)}) copy-start(s32[64]{0:T(128)} %param.19) | copy-start | bytes 772
  30.8 48.7 %copy-start.19 = (s32[6]{0:T(128)S(1)}, s32[6]{0:T(128)}, u32[]{:S(2)}) copy-start(s32[6]{0:T(128)} %constant.77.clone) | copy-start | bytes 76
  66.7 14.4 %collective-permute-start.5 = (bf16[1536,1024]{1,0:T(8,128)(2,1)}, bf16[1536,1024]{1,0:T(8,128)(2,1)}, u32[]{:S(2)}, u32[]{:S(2)}) collective-permute-start(bf16[1536,1024]{1,0:T(8,128)(2,1)} %collective-permute-done.2.refs_1_), channel_id=1, source_target_pairs={{0,2},{1,3},{2,0},{3,1},{4,6},{5,7},{6,4},{7,5},{8,10},{9,11},{10,... | collective-permute-start | bytes 9437192 | tf_op jit(solution)/shard_map/ppermute | solution.py:43
  66.7 32.1 %collective-permute-start.6 = (bf16[1536,512]{1,0:T(8,128)(2,1)}, bf16[1536,512]{1,0:T(8,128)(2,1)}, u32[]{:S(2)}, u32[]{:S(2)}) collective-permute-start(bf16[1536,512]{1,0:T(8,128)(2,1)} %pad_maximum_fusion.2.refs_0_), channel_id=1, source_target_pairs={{0,4},{1,5},{4,8},{5,9},{6,2},{7,3},{8,12},{9,13},{10,6},{11,7},{1... | collective-permute-start | bytes 4718600 | tf_op jit(solution)/shard_map/ppermute | solution.py:43
  91.2 8.4 %copy-start.5 = (bf16[384,512]{1,0:T(8,128)(2,1)}, bf16[384,512]{1,0:T(8,128)(2,1)S(1)}, u32[]{:S(2)}) copy-start(bf16[384,512]{1,0:T(8,128)(2,1)S(1)} %attend.3.refs_0_) | copy-start | bytes 1179652
  98.8 11.2 %copy-start.7 = (bf16[384,512]{1,0:T(8,128)(2,1)}, bf16[384,512]{1,0:T(8,128)(2,1)S(1)}, u32[]{:S(2)}) copy-start(bf16[384,512]{1,0:T(8,128)(2,1)S(1)} %attend.4.refs_1_) | copy-start | bytes 1179652
  98.8 3.7 %collective-permute-start.7 = (bf16[1536,512]{1,0:T(8,128)(2,1)}, bf16[1536,512]{1,0:T(8,128)(2,1)S(1)}, u32[]{:S(2)}, u32[]{:S(2)}) collective-permute-start(bf16[1536,512]{1,0:T(8,128)(2,1)} %collective-permute-done.6.refs_1_), channel_id=1, source_target_pairs={{0,2},{1,3},{2,0},{3,1},{4,6},{5,7},{6,4},{7,5},{8,10},{9,11},{10,... | collective-permute-start | bytes 4718600 | tf_op jit(solution)/shard_map/ppermute | solution.py:43
  98.9 21.9 %collective-permute-start.9 = (bf16[384,512]{1,0:T(8,128)(2,1)S(1)}, bf16[384,512]{1,0:T(8,128)(2,1)S(1)}, u32[]{:S(2)}, u32[]{:S(2)}) collective-permute-start(bf16[384,512]{1,0:T(8,128)(2,1)S(1)} %attend.4.refs_1_), channel_id=1, source_target_pairs={{0,1},{1,0},{2,3},{3,2},{4,5},{5,4},{6,7},{7,6},{8,9},{9,8},{10,11... | collective-permute-start | bytes 1179656 | tf_op jit(solution)/shard_map/ppermute | solution.py:43
  99.6 21.2 %collective-permute-start.8 = (bf16[384,512]{1,0:T(8,128)(2,1)S(1)}, bf16[384,512]{1,0:T(8,128)(2,1)S(1)}, u32[]{:S(2)}, u32[]{:S(2)}) collective-permute-start(bf16[384,512]{1,0:T(8,128)(2,1)S(1)} %attend.3.refs_0_), channel_id=1, source_target_pairs={{0,1},{1,0},{2,3},{3,2},{4,5},{5,4},{6,7},{7,6},{8,9},{9,8},{10,11... | collective-permute-start | bytes 1179656 | tf_op jit(solution)/shard_map/ppermute | solution.py:43
  110.0 17.7 %collective-permute-start.10 = (bf16[384,512]{1,0:T(8,128)(2,1)S(1)}, bf16[384,512]{1,0:T(8,128)(2,1)S(1)}, u32[]{:S(2)}, u32[]{:S(2)}) collective-permute-start(bf16[384,512]{1,0:T(8,128)(2,1)S(1)} %attend.5.refs_2_), channel_id=1, source_target_pairs={{0,1},{1,0},{2,3},{3,2},{4,5},{5,4},{6,7},{7,6},{8,9},{9,8},{10,11... | collective-permute-start | bytes 1179656 | tf_op jit(solution)/shard_map/ppermute | solution.py:43
  139.5 9.5 %collective-permute-start.11 = (bf16[384,3072]{1,0:T(8,128)(2,1)}, bf16[384,3072]{1,0:T(8,128)(2,1)S(1)}, u32[]{:S(2)}, u32[]{:S(2)}) collective-permute-start(bf16[384,3072]{1,0:T(8,128)(2,1)} %project_in.3.hidden_ref), channel_id=1, source_target_pairs={{0,2},{1,3},{2,0},{3,1},{4,6},{5,7},{6,4},{7,5},{8,10},{9,11},{10,... | collective-permute-start | bytes 7077896 | tf_op jit(solution)/shard_map/ppermute | solution.py:43
  148.3 29.6 %collective-permute-start.14 = (bf16[384,768]{1,0:T(8,128)(2,1)}, bf16[384,768]{1,0:T(8,128)(2,1)S(1)}, u32[]{:S(2)}, u32[]{:S(2)}) collective-permute-start(bf16[384,768]{1,0:T(8,128)(2,1)} %project_out.4), channel_id=1, source_target_pairs={{0,1},{1,0},{2,3},{3,2},{4,5},{5,4},{6,7},{7,6},{8,9},{9,8},{10,11... | collective-permute-start | bytes 1769480 | tf_op jit(solution)/shard_map/ppermute | solution.py:43
  158.0 11.8 %copy-start.18 = (f32[3072]{0:T(1024)S(1)}, f32[3072]{0:T(1024)}, u32[]{:S(2)}) copy-start(f32[3072]{0:T(1024)} %param.18) | copy-start | bytes 36868
  158.0 19.8 %collective-permute-start.15 = (bf16[384,768]{1,0:T(8,128)(2,1)}, bf16[384,768]{1,0:T(8,128)(2,1)S(1)}, u32[]{:S(2)}, u32[]{:S(2)}) collective-permute-start(bf16[384,768]{1,0:T(8,128)(2,1)} %project_out.5), channel_id=1, source_target_pairs={{0,3},{1,2},{2,1},{3,0},{4,7},{5,6},{6,5},{7,4},{8,11},{9,10},{10,... | collective-permute-start | bytes 1769480 | tf_op jit(solution)/shard_map/ppermute | solution.py:43
  169.2 8.5 %collective-permute-start.12 = (bf16[384,384]{1,0:T(8,128)(2,1)S(1)}, bf16[384,384]{1,0:T(8,128)(2,1)S(1)}, u32[]{:S(2)}, u32[]{:S(2)}) collective-permute-start(bf16[384,384]{1,0:T(8,128)(2,1)S(1)} %get-tuple-element.43), channel_id=1, source_target_pairs={{0,2},{1,3},{2,0},{3,1},{4,6},{5,7},{6,4},{7,5},{8,10},{9,11},{10,... | collective-permute-start | bytes 884744 | tf_op jit(solution)/shard_map/ppermute | solution.py:43
  169.5 8.3 %collective-permute-start.13 = (bf16[384,384]{1,0:T(8,128)(2,1)S(1)}, bf16[384,384]{1,0:T(8,128)(2,1)S(1)}, u32[]{:S(2)}, u32[]{:S(2)}) collective-permute-start(bf16[384,384]{1,0:T(8,128)(2,1)S(1)} %get-tuple-element.44), channel_id=1, source_target_pairs={{0,2},{1,3},{2,0},{3,1},{4,6},{5,7},{6,4},{7,5},{8,10},{9,11},{10,... | collective-permute-start | bytes 884744 | tf_op jit(solution)/shard_map/ppermute | solution.py:43
  (16 other events, 53.7 us)
Sparse Core Ops, SparseCore 0:
  21.3 118.2 all-gather.1

commit v6 on v4

--- a/solution.py
+++ b/solution.py
@@ -345,8 +345,7 @@
     done = send_frame(pack_1, other_1)
     mine[0] = after(mine[0], done)
     theirs.append(swap(mine[0]))
-    done = attend_heads(0, 0, 4)
-    done = attend_heads(0, 4, 4, done)
+    done = attend_heads(0, 0, 8)
     mine[1] = after(mine[1], done)
     theirs.append(swap(mine[1]))
     done = attend_heads(1, 0, 4)

time: 187 us -> 186 us (level)
  waiting for transfers between devices: 55.8 us -> 57.8 us
    ppermute x16 -> x15, waiting for transfers between devices: 55.8 us -> 57.8 us  [moved(): return lax.ppermute(value, AXES, pairs)]
    ppermute x16 -> x15, starting transfers between devices: 29.8 us -> 28 us  [moved(): return lax.ppermute(value, AXES, pairs)]
    pallas_call x3 -> x2, Pallas kernels: 22.5 us -> 21.2 us  [attend(): pl.pallas_call(attend_kernel, out_shape=jax.ShapeDtypeStruct((TILE, heads...]
    unnamed x40 -> x34, local copies, waits for them, and re-layouts: 6.08 us -> 5.96 us
  transfers between devices with their start and end apart: 17 -> 16, of which waited for: 7 -> 7; matrix products, arithmetic and copies ran while one was open for 4% -> 4% of each run, Pallas kernels for 36% -> 36%
where the time goes in v6:
time: 186 us; the launch traced here: 185 us
  Pallas kernels  67.9 us (37%)
  waiting for transfers between devices  57.8 us (31%)
  starting transfers between devices  28 us (15%)
  between operations  15.7 us (8%)
  local copies, waits for them, and re-layouts  11.4 us (6%)
  other arithmetic  4.02 us (2%)
    ppermute x15, waiting for transfers between devices, moved(): return lax.ppermute(value, AXES, pairs)  57.8 us
    ppermute x15, starting transfers between devices, moved(): return lax.ppermute(value, AXES, pairs)  28 us
    pallas_call x4, Pallas kernels, project_out(): pl.pallas_call(project_out_kernel, out_shape=jax.ShapeDtypeStruct((TILE,...  24.1 us
    pallas_call x2, Pallas kernels, attend(): pl.pallas_call(attend_kernel, out_shape=jax.ShapeDtypeStruct((TILE, heads...  21.2 us
    pallas_call x2, Pallas kernels, project_in(): pl.pallas_call(functools.partial(project_in_kernel, (len(own), len(other)...  21.1 us
    unnamed x34, local copies, waits for them, and re-layouts  5.96 us
  transfers between devices with their start and end apart: 16, of which 7 were waited for; matrix products, arithmetic and copies ran while one was open for 4% of the time, Pallas kernels for 36%

profile of v6, /device:TPU:7, one launch (start us, length us, event | category | flops | bytes accessed | tf_op | source)
XLA Modules:
  0.0 184.9 jit_solution(1255128876078246019)
XLA Ops:
  6.6 1.2 slice-done
  9.6 8.0 %collective-permute-done.1 = bf16[48,3072]{1,0:T(8,128)(2,1)} collective-permute-done((bf16[48,3072]{1,0:T(8,128)(2,1)S(1)}, bf16[48,3072]{1,0:T(8,128)(2,1)}, u32[]{:S(2)}, u32[]{:S(2)}) %collective-permute-start.1) | collective-permute-done | bytes 294944 | tf_op jit(solution)/shard_map/ppermute | solution.py:43
  21.2 8.4 %collective-permute-start.2 = (bf16[1536,1024]{1,0:T(8,128)(2,1)S(1)}, bf16[1536,1024]{1,0:T(8,128)(2,1)}, u32[]{:S(2)}, u32[]{:S(2)}) collective-permute-start(bf16[1536,1024]{1,0:T(8,128)(2,1)S(1)} %pad_maximum_fusion.refs_0_), channel_id=1, source_target_pairs={{0,4},{1,5},{4,8},{5,9},{6,2},{7,3},{8,12},{9,13},{10,6},{11,7},{1... | collective-permute-start | bytes 9437192 | tf_op jit(solution)/shard_map/ppermute | solution.py:43
  30.9 2.2 %collective-permute-done.4 = bf16[768,512]{1,0:T(8,128)(2,1)S(1)} collective-permute-done((bf16[768,512]{1,0:T(8,128)(2,1)S(1)}, bf16[768,512]{1,0:T(8,128)(2,1)S(1)}, u32[]{:S(2)}, u32[]{:S(2)}) %collective-permute-start.4) | collective-permute-done | bytes 786464 | tf_op jit(solution)/shard_map/ppermute | solution.py:43
  33.1 1.3 pad_maximum_fusion.2.refs_0_
  34.4 32.4 %collective-permute-done.2.refs_1_ = bf16[1536,1024]{1,0:T(8,128)(2,1)} collective-permute-done((bf16[1536,1024]{1,0:T(8,128)(2,1)S(1)}, bf16[1536,1024]{1,0:T(8,128)(2,1)}, u32[]{:S(2)}, u32[]{:S(2)}) %collective-permute-start.2) | collective-permute-done | bytes 3145760 | tf_op jit(solution)/shard_map/ppermute | solution.py:43
  66.7 11.1 %collective-permute-start.6 = (bf16[1536,512]{1,0:T(8,128)(2,1)}, bf16[1536,512]{1,0:T(8,128)(2,1)}, u32[]{:S(2)}, u32[]{:S(2)}) collective-permute-start(bf16[1536,512]{1,0:T(8,128)(2,1)} %pad_maximum_fusion.2.refs_0_), channel_id=1, source_target_pairs={{0,4},{1,5},{4,8},{5,9},{6,2},{7,3},{8,12},{9,13},{10,6},{11,7},{1... | collective-permute-start | bytes 4718600 | tf_op jit(solution)/shard_map/ppermute | solution.py:43
  81.5 1.3 copy-done.5
  82.8 1.3 copy-done.6
  84.0 13.8 %attend.2.refs_0_ = bf16[384,1024]{1,0:T(8,128)(2,1)S(1)} custom-call(f32[6]{0:T(128)S(1)} %and_select_fusion.bias_ref, bf16[384,1536]{1,0:T(8,128)(2,1)S(1)} %copy-done.5, bf16[384,1536]{1,0:T(8,128)(2,1)S(1)} %copy-done.6, bf16[1536,1024]{1,0:T(8,128)(2,1)S(1)} %pad_maximum_fusion.refs_0_, bf16[1536,1024]{1,0:T(8,128)(2,1)} %collective-permute-done.2.refs_1_, ...), custom_call_target="tpu_custom_call" | custom-call | flops 1 | bytes 1 | tf_op jit(solution)/shard_map/attend/pallas_call | solution.py:117
  98.7 2.9 %collective-permute-done.7.refs_2_ = bf16[1536,512]{1,0:T(8,128)(2,1)S(1)} collective-permute-done((bf16[1536,512]{1,0:T(8,128)(2,1)}, bf16[1536,512]{1,0:T(8,128)(2,1)S(1)}, u32[]{:S(2)}, u32[]{:S(2)}) %collective-permute-start.7) | collective-permute-done | bytes 1572896 | tf_op jit(solution)/shard_map/ppermute | solution.py:43
  101.6 7.4 %attend.3.refs_1_ = bf16[384,512]{1,0:T(8,128)(2,1)S(1)} custom-call(f32[6]{0:T(128)S(1)} %and_select_fusion.bias_ref, bf16[384,1536]{1,0:T(8,128)(2,1)S(1)} %copy-done.5, bf16[384,1536]{1,0:T(8,128)(2,1)S(1)} %copy-done.6, bf16[1536,512]{1,0:T(8,128)(2,1)} %pad_maximum_fusion.2.refs_0_, bf16[1536,512]{1,0:T(8,128)(2,1)} %collective-permute-done.6.refs_1_, ...), custom_call_target="tpu_custom_call" | custom-call | flops 1 | bytes 1 | tf_op jit(solution)/shard_map/attend/pallas_call | solution.py:117
  109.9 9.9 %project_in.2 = (f32[384,3072]{1,0:T(8,128)}, f32[384,1]{1,0:T(8,128)}) custom-call(s32[1]{0:T(128)} %bitcast.3.hid_ref, bf16[384,1024]{1,0:T(8,128)(2,1)} %copy-done.2, bf16[384,512]{1,0:T(8,128)(2,1)} %copy-done.7, f32[1,3072]{1,0:T(1,128)} %bitcast.9, bf16[3072,3072]{1,0:T(8,128)(2,1)} %refs_3_.3), custom_call_target="tpu_custom_call" | custom-call | flops 1 | bytes 1 | tf_op jit(solution)/shard_map/project_in/pallas_call | solution.py:202
  119.8 6.8 %collective-permute-done.9.refs_1_ = bf16[384,512]{1,0:T(8,128)(2,1)S(1)} collective-permute-done((bf16[384,512]{1,0:T(8,128)(2,1)S(1)}, bf16[384,512]{1,0:T(8,128)(2,1)S(1)}, u32[]{:S(2)}, u32[]{:S(2)}) %collective-permute-start.9) | collective-permute-done | bytes 393248 | tf_op jit(solution)/shard_map/ppermute | solution.py:43
  127.4 11.2 %project_in.3.hidden_ref = bf16[384,3072]{1,0:T(8,128)(2,1)} custom-call(s32[1]{0:T(128)} %bitcast.3.hid_ref, bf16[384,1024]{1,0:T(8,128)(2,1)} %copy-done.13, bf16[384,512]{1,0:T(8,128)(2,1)} %copy-done.14, f32[1,3072]{1,0:T(1,128)} %bitcast.10, bf16[3072,3072]{1,0:T(8,128)(2,1)} %refs_3_.3, f32[384,3072]{1,0:T(8,128)} %get-tuple-element.26.refs_4_, ...), custom_call_target="tpu_custom_call" | custom-call | flops 1 | bytes 1 | tf_op jit(solution)/shard_map/project_in/pallas_call | solution.py:202
  139.8 6.0 %project_out.4 = bf16[384,768]{1,0:T(8,128)(2,1)} custom-call(s32[1]{0:T(128)} %bitcast.part_ref.core_ref, bf16[384,3072]{1,0:T(8,128)(2,1)} %project_in.3.hidden_ref, bf16[1536,3072]{1,0:T(8,128)(2,1)} %all-gather.2.cloned.1.call-done.w_ref), custom_call_target="tpu_custom_call" | custom-call | flops 1 | bytes 1 | tf_op jit(solution)/shard_map/project_out/pallas_call | solution.py:226
  146.8 1.4 copy-done.10
  148.2 6.0 %project_out.5 = bf16[384,768]{1,0:T(8,128)(2,1)} custom-call(s32[1]{0:T(128)} %bitcast.part_ref.core_ref, bf16[384,3072]{1,0:T(8,128)(2,1)} %copy-done.10, bf16[1536,3072]{1,0:T(8,128)(2,1)} %all-gather.2.cloned.1.call-done.w_ref), custom_call_target="tpu_custom_call" | custom-call | flops 1 | bytes 1 | tf_op jit(solution)/shard_map/project_out/pallas_call | solution.py:226
  154.1 2.6 %collective-permute-start.14 = (bf16[384,768]{1,0:T(8,128)(2,1)}, bf16[384,768]{1,0:T(8,128)(2,1)S(1)}, u32[]{:S(2)}, u32[]{:S(2)}) collective-permute-start(bf16[384,768]{1,0:T(8,128)(2,1)} %project_out.5), channel_id=1, source_target_pairs={{0,3},{1,2},{2,1},{3,0},{4,7},{5,6},{6,5},{7,4},{8,11},{9,10},{10,... | collective-permute-start | bytes 1769480 | tf_op jit(solution)/shard_map/ppermute | solution.py:43
  156.8 5.9 %project_out.6 = bf16[384,768]{1,0:T(8,128)(2,1)} custom-call(s32[1]{0:T(128)S(6)} %sub.21.part_ref, bf16[384,3072]{1,0:T(8,128)(2,1)} %copy-done.10, bf16[1536,3072]{1,0:T(8,128)(2,1)} %all-gather.2.cloned.1.call-done.w_ref), custom_call_target="tpu_custom_call" | custom-call | flops 1 | bytes 1 | tf_op jit(solution)/shard_map/project_out/pallas_call | solution.py:226
  164.5 6.2 %project_out.7.refs_3_ = f32[384,768]{1,0:T(8,128)} custom-call(s32[1]{0:T(128)S(6)} %sub.21.part_ref, bf16[384,3072]{1,0:T(8,128)(2,1)} %project_in.3.hidden_ref, bf16[1536,3072]{1,0:T(8,128)(2,1)} %all-gather.2.cloned.1.call-done.w_ref), custom_call_target="tpu_custom_call" | custom-call | flops 1 | bytes 1 | tf_op jit(solution)/shard_map/project_out/pallas_call | solution.py:226
  170.8 4.5 %collective-permute-done.14.refs_5_ = bf16[384,768]{1,0:T(8,128)(2,1)S(1)} collective-permute-done((bf16[384,768]{1,0:T(8,128)(2,1)}, bf16[384,768]{1,0:T(8,128)(2,1)S(1)}, u32[]{:S(2)}, u32[]{:S(2)}) %collective-permute-start.14) | collective-permute-done | bytes 589856 | tf_op jit(solution)/shard_map/ppermute | solution.py:43
  175.3 1.3 copy-done.4
  176.5 1.5 finish.1
  (81 shorter events, 14.7 us)
Async XLA Ops:
  6.5 74.6 %copy-start = (s32[64,27]{0,1:T(8,128)S(1)}, s32[64,27]{0,1:T(8,128)}, u32[]{:S(2)}) copy-start(s32[64,27]{0,1:T(8,128)} %param.20) | copy-start | bytes 20740
  6.5 133.3 %all-gather.2.cloned.1.call-start = ((), (), s32[]{:S(2)}) async-start(), calls=%async_computation | async-start | bytes 10027008 | tf_op jit(solution)/shard_map/all_gather | solution.py:342
  8.1 10.5 %collective-permute-start = (bf16[768,1024]{1,0:T(8,128)(2,1)S(1)}, bf16[768,1024]{1,0:T(8,128)(2,1)S(1)}, u32[]{:S(2)}, u32[]{:S(2)}) collective-permute-start(bf16[768,1024]{1,0:T(8,128)(2,1)S(1)} %pad_maximum_fusion.1), channel_id=1, source_target_pairs={{0,2},{1,3},{2,0},{3,1},{4,6},{5,7},{6,4},{7,5},{8,10},{9,11},{10,... | collective-permute-start | bytes 4718600 | tf_op jit(solution)/shard_map/ppermute | solution.py:43
  8.9 8.7 %collective-permute-start.1 = (bf16[48,3072]{1,0:T(8,128)(2,1)S(1)}, bf16[48,3072]{1,0:T(8,128)(2,1)}, u32[]{:S(2)}, u32[]{:S(2)}) collective-permute-start(bf16[48,3072]{1,0:T(8,128)(2,1)S(1)} %bitcast.8), channel_id=1, source_target_pairs={{0,64},{1,65},{2,66},{3,67},{4,68},{5,69},{6,70},{7,71},{8,72},{9,... | collective-permute-start | bytes 884744 | tf_op jit(solution)/shard_map/ppermute | solution.py:43
  18.6 1.7 collective-permute-start.3
  19.2 11.4 %slice-start.1 = ((bf16[384,1536]{1,0:T(8,128)(2,1)}), bf16[384,512]{1,0:T(8,128)(2,1)S(1)}, s32[]{:S(2)}) async-start(bf16[384,1536]{1,0:T(8,128)(2,1)} %param.12), calls=%async_computation.2 | async-start | bytes 786432 | tf_op jit(solution)/shard_map/slice | solution.py:305
  21.2 45.5 %collective-permute-start.2 = (bf16[1536,1024]{1,0:T(8,128)(2,1)S(1)}, bf16[1536,1024]{1,0:T(8,128)(2,1)}, u32[]{:S(2)}, u32[]{:S(2)}) collective-permute-start(bf16[1536,1024]{1,0:T(8,128)(2,1)S(1)} %pad_maximum_fusion.refs_0_), channel_id=1, source_target_pairs={{0,4},{1,5},{4,8},{5,9},{6,2},{7,3},{8,12},{9,13},{10,6},{11,7},{1... | collective-permute-start | bytes 9437192 | tf_op jit(solution)/shard_map/ppermute | solution.py:43
  30.7 2.4 %collective-permute-start.4 = (bf16[768,512]{1,0:T(8,128)(2,1)S(1)}, bf16[768,512]{1,0:T(8,128)(2,1)S(1)}, u32[]{:S(2)}, u32[]{:S(2)}) collective-permute-start(bf16[768,512]{1,0:T(8,128)(2,1)S(1)} %pad_maximum_fusion.3), channel_id=1, source_target_pairs={{0,2},{1,3},{2,0},{3,1},{4,6},{5,7},{6,4},{7,5},{8,10},{9,11},{10,... | collective-permute-start | bytes 2359304 | tf_op jit(solution)/shard_map/ppermute | solution.py:43
  30.8 47.0 %copy-start.9 = (s32[64]{0:T(128)S(1)}, s32[64]{0:T(128)}, u32[]{:S(2)}) copy-start(s32[64]{0:T(128)} %param.19) | copy-start | bytes 772
  30.9 48.9 %copy-start.16 = (s32[6]{0:T(128)S(1)}, s32[6]{0:T(128)}, u32[]{:S(2)}) copy-start(s32[6]{0:T(128)} %constant.77.clone) | copy-start | bytes 76
  66.7 14.8 %collective-permute-start.5 = (bf16[1536,1024]{1,0:T(8,128)(2,1)}, bf16[1536,1024]{1,0:T(8,128)(2,1)}, u32[]{:S(2)}, u32[]{:S(2)}) collective-permute-start(bf16[1536,1024]{1,0:T(8,128)(2,1)} %collective-permute-done.2.refs_1_), channel_id=1, source_target_pairs={{0,2},{1,3},{2,0},{3,1},{4,6},{5,7},{6,4},{7,5},{8,10},{9,11},{10,... | collective-permute-start | bytes 9437192 | tf_op jit(solution)/shard_map/ppermute | solution.py:43
  66.7 31.2 %collective-permute-start.6 = (bf16[1536,512]{1,0:T(8,128)(2,1)}, bf16[1536,512]{1,0:T(8,128)(2,1)}, u32[]{:S(2)}, u32[]{:S(2)}) collective-permute-start(bf16[1536,512]{1,0:T(8,128)(2,1)} %pad_maximum_fusion.2.refs_0_), channel_id=1, source_target_pairs={{0,4},{1,5},{4,8},{5,9},{6,2},{7,3},{8,12},{9,13},{10,6},{11,7},{1... | collective-permute-start | bytes 4718600 | tf_op jit(solution)/shard_map/ppermute | solution.py:43
  97.9 11.2 %copy-start.2 = (bf16[384,1024]{1,0:T(8,128)(2,1)}, bf16[384,1024]{1,0:T(8,128)(2,1)S(1)}, u32[]{:S(2)}) copy-start(bf16[384,1024]{1,0:T(8,128)(2,1)S(1)} %attend.2.refs_0_) | copy-start | bytes 2359300
  97.9 3.7 %collective-permute-start.7 = (bf16[1536,512]{1,0:T(8,128)(2,1)}, bf16[1536,512]{1,0:T(8,128)(2,1)S(1)}, u32[]{:S(2)}, u32[]{:S(2)}) collective-permute-start(bf16[1536,512]{1,0:T(8,128)(2,1)} %collective-permute-done.6.refs_1_), channel_id=1, source_target_pairs={{0,2},{1,3},{2,0},{3,1},{4,6},{5,7},{6,4},{7,5},{8,10},{9,11},{10,... | collective-permute-start | bytes 4718600 | tf_op jit(solution)/shard_map/ppermute | solution.py:43
  98.0 21.9 %collective-permute-start.8 = (bf16[384,1024]{1,0:T(8,128)(2,1)S(1)}, bf16[384,1024]{1,0:T(8,128)(2,1)S(1)}, u32[]{:S(2)}, u32[]{:S(2)}) collective-permute-start(bf16[384,1024]{1,0:T(8,128)(2,1)S(1)} %attend.2.refs_0_), channel_id=1, source_target_pairs={{0,1},{1,0},{2,3},{3,2},{4,5},{5,4},{6,7},{7,6},{8,9},{9,8},{10,11... | collective-permute-start | bytes 2359304 | tf_op jit(solution)/shard_map/ppermute | solution.py:43
  109.0 17.7 %collective-permute-start.9 = (bf16[384,512]{1,0:T(8,128)(2,1)S(1)}, bf16[384,512]{1,0:T(8,128)(2,1)S(1)}, u32[]{:S(2)}, u32[]{:S(2)}) collective-permute-start(bf16[384,512]{1,0:T(8,128)(2,1)S(1)} %attend.3.refs_1_), channel_id=1, source_target_pairs={{0,1},{1,0},{2,3},{3,2},{4,5},{5,4},{6,7},{7,6},{8,9},{9,8},{10,11... | collective-permute-start | bytes 1179656 | tf_op jit(solution)/shard_map/ppermute | solution.py:43
  138.6 8.2 %collective-permute-start.10 = (bf16[384,3072]{1,0:T(8,128)(2,1)}, bf16[384,3072]{1,0:T(8,128)(2,1)S(1)}, u32[]{:S(2)}, u32[]{:S(2)}) collective-permute-start(bf16[384,3072]{1,0:T(8,128)(2,1)} %project_in.3.hidden_ref), channel_id=1, source_target_pairs={{0,2},{1,3},{2,0},{3,1},{4,6},{5,7},{6,4},{7,5},{8,10},{9,11},{10,... | collective-permute-start | bytes 7077896 | tf_op jit(solution)/shard_map/ppermute | solution.py:43
  145.8 29.4 %collective-permute-start.13 = (bf16[384,768]{1,0:T(8,128)(2,1)}, bf16[384,768]{1,0:T(8,128)(2,1)S(1)}, u32[]{:S(2)}, u32[]{:S(2)}) collective-permute-start(bf16[384,768]{1,0:T(8,128)(2,1)} %project_out.4), channel_id=1, source_target_pairs={{0,1},{1,0},{2,3},{3,2},{4,5},{5,4},{6,7},{7,6},{8,9},{9,8},{10,11... | collective-permute-start | bytes 1769480 | tf_op jit(solution)/shard_map/ppermute | solution.py:43
  154.1 10.3 %copy-start.15 = (f32[3072]{0:T(1024)S(1)}, f32[3072]{0:T(1024)}, u32[]{:S(2)}) copy-start(f32[3072]{0:T(1024)} %param.18) | copy-start | bytes 36868
  154.1 21.1 %collective-permute-start.14 = (bf16[384,768]{1,0:T(8,128)(2,1)}, bf16[384,768]{1,0:T(8,128)(2,1)S(1)}, u32[]{:S(2)}, u32[]{:S(2)}) collective-permute-start(bf16[384,768]{1,0:T(8,128)(2,1)} %project_out.5), channel_id=1, source_target_pairs={{0,3},{1,2},{2,1},{3,0},{4,7},{5,6},{6,5},{7,4},{8,11},{9,10},{10,... | collective-permute-start | bytes 1769480 | tf_op jit(solution)/shard_map/ppermute | solution.py:43
  163.8 6.9 %collective-permute-start.11 = (bf16[384,384]{1,0:T(8,128)(2,1)S(1)}, bf16[384,384]{1,0:T(8,128)(2,1)S(1)}, u32[]{:S(2)}, u32[]{:S(2)}) collective-permute-start(bf16[384,384]{1,0:T(8,128)(2,1)S(1)} %get-tuple-element.41), channel_id=1, source_target_pairs={{0,2},{1,3},{2,0},{3,1},{4,6},{5,7},{6,4},{7,5},{8,10},{9,11},{10,... | collective-permute-start | bytes 884744 | tf_op jit(solution)/shard_map/ppermute | solution.py:43
  163.9 6.8 %collective-permute-start.12 = (bf16[384,384]{1,0:T(8,128)(2,1)S(1)}, bf16[384,384]{1,0:T(8,128)(2,1)S(1)}, u32[]{:S(2)}, u32[]{:S(2)}) collective-permute-start(bf16[384,384]{1,0:T(8,128)(2,1)S(1)} %get-tuple-element.42), channel_id=1, source_target_pairs={{0,2},{1,3},{2,0},{3,1},{4,6},{5,7},{6,4},{7,5},{8,10},{9,11},{10,... | collective-permute-start | bytes 884744 | tf_op jit(solution)/shard_map/ppermute | solution.py:43
  164.5 10.8 %copy-start.3 = (bf16[384,1024]{1,0:T(8,128)(2,1)S(1)}, bf16[384,1024]{1,0:T(8,128)(2,1)}, u32[]{:S(2)}) copy-start(bf16[384,1024]{1,0:T(8,128)(2,1)} %copy-done.2) | copy-start | bytes 2359300
  164.5 10.8 %copy-start.8 = (bf16[384,512]{1,0:T(8,128)(2,1)S(1)}, bf16[384,512]{1,0:T(8,128)(2,1)}, u32[]{:S(2)}) copy-start(bf16[384,512]{1,0:T(8,128)(2,1)} %copy-done.7) | copy-start | bytes 1179652
  (12 other events, 27.5 us)
Sparse Core Ops, SparseCore 0:
  21.3 118.2 all-gather.1
